TPU v7x, 32 devices: a whole 2x2x4 slice. The times are simulated.
32 devices in a mesh: dp: 8 (over z, y), blk: 4 (over x, core).
Axes of the slice: x: 2, y: 2, z: 4, core: 2. Of those that a mesh axis runs over, the one named last changes fastest.
Arguments:
- tokens: bfloat16 [2, 8, 3072, 512], P(None, 'dp', 'blk'), may hold values from -6 to 6
- cotangent: bfloat16 [2, 8, 3072, 512], P(None, 'dp', 'blk'), may hold values from -6 to 6
- segments: int32 [2, 8, 3072], P(None, 'dp', 'blk'), may hold values from 0 to 766, as said below
- padding: int32 [2, 8, 3072], P(None, 'dp', 'blk'), may hold values from 0 to 1, as said below
- known: int32 [2, 8, 3072], P(None, 'dp', 'blk'), may hold values from 0 to 1, as said below
- w_qkv: bfloat16 [512, 1536], P(('dp', 'blk')), may hold values from -0.25 to 0.25
- w_out: bfloat16 [512, 512], P(('dp', 'blk')), may hold values from -2 to 2
- w_up: bfloat16 [512, 512], P(('dp', 'blk')), may hold values from -0.25 to 0.25
- w_down: bfloat16 [512, 512], P(('dp', 'blk')), may hold values from -0.25 to 0.25
- norm_gains: bfloat16 [2, 512], P(None, ('dp', 'blk')), may hold values from 0.25 to 1.75
- norm_shifts: bfloat16 [2, 512], P(None, ('dp', 'blk')), may hold values from -3 to 3
Outputs:
- layer_out: bfloat16 [2, 8, 3072, 512], P(None, 'dp', 'blk')
- token_grad: bfloat16 [2, 8, 3072, 512], P(None, 'dp', 'blk')
- grad_qkv: float32 [512, 1536], P(('dp', 'blk'))
- grad_out: float32 [512, 512], P(('dp', 'blk'))
- grad_up: float32 [512, 512], P(('dp', 'blk'))
- grad_down: float32 [512, 512], P(('dp', 'blk'))
- grad_gains: float32 [2, 512], P(None, ('dp', 'blk'))
- grad_shifts: float32 [2, 512], P(None, ('dp', 'blk'))
Inputs may be any that keep to these rules, and one draw needn't show every extreme that they name: `segments`: within a row the ids start at 0 and never fall; one segment of every row covers positions 384 to 2687. `padding`: 0 at the first position of every segment. `known`: 1 at the first position of every segment.
All inputs are finite; a program needn't handle non-finite values.
Results may differ from a plain program's by a relative error of at most 0.018.
Values may be sent and summed in bfloat16 or wider, within the bound.
A program may use at most 384 MiB of HBM per device.

v0:
```python
import jax
import jax.numpy as jnp
from jax import lax
from jax.sharding import PartitionSpec as P

HEADS = 8


EPSILON = 1e-05
MASKED_SCORE = -1e30


def piece_len(span_len):
    divisor = 1
    for candidate in range(1, min(span_len, 512) + 1):
        if span_len % candidate == 0:
            divisor = candidate
    return divisor


def allowed(query_seg, query_pos, key_seg, key_pad, key_known, key_pos):
    same_cell = query_seg[:, :, None] == key_seg[:, None, :]
    usable = (key_pad[:, None, :] == 0) & (
        (key_known[:, None, :] == 1) | (query_pos[None, :, None] == key_pos[None, None, :])
    )
    return (same_cell & usable)[:, :, None, :]


def layer_norm(rows_in, gain, shift):
    center = rows_in - jnp.mean(rows_in, axis=-1, keepdims=True)
    inverse = lax.rsqrt(jnp.mean(center * center, axis=-1, keepdims=True) + EPSILON)
    normed = center * inverse
    return (normed * gain + shift, normed, inverse)


def norm_back(grad_in, normed, inverse, gain):
    scaled = grad_in * gain
    return inverse * (
        scaled
        - jnp.mean(scaled, axis=-1, keepdims=True)
        - normed * jnp.mean(scaled * normed, axis=-1, keepdims=True)
    )


def gelu_exact(values_in):
    return jax.nn.gelu(values_in, approximate=False)


def score_grads(query_h, out_h, lse_part, delta_part, key_h, value_h, allow_mask, factor):
    scores = (
        jnp.einsum("rqhd,rkhd->rqhk", query_h, key_h, preferred_element_type=jnp.float32) * factor
    )
    probabilities = jnp.where(allow_mask, jnp.exp(scores - lse_part[..., None]), 0.0)
    grad_probs = jnp.einsum("rqhd,rkhd->rqhk", out_h, value_h, preferred_element_type=jnp.float32)
    grad_scores = (probabilities * (grad_probs - delta_part[..., None])).astype(jnp.bfloat16)
    return (probabilities, grad_scores)


def pair_grads(query_h, out_h, lse_part, delta_part, key_h, value_h, allow_mask, factor):
    probabilities, grad_scores = score_grads(
        query_h, out_h, lse_part, delta_part, key_h, value_h, allow_mask, factor
    )
    part_q = (
        jnp.einsum("rqhk,rkhd->rqhd", grad_scores, key_h, preferred_element_type=jnp.float32)
        * factor
    )
    part_k = (
        jnp.einsum("rqhk,rqhd->rkhd", grad_scores, query_h, preferred_element_type=jnp.float32)
        * factor
    )
    part_v = jnp.einsum(
        "rqhk,rqhd->rkhd",
        probabilities.astype(jnp.bfloat16),
        out_h,
        preferred_element_type=jnp.float32,
    )
    return (part_q, part_k, part_v)


def add_rows(target, position, addend):
    current = lax.dynamic_slice_in_dim(target, position, addend.shape[1], 1)
    return lax.dynamic_update_slice_in_dim(target, current + addend, position, 1)


def shards(
    tokens, cotangent, segments, padding, known, w_qkv, w_out, w_up, w_down, norm_gains, norm_shifts
):
    micro_count, row_count, block_len, model_width = tokens.shape
    head_count = HEADS
    head_size = model_width // head_count
    factor = head_size ** (-0.5)
    hidden_width = w_up.shape[1]
    row_len = block_len * lax.axis_size("blk")
    seg_all, pad_all, known_all = (
        lax.all_gather(segments, "blk", axis=2, tiled=True),
        lax.all_gather(padding, "blk", axis=2, tiled=True),
        lax.all_gather(known, "blk", axis=2, tiled=True),
    )
    own_pos = lax.axis_index("blk") * block_len + jnp.arange(block_len, dtype=jnp.int32)
    acc_qkv = jnp.zeros((model_width, 3 * model_width), jnp.float32)
    acc_out = jnp.zeros((model_width, model_width), jnp.float32)
    acc_up = jnp.zeros((model_width, hidden_width), jnp.float32)
    acc_down = jnp.zeros((hidden_width, model_width), jnp.float32)
    acc_gain = jnp.zeros((2, model_width), jnp.float32)
    acc_shift = jnp.zeros((2, model_width), jnp.float32)
    outputs = []
    input_grads = []
    for micro_index in range(micro_count):
        params = (
            lax.all_gather(w_qkv, ("dp", "blk"), axis=0, tiled=True),
            lax.all_gather(w_out, ("dp", "blk"), axis=0, tiled=True),
            lax.all_gather(w_up, ("dp", "blk"), axis=0, tiled=True),
            lax.all_gather(w_down, ("dp", "blk"), axis=0, tiled=True),
            lax.all_gather(norm_gains, ("dp", "blk"), axis=1, tiled=True),
            lax.all_gather(norm_shifts, ("dp", "blk"), axis=1, tiled=True),
        )
        full_qkv, full_out, full_up, full_down, gain_rows, shift_rows = params
        gain_rows = gain_rows.astype(jnp.float32)
        shift_rows = shift_rows.astype(jnp.float32)
        tokens_now = tokens[micro_index]
        seg_own = segments[micro_index]
        seg_row = seg_all[micro_index]
        pad_row = pad_all[micro_index]
        known_row = known_all[micro_index]
        qkv = jnp.einsum(
            "rbd,de->rbe", tokens_now, full_qkv, preferred_element_type=jnp.float32
        ).astype(jnp.bfloat16)
        queries_flat = qkv[..., :model_width]
        keys_flat = qkv[..., model_width : 2 * model_width]
        values_flat = qkv[..., 2 * model_width :]
        queries = queries_flat.reshape(row_count, block_len, head_count, head_size)
        start_state = (
            jnp.full((row_count, block_len, head_count), MASKED_SCORE, jnp.float32),
            jnp.zeros((row_count, block_len, head_count), jnp.float32),
            jnp.zeros((row_count, block_len, head_count, head_size), jnp.float32),
        )
        start_index = jnp.int32(0)
        key_rows = lax.all_gather(keys_flat, "blk", axis=1, tiled=True)
        value_rows = lax.all_gather(values_flat, "blk", axis=1, tiled=True)
        span_len = key_rows.shape[1]
        sub_len = piece_len(span_len)

        def attend_one(running, sub_index):
            run_max, row_total, weighted = running
            offset = sub_index * sub_len
            position = start_index + offset
            key_h = lax.dynamic_slice_in_dim(key_rows, offset, sub_len, 1).reshape(
                row_count, sub_len, head_count, head_size
            )
            value_h = lax.dynamic_slice_in_dim(value_rows, offset, sub_len, 1).reshape(
                row_count, sub_len, head_count, head_size
            )
            key_pos = position + jnp.arange(sub_len, dtype=jnp.int32)
            allow_mask = allowed(
                seg_own,
                own_pos,
                lax.dynamic_slice_in_dim(seg_row, position, sub_len, 1),
                lax.dynamic_slice_in_dim(pad_row, position, sub_len, 1),
                lax.dynamic_slice_in_dim(known_row, position, sub_len, 1),
                key_pos,
            )
            scores = (
                jnp.einsum("rqhd,rkhd->rqhk", queries, key_h, preferred_element_type=jnp.float32)
                * factor
            )
            scores = jnp.where(allow_mask, scores, MASKED_SCORE)
            new_max = jnp.maximum(run_max, jnp.max(scores, axis=-1))
            exps = jnp.where(allow_mask, jnp.exp(scores - new_max[..., None]), 0.0)
            rescale = jnp.exp(run_max - new_max)
            row_total = row_total * rescale + jnp.sum(exps, axis=-1)
            weighted = weighted * rescale[..., None] + jnp.einsum(
                "rqhk,rkhd->rqhd",
                exps.astype(jnp.bfloat16),
                value_h,
                preferred_element_type=jnp.float32,
            )
            return ((new_max, row_total, weighted), None)

        running, unused = lax.scan(attend_one, start_state, jnp.arange(span_len // sub_len))
        run_max, row_total, weighted = running
        attended = weighted / row_total[..., None]
        lse = run_max + jnp.log(row_total)
        attended_low = attended.reshape(row_count, block_len, model_width).astype(jnp.bfloat16)
        branch = jnp.einsum(
            "rbd,de->rbe", attended_low, full_out, preferred_element_type=jnp.float32
        )
        first, normed_one, inverse_one = layer_norm(
            tokens_now.astype(jnp.float32) + branch, gain_rows[0], shift_rows[0]
        )
        first_low = first.astype(jnp.bfloat16)
        hidden = jnp.einsum("rbd,df->rbf", first_low, full_up, preferred_element_type=jnp.float32)
        activated, gelu_back = jax.vjp(gelu_exact, hidden)
        activated_low = activated.astype(jnp.bfloat16)
        feed = jnp.einsum(
            "rbf,fd->rbd", activated_low, full_down, preferred_element_type=jnp.float32
        )
        result, normed_two, inverse_two = layer_norm(
            first_low.astype(jnp.float32) + feed, gain_rows[1], shift_rows[1]
        )
        outputs.append(result.astype(jnp.bfloat16))
        grad_result = cotangent[micro_index].astype(jnp.float32)
        grad_r2 = norm_back(grad_result, normed_two, inverse_two, gain_rows[1])
        grad_feed = grad_r2.astype(jnp.bfloat16)
        acc_down = acc_down + jnp.einsum(
            "rbf,rbd->fd", activated_low, grad_feed, preferred_element_type=jnp.float32
        )
        grad_act = jnp.einsum(
            "rbd,fd->rbf", grad_feed, full_down, preferred_element_type=jnp.float32
        )
        grad_hidden = gelu_back(grad_act)[0].astype(jnp.bfloat16)
        acc_up = acc_up + jnp.einsum(
            "rbd,rbf->df", first_low, grad_hidden, preferred_element_type=jnp.float32
        )
        grad_first = grad_r2 + jnp.einsum(
            "rbf,df->rbd", grad_hidden, full_up, preferred_element_type=jnp.float32
        )
        grad_r1 = norm_back(grad_first, normed_one, inverse_one, gain_rows[0])
        acc_gain = acc_gain + jnp.stack(
            [
                jnp.sum(grad_first * normed_one, axis=(0, 1)),
                jnp.sum(grad_result * normed_two, axis=(0, 1)),
            ]
        )
        acc_shift = acc_shift + jnp.stack(
            [jnp.sum(grad_first, axis=(0, 1)), jnp.sum(grad_result, axis=(0, 1))]
        )
        grad_branch = grad_r1.astype(jnp.bfloat16)
        acc_out = acc_out + jnp.einsum(
            "rbd,rbe->de", attended_low, grad_branch, preferred_element_type=jnp.float32
        )
        grad_att = jnp.einsum(
            "rbe,de->rbd", grad_branch, full_out, preferred_element_type=jnp.float32
        ).astype(jnp.bfloat16)
        grad_att_h = grad_att.reshape(row_count, block_len, head_count, head_size)
        delta = jnp.sum(grad_att_h.astype(jnp.float32) * attended, axis=-1)
        empty_own = jnp.zeros((row_count, block_len, head_count, head_size), jnp.float32)
        empty_full = jnp.zeros((row_count, row_len, head_count, head_size), jnp.float32)

        def key_back(carried, pieces, start_index):
            key_rows, value_rows = pieces
            span_len = key_rows.shape[1]
            sub_len = piece_len(span_len)

            def key_one(running, sub_index):
                grad_q, grad_k_all, grad_v_all = running
                offset = sub_index * sub_len
                position = start_index + offset
                key_h = lax.dynamic_slice_in_dim(key_rows, offset, sub_len, 1).reshape(
                    row_count, sub_len, head_count, head_size
                )
                value_h = lax.dynamic_slice_in_dim(value_rows, offset, sub_len, 1).reshape(
                    row_count, sub_len, head_count, head_size
                )
                key_pos = position + jnp.arange(sub_len, dtype=jnp.int32)
                allow_mask = allowed(
                    seg_own,
                    own_pos,
                    lax.dynamic_slice_in_dim(seg_row, position, sub_len, 1),
                    lax.dynamic_slice_in_dim(pad_row, position, sub_len, 1),
                    lax.dynamic_slice_in_dim(known_row, position, sub_len, 1),
                    key_pos,
                )
                part_q, part_k, part_v = pair_grads(
                    queries, grad_att_h, lse, delta, key_h, value_h, allow_mask, factor
                )
                return (
                    (
                        grad_q + part_q,
                        add_rows(grad_k_all, position, part_k),
                        add_rows(grad_v_all, position, part_v),
                    ),
                    None,
                )

            running, unused = lax.scan(key_one, carried, jnp.arange(span_len // sub_len))
            return running

        grad_q, grad_k_all, grad_v_all = key_back(
            (empty_own, empty_full, empty_full),
            (
                lax.all_gather(keys_flat, "blk", axis=1, tiled=True),
                lax.all_gather(values_flat, "blk", axis=1, tiled=True),
            ),
            jnp.int32(0),
        )
        grad_k, grad_v = (
            lax.psum_scatter(
                grad_k_all.astype(jnp.bfloat16), "blk", scatter_dimension=1, tiled=True
            ).astype(jnp.float32),
            lax.psum_scatter(
                grad_v_all.astype(jnp.bfloat16), "blk", scatter_dimension=1, tiled=True
            ).astype(jnp.float32),
        )
        grad_qkv_low = jnp.concatenate(
            [
                grad_q.reshape(row_count, block_len, model_width),
                grad_k.reshape(row_count, block_len, model_width),
                grad_v.reshape(row_count, block_len, model_width),
            ],
            axis=-1,
        ).astype(jnp.bfloat16)
        acc_qkv = acc_qkv + jnp.einsum(
            "rbd,rbe->de", tokens_now, grad_qkv_low, preferred_element_type=jnp.float32
        )
        grad_tokens = grad_r1 + jnp.einsum(
            "rbe,de->rbd", grad_qkv_low, full_qkv, preferred_element_type=jnp.float32
        )
        input_grads.append(grad_tokens.astype(jnp.bfloat16))
    grad_qkv, grad_out, grad_up, grad_down, grad_gains, grad_shifts = (
        lax.psum_scatter(acc_qkv, ("dp", "blk"), scatter_dimension=0, tiled=True),
        lax.psum_scatter(acc_out, ("dp", "blk"), scatter_dimension=0, tiled=True),
        lax.psum_scatter(acc_up, ("dp", "blk"), scatter_dimension=0, tiled=True),
        lax.psum_scatter(acc_down, ("dp", "blk"), scatter_dimension=0, tiled=True),
        lax.psum_scatter(acc_gain, ("dp", "blk"), scatter_dimension=1, tiled=True),
        lax.psum_scatter(acc_shift, ("dp", "blk"), scatter_dimension=1, tiled=True),
    )
    return (
        jnp.stack(outputs),
        jnp.stack(input_grads),
        grad_qkv,
        grad_out,
        grad_up,
        grad_down,
        grad_gains,
        grad_shifts,
    )


def solution(mesh):
    in_specs = (
        P(None, "dp", "blk", None),
        P(None, "dp", "blk", None),
        P(None, "dp", "blk"),
        P(None, "dp", "blk"),
        P(None, "dp", "blk"),
        P(("dp", "blk"), None),
        P(("dp", "blk"), None),
        P(("dp", "blk"), None),
        P(("dp", "blk"), None),
        P(None, ("dp", "blk")),
        P(None, ("dp", "blk")),
    )
    out_specs = (
        P(None, "dp", "blk", None),
        P(None, "dp", "blk", None),
        P(("dp", "blk"), None),
        P(("dp", "blk"), None),
        P(("dp", "blk"), None),
        P(("dp", "blk"), None),
        P(None, ("dp", "blk")),
        P(None, ("dp", "blk")),
    )
    return jax.shard_map(shards, mesh=mesh, in_specs=in_specs, out_specs=out_specs, check_vma=False)
```

profile of v0, /device:TPU:0, one launch (start us, length us, event | category | flops | bytes accessed | tf_op | source)
XLA Modules:
  0.0 1931.9 jit_solution(17021722207710781546)
XLA Ops:
  7.9 60.6 %all-gather.8.cloned.1.call-done = bf16[512,1536]{1,0:T(8,128)(2,1)} async-done(((bf16[16,1536]{1,0:T(8,128)(2,1)}), bf16[512,1536]{1,0:T(8,128)(2,1)}) %all-gather.8.cloned.1.call-update) | async-done | bytes 1572880 | tf_op jit(solution)/shard_map/all_gather | solution.py:110
  82.7 39.0 %all-gather = bf16[32,16,2]{1,2,0:T(2,128)(2,1)S(1)} all-gather(bf16[1,16,2]{1,2,0:T(2,128)(2,1)S(1)} %bitcast.674), channel_id=1, replica_groups=mesh['dp'=8,'blk'=4] {'dp','blk'}, dimensions={0}, use_global_device_ids=true | all-gather | bytes 2112 | tf_op jit(solution)/shard_map/all_gather | solution.py:114
  122.1 36.4 %all-gather.1 = bf16[32,16,2]{1,2,0:T(2,128)(2,1)S(1)} all-gather(bf16[1,16,2]{1,2,0:T(2,128)(2,1)S(1)} %bitcast.675), channel_id=1, replica_groups=mesh['dp'=8,'blk'=4] {'dp','blk'}, dimensions={0}, use_global_device_ids=true | all-gather | bytes 2112 | tf_op jit(solution)/shard_map/all_gather | solution.py:115
  178.8 39.6 %all_gather.55 = bf16[512,512]{1,0:T(8,128)(2,1)S(1)} all-gather(bf16[16,512]{1,0:T(8,128)(2,1)S(1)} %copy-done.93), channel_id=1, replica_groups=mesh['dp'=8,'blk'=4] {'dp','blk'}, dimensions={0}, use_global_device_ids=true | all-gather | bytes 540672 | tf_op jit(solution)/shard_map/all_gather | solution.py:111
  218.4 40.7 %all_gather.58 = bf16[512,512]{1,0:T(8,128)(2,1)} all-gather(bf16[16,512]{1,0:T(8,128)(2,1)S(1)} %copy-done.94), channel_id=1, replica_groups=mesh['dp'=8,'blk'=4] {'dp','blk'}, dimensions={0}, use_global_device_ids=true | all-gather | bytes 540672 | tf_op jit(solution)/shard_map/all_gather | solution.py:112
  259.1 42.1 %all_gather.59 = bf16[512,512]{1,0:T(8,128)(2,1)} all-gather(bf16[16,512]{1,0:T(8,128)(2,1)S(1)} %copy-done.95), channel_id=1, replica_groups=mesh['dp'=8,'blk'=4] {'dp','blk'}, dimensions={0}, use_global_device_ids=true | all-gather | bytes 540672 | tf_op jit(solution)/shard_map/all_gather | solution.py:113
  313.5 133.1 %while.61 = (s32[]{:T(128)}, f32[1,768,8]{1,2,0:T(8,128)S(1)}, f32[1,768,8]{1,2,0:T(8,128)S(1)}, f32[1,768,8,64]{1,3,2,0:T(8,128)}, s32[1,1,768]{2,1,0:T(1,128)S...) while((s32[]{:T(128)}, f32[1,768,8]{1,2,0:T(8,128)S(1)}, ...), condition=%wide.region_11.12_spmd.clone, body=%wide.region_8.0_spmd.clone.sunk | while | flops 849385728 | bytes 97156368 | solution.py:179
  316.8 6.6 fusion.279
  323.5 7.9 bitcast_add_fusion.15
  338.7 6.6 fusion.279
  345.4 8.4 bitcast_add_fusion.15
  361.0 6.6 fusion.279
  367.6 8.4 bitcast_add_fusion.15
  383.2 6.6 fusion.279
  389.9 8.4 bitcast_add_fusion.15
  405.5 6.6 fusion.279
  412.1 8.4 bitcast_add_fusion.15
  427.7 6.6 fusion.279
  434.4 8.4 bitcast_add_fusion.15
  459.0 144.3 %while.60 = (s32[]{:T(128)}, f32[1,768,8]{1,2,0:T(8,128)S(1)}, f32[1,768,8]{1,2,0:T(8,128)S(1)}, f32[1,768,8,64]{1,3,2,0:T(8,128)}, s32[1,1,768]{2,1,0:T(1,128)S...) while((s32[]{:T(128)}, f32[1,768,8]{1,2,0:T(8,128)S(1)}, ...), condition=%wide.region_3.4_spmd.clone, body=%wide.region_0.3_spmd.clone.sunk | while | flops 849385728 | bytes 97156368 | solution.py:179
  463.2 7.7 fusion.273
  471.0 8.0 bitcast_add_fusion.13
  486.9 7.7 fusion.273
  494.7 8.4 bitcast_add_fusion.13
  511.0 7.7 fusion.273
  518.7 8.4 bitcast_add_fusion.13
  535.1 7.7 fusion.273
  542.9 8.4 bitcast_add_fusion.13
  559.2 7.7 fusion.273
  567.0 8.4 bitcast_add_fusion.13
  583.3 7.7 fusion.273
  591.1 8.4 bitcast_add_fusion.13
  643.0 207.3 %while.62 = (s32[]{:T(128)}, f32[1,768,8,64]{1,3,2,0:T(8,128)}, f32[1,3072,8,64]{1,3,2,0:T(8,128)}, f32[1,3072,8,64]{1,3,2,0:T(8,128)}, s32[6]{0:T(128)}, /*inde...) while((s32[]{:T(128)}, f32[1,768,8,64]{1,3,2,0:T(8,128)}, ...), condition=%wide.region_22.23_spmd.clone, body=%wide.region_21.22_spmd.clone.sunk | while | flops 2048657664 | bytes 201661904 | solution.py:275
  651.7 6.5 fusion.293
  720.3 6.5 fusion.293
  872.4 200.9 %while.63 = (s32[]{:T(128)}, f32[1,768,8,64]{1,3,2,0:T(8,128)}, f32[1,3072,8,64]{1,3,2,0:T(8,128)}, f32[1,3072,8,64]{1,3,2,0:T(8,128)}, s32[6]{0:T(128)S(1)}, /*...) while((s32[]{:T(128)}, f32[1,768,8,64]{1,3,2,0:T(8,128)}, ...), condition=%wide.region_31.32_spmd.clone, body=%wide.region_30.31_spmd.clone.sunk | while | flops 2048657664 | bytes 204807664 | solution.py:275
  879.9 6.5 fusion.307
  914.1 6.5 fusion.307
  980.8 6.5 fusion.307
  1014.1 6.5 fusion.307
  1047.3 6.5 fusion.307
  1112.5 40.7 %reduce-scatter.23.cloned.1.call-done = bf16[1,768,8,64]{1,3,2,0:T(8,128)(2,1)} async-done(((bf16[1,3072,8,64]{1,3,2,0:T(8,128)(2,1)}), bf16[1,768,8,64]{1,3,2,0:T(8,128)(2,1)}) %reduce-scatter.23.cloned.1.call-update) | async-done | bytes 786448 | tf_op jit(solution)/shard_map/reduce_scatter | solution.py:290
  1162.9 125.8 %reduce-scatter.33.cloned.1.call-done = f32[16,2]{1,0:T(8,128)} async-done(((f32[512,2]{1,0:T(8,128)}), f32[16,2]{1,0:T(8,128)}) %reduce-scatter.33.cloned.1.call-update) | async-done | bytes 144
  1290.0 130.4 %reduce-scatter.35.cloned.1.call-done = f32[16,2]{1,0:T(8,128)} async-done(((f32[512,2]{1,0:T(8,128)}), f32[16,2]{1,0:T(8,128)}) %reduce-scatter.35.cloned.1.call-update) | async-done | bytes 144
  1428.6 125.2 %reduce-scatter.29.cloned.1.call-done = f32[16,512]{1,0:T(8,128)} async-done(((f32[512,512]{1,0:T(8,128)}), f32[16,512]{1,0:T(8,128)}) %reduce-scatter.29.cloned.1.call-update) | async-done | bytes 32784 | tf_op jit(solution)/shard_map/reduce_scatter | solution.py:313
  1553.8 133.7 %reduce-scatter.27.cloned.1.call-done = f32[16,512]{1,0:T(8,128)} async-done(((f32[512,512]{1,0:T(8,128)}), f32[16,512]{1,0:T(8,128)}) %reduce-scatter.27.cloned.1.call-update) | async-done | bytes 32784 | tf_op jit(solution)/shard_map/reduce_scatter | solution.py:312
  1687.4 133.4 %reduce-scatter.25.cloned.1.call-done = f32[16,512]{1,0:T(8,128)} async-done(((f32[512,512]{1,0:T(8,128)}), f32[16,512]{1,0:T(8,128)}) %reduce-scatter.25.cloned.1.call-update) | async-done | bytes 32784 | tf_op jit(solution)/shard_map/reduce_scatter | solution.py:311
  1820.8 104.2 %reduce-scatter.31.cloned.1.call-done = f32[16,1536]{1,0:T(8,128)} async-done(((f32[512,1536]{1,0:T(8,128)}), f32[16,1536]{1,0:T(8,128)}) %reduce-scatter.31.cloned.1.call-update) | async-done | bytes 98320
  (826 shorter events, 615.0 us)
Async XLA Ops:
  7.2 61.4 %all-gather.8.cloned.1.call-start = ((), (), s32[]{:S(2)}) async-start(), calls=%async_computation.10 | async-start | bytes 1622016 | tf_op jit(solution)/shard_map/all_gather | solution.py:110
  7.9 296.1 %all-gather.14.cloned.1.call-start = ((), (), s32[]{:S(2)}) async-start(), calls=%async_computation.13 | async-start | bytes 3932160 | tf_op jit(solution)/shard_map/all_gather | solution.py:138
  72.9 235.9 %all-gather.16.cloned.1.call-start = ((), (), s32[]{:S(2)}) async-start(), calls=%async_computation.14 | async-start | bytes 3932160 | tf_op jit(solution)/shard_map/all_gather | solution.py:139
  73.7 373.1 %all-gather.10.cloned.1.call-start = ((), (), s32[]{:S(2)}) async-start(), calls=%async_computation.11 | async-start | bytes 3932160 | tf_op jit(solution)/shard_map/all_gather | solution.py:138
  78.6 375.3 %all-gather.12.cloned.1.call-start = ((), (), s32[]{:S(2)}) async-start(), calls=%async_computation.12 | async-start | bytes 3932160 | tf_op jit(solution)/shard_map/all_gather | solution.py:139
  80.3 41.7 %copy-start.111 = (bf16[2,16]{1,0:T(2,128)(2,1)S(1)}, bf16[2,16]{1,0:T(2,128)(2,1)}, u32[]{:S(2)}) copy-start(bf16[2,16]{1,0:T(2,128)(2,1)} %param.29) | copy-start | bytes 196
  160.2 11.0 copy-start.103
  160.5 16.9 copy-start.30
  160.5 18.2 copy-start.93
  160.6 57.8 %copy-start.94 = (bf16[16,512]{1,0:T(8,128)(2,1)S(1)}, bf16[16,512]{1,0:T(8,128)(2,1)}, u32[]{:S(2)}) copy-start(bf16[16,512]{1,0:T(8,128)(2,1)} %param.26) | copy-start | bytes 49156
  160.9 140.3 %copy-start.18 = (bf16[1,1,768,512]{2,3,1,0:T(8,128)(2,1)}, bf16[1,1,768,512]{2,3,1,0:T(8,128)(2,1)S(1)}, u32[]{:S(2)}) copy-start(bf16[1,1,768,512]{2,3,1,0:T(8,128)(2,1)S(1)} %copy.166) | copy-start | bytes 2359300
  160.9 98.2 %copy-start.95 = (bf16[16,512]{1,0:T(8,128)(2,1)S(1)}, bf16[16,512]{1,0:T(8,128)(2,1)}, u32[]{:S(2)}) copy-start(bf16[16,512]{1,0:T(8,128)(2,1)} %param.27) | copy-start | bytes 49156
  178.8 123.8 %copy-start.48 = (bf16[1,768,512]{2,1,0:T(8,128)(2,1)S(1)}, bf16[1,768,512]{2,1,0:T(8,128)(2,1)}, u32[]{:S(2)}) copy-start(bf16[1,768,512]{2,1,0:T(8,128)(2,1)} %get-tuple-element.947) | copy-start | bytes 2359300
  218.4 413.5 %copy-start.28 = (bf16[512,512]{1,0:T(8,128)(2,1)}, bf16[512,512]{1,0:T(8,128)(2,1)S(1)}, u32[]{:S(2)}) copy-start(bf16[512,512]{1,0:T(8,128)(2,1)S(1)} %all_gather.55) | copy-start | bytes 1572868
  303.8 801.8 %reduce-scatter.17.cloned.1.call-start = ((), (), s32[]{:S(2)}) async-start(), calls=%async_computation.15 | async-start | bytes 3932160 | tf_op jit(solution)/shard_map/reduce_scatter | solution.py:287
  323.5 8.8 copy-start
  345.4 9.2 copy-start
  367.6 9.2 copy-start
  389.9 9.2 copy-start
  412.1 9.2 copy-start
  434.4 9.2 copy-start
  453.7 174.6 %copy-start.16 = (f32[768,512]{0,1:T(8,128)}, f32[768,512]{0,1:T(8,128)S(1)}, u32[]{:S(2)}) copy-start(f32[768,512]{0,1:T(8,128)S(1)} %get-tuple-element.979) | copy-start | bytes 4718596
  471.0 8.7 copy-start.1
  494.6 9.2 copy-start.1
  518.7 9.2 copy-start.1
  542.8 9.2 copy-start.1
  567.0 9.2 copy-start.1
  591.1 9.2 copy-start.1
  607.1 10.6 copy-start.35
  612.8 12.1 copy-start.24
  612.8 12.1 copy-start.82
  613.0 11.9 copy-start.91
  618.6 9.7 copy-start.14
  618.7 9.7 copy-start.68
  618.9 9.5 copy-start.73
  855.2 250.4 %reduce-scatter.19.cloned.1.call-start = ((), (), s32[]{:S(2)}) async-start(), calls=%async_computation.16 | async-start | bytes 3932160 | tf_op jit(solution)/shard_map/reduce_scatter | solution.py:290
  865.5 246.9 %reduce-scatter.21.cloned.1.call-start = ((), (), s32[]{:S(2)}) async-start(), calls=%async_computation.17 | async-start | bytes 3932160 | tf_op jit(solution)/shard_map/reduce_scatter | solution.py:287
  893.6 8.4 copy-start.7
  893.6 8.4 copy-start.34
  893.6 8.4 copy-start.86
  1078.3 74.9 %reduce-scatter.23.cloned.1.call-start = ((), (), s32[]{:S(2)}) async-start(), calls=%async_computation.18 | async-start | bytes 3932160 | tf_op jit(solution)/shard_map/reduce_scatter | solution.py:290
  1083.9 204.8 %reduce-scatter.33.cloned.1.call-start = ((), (), s32[]{:S(2)}) async-start(), calls=%async_computation.23 | async-start | bytes 270336
  1090.0 330.4 %reduce-scatter.35.cloned.1.call-start = ((), (), s32[]{:S(2)}) async-start(), calls=%async_computation.24 | async-start | bytes 270336
  1091.0 462.8 %reduce-scatter.29.cloned.1.call-start = ((), (), s32[]{:S(2)}) async-start(), calls=%async_computation.21 | async-start | bytes 1081344 | tf_op jit(solution)/shard_map/reduce_scatter | solution.py:313
  1094.7 592.7 %reduce-scatter.27.cloned.1.call-start = ((), (), s32[]{:S(2)}) async-start(), calls=%async_computation.20 | async-start | bytes 1081344 | tf_op jit(solution)/shard_map/reduce_scatter | solution.py:312
  1099.4 721.4 %reduce-scatter.25.cloned.1.call-start = ((), (), s32[]{:S(2)}) async-start(), calls=%async_computation.19 | async-start | bytes 1081344 | tf_op jit(solution)/shard_map/reduce_scatter | solution.py:311
  1103.1 822.0 %reduce-scatter.31.cloned.1.call-start = ((), (), s32[]{:S(2)}) async-start(), calls=%async_computation.22 | async-start | bytes 3244032
  1161.3 260.5 %copy-start.23 = (f32[768,512]{0,1:T(8,128)S(1)}, f32[768,512]{0,1:T(8,128)}, u32[]{:S(2)}) copy-start(f32[768,512]{0,1:T(8,128)} %copy-done.21) | copy-start | bytes 4718596
  (157 other events, 649.0 us)
Sparse Core Ops, SparseCore 0:
  10.9 57.6 all-gather.7
  73.1 27.4 all-gather.13
  102.2 28.6 all-gather.15
  132.2 28.5 all-gather.9
  303.9 24.6 all-gather.11
  855.3 34.0 reduce-scatter.16
  892.1 37.9 reduce-scatter.18
  1078.4 34.0 reduce-scatter.20
  1115.2 37.9 reduce-scatter.22
  1155.2 133.4 reduce-scatter.32
  1291.0 129.3 reduce-scatter.34
  1423.1 130.6 reduce-scatter.28
  1556.7 130.7 reduce-scatter.26
  1690.1 130.7 reduce-scatter.24
  1827.6 97.4 reduce-scatter.30
where the time goes:
time: 1940 us; the launch traced here: 1930 us
  waiting for transfers between devices  857 us (44%)
  matrix products  530 us (27%)
  blocking collectives  213 us (11%)
  local copies, waits for them, and re-layouts  187 us (10%)
  other arithmetic  110 us (6%)
    unnamed x18, waiting for transfers between devices  362 us
    reduce_scatter x1, waiting for transfers between devices, shards(): lax.psum_scatter(acc_up, ('dp', 'blk'), scatter_dimension=0, tiled=True)  134 us
    reduce_scatter x1, waiting for transfers between devices, shards(): lax.psum_scatter(acc_out, ('dp', 'blk'), scatter_dimension=0, tiled=True)  133 us
    reduce_scatter x1, waiting for transfers between devices, shards(): lax.psum_scatter(acc_down, ('dp', 'blk'), scatter_dimension=0, tiled=True)  125 us
    dot_general x12, matrix products, attend_one(): jnp.einsum('rqhk,rkhd->rqhd', exps.astype(jnp.bfloat16), value_h, preferr...  99.6 us
    dot_general x12, matrix products, attend_one(): jnp.einsum('rqhd,rkhd->rqhk', queries, key_h, preferred_element_type=jnp....  86.1 us
    dot_general x12, matrix products, score_grads(): jnp.einsum('rqhd,rkhd->rqhk', out_h, value_h, preferred_element_type=jnp....  78.2 us
    dot_general x12, matrix products, pair_grads(): jnp.einsum('rqhk,rkhd->rqhd', grad_scores, key_h, preferred_element_type=...  69.2 us
  transfers between devices with their start and end apart: 15, of which 9 were waited for; matrix products, arithmetic and copies ran while one was open for 20% of the time, Pallas kernels for 0%

commit v1 on v0

v1 whole, which is shorter than its diff:
```python
import functools, math
import jax, jax.numpy as jnp
from jax import lax
from jax.experimental import pallas as pl
from jax.experimental.pallas import tpu as pltpu
from jax.sharding import PartitionSpec as P

HEADS = 8
bf=jnp.bfloat16; f32=jnp.float32
HEAD=64
QB=512
KB=512
SRC=512
SAFE=60.0
CODE=16
SLOTS=3
def dot(a,b,ca,cb): return lax.dot_general(a,b,(((ca,),(cb,)),((),())),preferred_element_type=f32)
def al(x,n): return pl.multiple_of(x,n)
def iota(shape,axis): return lax.broadcasted_iota(jnp.int32,shape,axis)

class Counts:
    def __init__(self,L):
        self.nd=L//256; self.ns=L//SRC; self.nq=L//QB
        self.total=0; self.src=1; self.start=self.src+2*self.nd; self.size=self.start+self.nq; self.begin=self.size+self.nq
        self.length=self.begin+self.nd

def window(cnt_ref,at,i):
    groups=cnt_ref[at.size+i]
    full=(groups-1)//(KB//128)
    return cnt_ref[at.start+i],full,groups-full*(KB//128)

def by_piece(first,full,rest,g,fn):
    def body(j,g):
        fn(al(first+j*KB,128),KB,g)
        return g+1
    g=lax.fori_loop(0,full,body,g)
    for r in range(1,KB//128+1):
        @pl.when(rest==r)
        def _(): fn(al(first+full*KB,128),r*128,g)
    return g+1

def attend_kernel(L,H,cnt_ref,qkvt_ref,codet_ref,meta_ref,p_hbm,att_hbm,ot_hbm,inv_ref,kaug_hbm,vaug_hbm,
                  kaug_ref,vaug_ref,kvt,vct,acc,pbuf,obuf,abuf,top_ref,psem,osem,asem,ksem):
    W=H*HEAD; at=Counts(L)
    total=cnt_ref[at.total]
    for h in range(H):
        kvt[h*128:h*128+HEAD,:]=qkvt_ref[W+h*HEAD:W+(h+1)*HEAD,:]
        kvt[h*128+HEAD:h*128+HEAD+CODE,:]=codet_ref[...]
        kvt[h*128+HEAD+CODE:(h+1)*128,:]=jnp.zeros((HEAD-CODE,L),bf)
    lane=iota((256,128),1)
    down=iota((256,SRC),0)
    def dest(d,c):
        def src(s,a):
            ssl=pl.ds(al(s*SRC,SRC),SRC)
            oh=(meta_ref[0:1,ssl]==(down+d*256)).astype(f32).astype(bf)
            ka=a[0]+dot(oh,kvt[:,ssl],1,1)
            va=a[1]+dot(oh,qkvt_ref[2*W:3*W,ssl],1,1)
            return ka,va
        ka,va=lax.fori_loop(cnt_ref[at.src+2*d],cnt_ref[at.src+1+2*d],src,(jnp.zeros((256,H*128),f32),jnp.zeros((256,W),f32)))
        dsl=pl.ds(al(d*256,256),256)
        vat=va.T
        for h in range(H):
            k1=ka[:,h*128:(h+1)*128]
            kaug_ref[h,dsl,:]=jnp.where(lane==HEAD+10,-2560.0,k1).astype(bf)
            pair=va[:,(h//2)*128:(h//2+1)*128]
            if h%2: pair=jnp.concatenate([pair[:,HEAD:],pair[:,:HEAD]],1)
            vaug_ref[h,dsl,:]=jnp.where(lane<HEAD,pair,jnp.where(lane<HEAD+3,-1.0,0.0)).astype(bf)
            vct[h,:HEAD,dsl]=vat[h*HEAD:(h+1)*HEAD,:].astype(bf)
            vct[h,HEAD:HEAD+16,dsl]=jnp.ones((16,256),bf)
        return c
    lax.fori_loop(0,(total+255)//256,dest,0)
    keep=[pltpu.make_async_copy(kaug_ref,kaug_hbm,ksem.at[0]),pltpu.make_async_copy(vaug_ref,vaug_hbm,ksem.at[1])]
    for x in keep: x.start()
    bound=jnp.float32(0)
    for h in range(H):
        q=qkvt_ref[h*HEAD:(h+1)*HEAD,:].astype(f32); k=qkvt_ref[W+h*HEAD:W+(h+1)*HEAD,:].astype(f32)
        bound=jnp.maximum(bound,jnp.max(jnp.sum(q*q,0,keepdims=True))*jnp.max(jnp.sum(k*k,0,keepdims=True)))
    safe=bound<SAFE*SAFE

    def pcopy(g):
        slot=lax.rem(g,SLOTS)
        return pltpu.make_async_copy(pbuf.at[slot],p_hbm.at[g],psem.at[slot])
    def ocopy(i):
        slot=lax.rem(i,2)
        return pltpu.make_async_copy(obuf.at[slot],ot_hbm.at[i],osem.at[slot])
    def acopy(i):
        slot=lax.rem(i,2)
        return pltpu.make_async_copy(abuf.at[slot],att_hbm.at[:,pl.ds(al(i*QB,QB),QB),:],asem.at[slot])
    def block(i,g):
        slot=lax.rem(i,2)
        qsl=pl.ds(al(i*QB,QB),QB)
        first,full,rest=window(cnt_ref,at,i)
        qa=[jnp.concatenate([qkvt_ref[h*HEAD:(h+1)*HEAD,qsl],codet_ref[:,qsl],jnp.zeros((HEAD-CODE,QB),bf)],0) for h in range(H)]
        own=meta_ref[1:2,qsl]>0
        sself=[]
        for h in range(H):
            x=qkvt_ref[h*HEAD:(h+1)*HEAD,qsl].astype(f32)*qkvt_ref[W+h*HEAD:W+(h+1)*HEAD,qsl].astype(f32)
            sself.append(jnp.where(own,jnp.sum(x,0,keepdims=True),-1e30))
        acc[...]=jnp.zeros_like(acc)
        top_ref[...]=jnp.zeros_like(top_ref)
        row=iota((128,QB),0)
        def strict(h,osl):
            k=kaug_ref[h,osl,:]
            x=qa[h].astype(f32)
            plain=dot(k,jnp.where(row<HEAD,x,0.0).astype(bf),1,0)
            return jnp.where(dot(k,jnp.where(row<HEAD,0.0,x).astype(bf),1,0)>-1.0,plain,-1e30)
        @pl.when(jnp.logical_not(safe))
        def _():
            for h in range(H):
                def more(j,m): return jnp.maximum(m,jnp.max(strict(h,pl.ds(al(first+j*128,128),128)),0,keepdims=True))
                top_ref[h:h+1,:]=lax.fori_loop(0,cnt_ref[at.size+i],more,sself[h])
        def piece(off,size,g):
            ps=lax.rem(g,SLOTS)
            osl=pl.ds(off,size)
            @pl.when(g>=SLOTS)
            def _(): pcopy(g-SLOTS).wait()
            @pl.when(safe)
            def _():
                keepp=[]
                for h in range(H):
                    p=jnp.exp2(dot(kaug_ref[h,osl,:],qa[h],1,0)).astype(bf)
                    pbuf[ps,h,:size,:]=p
                    keepp.append(p)
                for h in range(H): acc[h]+=dot(vct[h,:,osl],keepp[h],1,0)
            @pl.when(jnp.logical_not(safe))
            def _():
                for h in range(H):
                    def put(j,c):
                        jsl=pl.ds(al(off+j*128,128),128)
                        p=jnp.exp2(strict(h,jsl)-top_ref[h:h+1,:]).astype(bf)
                        pbuf[ps,h,pl.ds(al(j*128,128),128),:]=p
                        acc[h]+=dot(vct[h,:,jsl],p,1,0)
                        return c
                    lax.fori_loop(0,size//128,put,0)
            pcopy(g).start()
        g=by_piece(first,full,rest,g,piece)
        @pl.when(i>=2)
        def _(): ocopy(i-2).wait(); acopy(i-2).wait()
        for h in range(H):
            ps=jnp.exp2(sself[h]-top_ref[h:h+1,:])
            inv=1.0/(acc[h,HEAD:HEAD+1,:]+ps)
            obuf[slot,h*HEAD:(h+1)*HEAD,:]=(acc[h,:HEAD,:]+ps*qkvt_ref[2*W+h*HEAD:2*W+(h+1)*HEAD,qsl].astype(f32))*inv
            inv_ref[h,0:1,qsl]=inv
            inv_ref[h,1:2,qsl]=ps
        for hp in range(H//2): abuf[slot,hp]=obuf[slot,hp*128:(hp+1)*128,:].T.astype(bf)
        ocopy(i).start(); acopy(i).start()
        return g
    g=lax.fori_loop(0,at.nq,block,0)
    for s in range(SLOTS):
        last=g-1-s
        @pl.when(last>=0)
        def _(): pcopy(last).wait()
    for i in range(max(at.nq-2,0),at.nq): ocopy(i).wait(); acopy(i).wait()
    for x in keep: x.wait()

def attend(cnt,qkvt,codet,meta,H):
    L=qkvt.shape[1]; W=H*HEAD; nq=L//QB; cap=nq*(L//KB+1)
    V=pl.BlockSpec(memory_space=pltpu.VMEM); A=pl.BlockSpec(memory_space=pl.ANY)
    S=jax.ShapeDtypeStruct; M=pltpu.VMEM; D=pltpu.SemaphoreType.DMA
    return pl.pallas_call(functools.partial(attend_kernel,L,H),
        out_shape=[S((cap,H,KB,QB),bf),S((H//2,L,128),bf),S((nq,W,QB),f32),S((H,8,L),f32),S((H,L,128),bf),S((H,L,128),bf)],
        in_specs=[pl.BlockSpec(memory_space=pltpu.SMEM),V,V,V],
        out_specs=[A,A,A,V,A,A],
        scratch_shapes=[M((H,L,128),bf),M((H,L,128),bf),M((H*128,L),bf),M((H,HEAD+16,L),bf),M((H,HEAD+16,QB),f32),M((SLOTS,H,KB,QB),bf),
            M((2,W,QB),f32),M((2,H//2,QB,128),bf),M((8,QB),f32),D((SLOTS,)),D((2,)),D((2,)),D((2,))],
        compiler_params=pltpu.CompilerParams(vmem_limit_bytes=56<<20))(cnt,qkvt,codet,meta)

def flags(seg,pad,known):
    L=seg.shape[0]; at=Counts(L)
    use=(pad==0)&(known==1)
    csum=jnp.cumsum(use.astype(jnp.int32))
    rank=jnp.where(use,csum-1,-1)
    own=((pad==0)&(known!=1)).astype(jnp.int32)
    bits=jnp.arange(CODE,dtype=jnp.int32)[:,None]
    codet=jnp.where(bits<10,jnp.where(((seg[None,:]>>jnp.minimum(bits,9))&1)==1,16.0,-16.0),jnp.where(bits==10,1.0,0.0)).astype(bf)
    meta=jnp.concatenate([rank[None],own[None],jnp.zeros((6,L),jnp.int32)],0)
    def edges(n):
        ends=csum.reshape(n,-1)[:,-1]
        return jnp.concatenate([jnp.zeros(1,jnp.int32),ends[:-1]]),ends
    begins,ends=edges(L//SRC)
    d=jnp.arange(at.nd,dtype=jnp.int32)*256
    lo=jnp.sum((ends[None,:]<=d[:,None]).astype(jnp.int32),1)
    hi=jnp.sum((begins[None,:]<d[:,None]+256).astype(jnp.int32),1)
    blocks=seg.reshape(at.nq,QB)
    low=jnp.sum((use[None,:]&(seg[None,:]<blocks[:,:1])).astype(jnp.int32),1)//128*128
    high=jnp.sum((use[None,:]&(seg[None,:]<=blocks[:,-1:])).astype(jnp.int32),1)
    cnt=jnp.concatenate([csum[-1:],jnp.stack([lo,hi],1).reshape(-1),low,(high-low+127)//128,edges(at.nd)[0]])
    return cnt,codet,meta
LN2=math.log(2.0)
def back_kernel(L,H,cnt_ref,datt_ref,p_hbm,ot_ref,inv_ref,kaug_ref,vaug_ref,qkvt_ref,meta_ref,tok_hbm,w_ref,
                tg_hbm,grad_ref,kct,dkv,dkvt,dq_ref,pbuf,qacc,tok_ref,tbuf,psem,tsem,ksem):
    W=H*HEAD; at=Counts(L)
    total=cnt_ref[at.total]; groups=(total+127)//128
    pieces=lax.fori_loop(0,at.nq,lambda i,s:s+(cnt_ref[at.size+i]+KB//128-1)//(KB//128),0)
    def pcopy(g):
        slot=lax.rem(g,SLOTS)
        return pltpu.make_async_copy(p_hbm.at[g],pbuf.at[slot],psem.at[slot])
    for s in range(SLOTS-1):
        @pl.when(s<pieces)
        def _(): pcopy(s).start()
    tcopy=pltpu.make_async_copy(tok_hbm,tok_ref,ksem.at[0])
    tcopy.start()
    def prep(j,c):
        jsl=pl.ds(al(j*128,128),128)
        for h in range(H): kct[h,:,jsl]=kaug_ref[h,jsl,:].T[:HEAD]
        dkv[jsl,:]=jnp.zeros((128,2*W),f32)
        return c
    lax.fori_loop(0,groups,prep,0)
    def block(i,g):
        qsl=pl.ds(al(i*QB,QB),QB)
        first,full,rest=window(cnt_ref,at,i)
        dt=jnp.concatenate([datt_ref[hp,qsl,:].astype(f32).T for hp in range(H//2)],0)
        prod=dt*ot_ref[i]
        daug=[];dz=[];qz=[];deltas=[];d1s=[]
        zero=jnp.zeros((HEAD,QB),bf)
        row=iota((16,QB),0)
        for h in range(H):
            hsl=slice(h*HEAD,(h+1)*HEAD)
            inv=inv_ref[h,0:1,qsl]
            delta=jnp.sum(prod[hsl],0,keepdims=True)*inv
            d1=dt[hsl]*inv
            low=d1.astype(bf)
            a=delta.astype(bf).astype(f32); b=(delta-a).astype(bf).astype(f32)
            extra=jnp.where(row==0,a,jnp.where(row==1,b,jnp.where(row==2,delta-a-b,0.0))).astype(bf)
            daug.append(jnp.concatenate([low,extra,jnp.zeros((HEAD-16,QB),bf)],0))
            q=qkvt_ref[hsl,qsl]
            dz.append(jnp.concatenate([zero,low] if h%2 else [low,zero],0))
            qz.append(jnp.concatenate([zero,q] if h%2 else [q,zero],0))
            deltas.append(delta); d1s.append(d1)
        qacc[...]=jnp.zeros_like(qacc)
        def piece(off,size,g):
            slot=lax.rem(g,SLOTS)
            osl=pl.ds(off,size)
            @pl.when(g+SLOTS-1<pieces)
            def _(): pcopy(g+SLOTS-1).start()
            pcopy(g).wait()
            dss=[]
            for h in range(H):
                dss.append((pbuf[slot,h,:size,:].astype(f32)*dot(vaug_ref[h,osl,:],daug[h],1,0)).astype(bf))
            for h in range(H): qacc[h*HEAD:(h+1)*HEAD,:]+=dot(kct[h,:,osl],dss[h],1,0)
            for h in range(0,H,2):
                dkv[osl,h*HEAD:(h+2)*HEAD]+=dot(dss[h],qz[h],1,1)+dot(dss[h+1],qz[h+1],1,1)
                dkv[osl,W+h*HEAD:W+(h+2)*HEAD]+=dot(pbuf[slot,h,:size,:],dz[h],1,1)+dot(pbuf[slot,h+1,:size,:],dz[h+1],1,1)
        g=by_piece(first,full,rest,g,piece)
        for h in range(H):
            hsl=slice(h*HEAD,(h+1)*HEAD); ksl=slice(W+h*HEAD,W+(h+1)*HEAD); vsl=slice(2*W+h*HEAD,2*W+(h+1)*HEAD)
            ps=inv_ref[h,1:2,qsl]
            ds=ps*(jnp.sum(qkvt_ref[vsl,qsl].astype(f32)*d1s[h],0,keepdims=True)-deltas[h])
            dq_ref[hsl,qsl]=((qacc[hsl,:]+ds*qkvt_ref[ksl,qsl].astype(f32))*0.125).astype(bf)
            dq_ref[ksl,qsl]=(ds*qkvt_ref[hsl,qsl].astype(f32)*LN2).astype(bf)
            dq_ref[vsl,qsl]=(ps*d1s[h]).astype(bf)
        return g
    lax.fori_loop(0,at.nq,block,0)
    lanes=iota((128,2*W),1)
    def turn(j,c):
        jsl=pl.ds(al(j*128,128),128)
        x=jnp.where(j<groups,dkv[jsl,:],0.0)
        dkvt[:,jsl]=jnp.where(lanes<W,x*LN2,x).astype(bf).T
        return c
    lax.fori_loop(0,groups+3,turn,0)
    deep=iota((384,256),0)
    def tgcopy(s):
        slot=lax.rem(s,2)
        return pltpu.make_async_copy(tbuf.at[slot],tg_hbm.at[pl.ds(al(s*256,256),256),:],tsem.at[slot])
    def place(s,c):
        ssl=pl.ds(al(s*256,256),256)
        r0=cnt_ref[at.begin+s]//128*128
        oh=(meta_ref[0:1,ssl]==deep+r0).astype(f32).astype(bf)
        g=dot(dkvt[:,pl.ds(al(r0,128),384)],oh,1,0)+dq_ref[W:3*W,ssl].astype(f32)
        dq_ref[W:3*W,ssl]=g.astype(bf)
        @pl.when(s>=2)
        def _(): tgcopy(s-2).wait()
        tbuf[lax.rem(s,2)]=dot(dq_ref[:,ssl],w_ref[...],0,1).astype(bf)
        tgcopy(s).start()
        return c
    lax.fori_loop(0,at.nd,place,0)
    tcopy.wait()
    grad_ref[...]=dot(dq_ref[...],tok_ref[...],1,0)
    for s in range(at.nd-2,at.nd): tgcopy(s).wait()

def back(cnt,datt,p,ot,inv,kaug,vaug,qkvt,meta,tok,w,H):
    L=qkvt.shape[1]; W=H*HEAD; E=tok.shape[1]
    V=pl.BlockSpec(memory_space=pltpu.VMEM); A=pl.BlockSpec(memory_space=pl.ANY)
    S=jax.ShapeDtypeStruct; M=pltpu.VMEM; D=pltpu.SemaphoreType.DMA
    return pl.pallas_call(functools.partial(back_kernel,L,H),
        out_shape=[S((L,E),bf),S((3*W,E),f32)],
        in_specs=[pl.BlockSpec(memory_space=pltpu.SMEM),V,A]+[V]*6+[A,V],
        out_specs=[A,V],
        scratch_shapes=[M((H,HEAD,L),bf),M((L,2*W),f32),M((2*W,L+384),bf),M((3*W,L),bf),M((SLOTS,H,KB,QB),bf),M((W,QB),f32),
            M((L,E),bf),M((2,256,E),bf),D((SLOTS,)),D((2,)),D((1,))],
        compiler_params=pltpu.CompilerParams(vmem_limit_bytes=56<<20))(cnt,datt,p,ot,inv,kaug,vaug,qkvt,meta,tok,w)
EPSILON=1e-05
def erf(x):
    x=jnp.clip(x,-3.832506856900711,3.832506856900711)
    x2=x*x
    top=0.00022905065861350646
    for c in (0.0034082910107109506,0.050955695062380861,0.18520832239976145,1.128379143519084): top=top*x2+c
    low=-1.1791602954361697e-7
    for c in (0.000023547966471313185,0.0010179625278914885,0.014070470171167667,0.11098505178285362,0.49746925110067538,1.0): low=low*x2+c
    return x*top/low
def norm(x):
    center=x-jnp.mean(x,-1,keepdims=True)
    inverse=lax.rsqrt(jnp.mean(center*center,-1,keepdims=True)+EPSILON)
    return center*inverse,inverse
def norm_back(e,n,inverse):
    return inverse*(e-jnp.mean(e,-1,keepdims=True)-n*jnp.mean(e*n,-1,keepdims=True))
def middle_kernel(a0_ref,a1_ref,tok_ref,cot_ref,wo_ref,wu_ref,wd_ref,gs_ref,out_ref,r1_ref,da_ref,go_ref,gu_ref,gd_ref,gg_ref):
    @pl.when(pl.program_id(0)==0)
    def _():
        for r in (go_ref,gu_ref,gd_ref,gg_ref): r[...]=jnp.zeros_like(r)
    P2=a0_ref.shape[0]
    att=jnp.concatenate([a0_ref[p] for p in range(P2)]+[a1_ref[p] for p in range(P2)],1)
    g0,g1,b0,b1=[gs_ref[r:r+1,:] for r in range(4)]
    n1,inv1=norm(tok_ref[...].astype(f32)+dot(att,wo_ref[...],1,0))
    first=(n1*g0+b0).astype(bf)
    hidden=dot(first,wu_ref[...],1,0)
    cdf=0.5*(1.0+erf(hidden*math.sqrt(0.5)))
    act=(hidden*cdf).astype(bf)
    slope=cdf+hidden*jnp.exp(-0.5*hidden*hidden)*(1.0/math.sqrt(2.0*math.pi))
    n2,inv2=norm(first.astype(f32)+dot(act,wd_ref[...],1,0))
    out_ref[...]=(n2*g1+b1).astype(bf)
    cot=cot_ref[...].astype(f32)
    r2=norm_back(cot*g1,n2,inv2)
    feed=r2.astype(bf)
    gd_ref[...]+=dot(act,feed,0,0)
    dh=(dot(feed,wd_ref[...],1,1)*slope).astype(bf)
    gu_ref[...]+=dot(first,dh,0,0)
    df=r2+dot(dh,wu_ref[...],1,1)
    r1=norm_back(df*g0,n1,inv1)
    r1_ref[...]=r1
    db=r1.astype(bf)
    go_ref[...]+=dot(att,db,0,0)
    da=dot(db,wo_ref[...],1,1).astype(bf)
    for p in range(2*P2): da_ref[p]=da[:,p*128:(p+1)*128]
    gg_ref[0:1,:]+=jnp.sum(df*n1,0,keepdims=True)
    gg_ref[1:2,:]+=jnp.sum(cot*n2,0,keepdims=True)
    gg_ref[2:3,:]+=jnp.sum(df,0,keepdims=True)
    gg_ref[3:4,:]+=jnp.sum(cot,0,keepdims=True)

def middle(a0,a1,tok,cot,wo,wu,wd,gs):
    P2,N,_=a0.shape; D=tok.shape[1]; F=wu.shape[1]
    T=max(t for t in (256,192,128,64,32,16) if N%t==0)
    tile=pl.BlockSpec((T,D),lambda i:(i,0))
    def pairs(k): return pl.BlockSpec((k,T,128),lambda i:(0,i,0))
    def whole(s): return pl.BlockSpec(s,lambda i:(0,)*len(s))
    return pl.pallas_call(middle_kernel,grid=(N//T,),
        in_specs=[pairs(P2),pairs(P2),tile,tile,whole((D,D)),whole((D,F)),whole((F,D)),whole((8,D))],
        out_specs=[tile,tile,pairs(2*P2),whole((D,D)),whole((D,F)),whole((F,D)),whole((8,D))],
        out_shape=[jax.ShapeDtypeStruct((N,D),bf),jax.ShapeDtypeStruct((N,D),f32),jax.ShapeDtypeStruct((2*P2,N,128),bf),
            jax.ShapeDtypeStruct((D,D),f32),jax.ShapeDtypeStruct((D,F),f32),jax.ShapeDtypeStruct((F,D),f32),jax.ShapeDtypeStruct((8,D),f32)],
        compiler_params=pltpu.CompilerParams(vmem_limit_bytes=60<<20))(a0,a1,tok,cot,wo,wu,wd,gs)
MESH=pl.DeviceIdType.MESH
class Net:
    def __init__(self,Z):
        dp=lax.axis_index("dp"); blk=lax.axis_index("blk")
        self.Z=Z; self.z=dp//2; self.y=dp%2; self.j=blk//2; self.c=blk%2
        self.sent=[]
    def at(self,z=None,y=None,j=None,c=None):
        z=self.z if z is None else z; y=self.y if y is None else y; j=self.j if j is None else j; c=self.c if c is None else c
        return (z*2+y,j*2+c)
    def greet(self):
        barrier=pltpu.get_barrier_semaphore()
        def signal(d): pl.semaphore_signal(barrier,inc=1,device_id=d,device_id_type=MESH)
        signal(self.at(j=1-self.j)); signal(self.at(y=1-self.y)); signal(self.at(c=1-self.c))
        @pl.when(self.z>0)
        def _(): signal(self.at(z=self.z-1))
        @pl.when(self.z<self.Z-1)
        def _(): signal(self.at(z=self.z+1))
        pl.semaphore_wait(barrier,3+(self.z>0).astype(jnp.int32)+(self.z<self.Z-1).astype(jnp.int32))
    def copy(self,src,dst,ssem,rsem,device):
        return pltpu.make_async_remote_copy(src_ref=src,dst_ref=dst,send_sem=ssem,recv_sem=rsem,device_id=device,device_id_type=MESH)
    def send(self,src,dst,ssem,rsem,device,when=None):
        c=self.copy(src,dst,ssem,rsem,device)
        if when is None: c.start()
        else: pl.when(when)(c.start)
        self.sent.append((c,when))
    def drain(self):
        for c,when in self.sent:
            if when is None: c.wait_send()
            else: pl.when(when)(c.wait_send)

def gather_kernel(Z,block,E,W,waves,rows,tok_hbm,info_ref,pack_ref,tok_out,info_out,wall_out,wmine_out,qkvt_out,
                  tokb,infob,wall,wt,qkvt,lsem,qsem,xs,xr,zs,zr,ys,yr,cs,cr,ts,tr,iss,isr):
    net=Net(Z); z,y,j,c=net.z,net.y,net.j,net.c
    NCH=block//rows; D=E
    sib=net.at(c=1-c); xd=net.at(j=1-j); yd=net.at(y=1-y)
    mine=pltpu.make_async_copy(tok_hbm.at[j],tokb.at[j,c],lsem.at[0]); mine.start()
    wall[z,y,j,c]=pack_ref[...]
    infob[j,c]=info_ref[j]
    net.greet()
    NW=len(waves)
    cut=[pl.ds(a,b-a) for a,b in waves]
    for w in range(NW): net.send(pack_ref.at[:,cut[w]],wall.at[z,y,j,c,:,cut[w]],xs.at[w],xr.at[w],xd)
    net.send(info_ref.at[1-j],infob.at[j,c],iss.at[0],isr.at[0],xd)
    net.send(info_ref.at[j],infob.at[j,c],iss.at[1],isr.at[1],sib)
    def chunk(k): return pl.ds(k*rows,rows)
    for k in range(NCH):
        net.send(tok_hbm.at[1-j,chunk(k)],tokb.at[j,c,chunk(k)],ts.at[0,k],tr.at[0,k],xd)
        net.send(tok_hbm.at[j,chunk(k)],tokb.at[j,c,chunk(k)],ts.at[1,k],tr.at[1,k],sib)
    def piece(w,o,y_): return wall.at[o,y_,:,c,:,cut[w]]
    def arrived(w,o,y_,sem): pltpu.make_async_copy(piece(w,o,y_),piece(w,o,y_),sem).wait()
    def spread(w,o,when=None):
        net.send(piece(w,o,y),piece(w,o,y),ys.at[w,o],yr.at[w,o],yd,when)
        net.send(piece(w,o,y),piece(w,o,y),cs.at[w,0,o],cr.at[w,0,o],sib,when)
    def across(w,o,when=None):
        def go(): arrived(w,o,1-y,yr.at[w,o])
        go() if when is None else pl.when(when)(go)
        net.send(piece(w,o,1-y),piece(w,o,1-y),cs.at[w,1,o],cr.at[w,1,o],sib,when)
    def step(w,k):
        if k==0:
            pltpu.make_async_copy(wall.at[z,y,1-j,c,:,cut[w]],wall.at[z,y,1-j,c,:,cut[w]],xr.at[w]).wait()
            net.send(piece(w,z,y),piece(w,z,y),zs.at[w,0,0],zr.at[w,z],net.at(z=z+1),z<Z-1)
            net.send(piece(w,z,y),piece(w,z,y),zs.at[w,1,0],zr.at[w,z],net.at(z=z-1),z>0)
            spread(w,z)
            return
        for d,(o,here,more) in enumerate(((z-k,z-k>=0,(z-k>=0)&(z<Z-1)),(z+k,z+k<Z,(z+k<Z)&(z>0)))):
            at=jnp.clip(o,0,Z-1)
            @pl.when(here)
            def _(): arrived(w,at,y,zr.at[w,at])
            net.send(piece(w,at,y),piece(w,at,y),zs.at[w,d,k],zr.at[w,at],net.at(z=z+1 if d==0 else z-1),more)
            spread(w,at,here)
        if k==1: across(w,z)
        else:
            for o,here in ((z-k+1,z-k+1>=0),(z+k-1,z+k-1<Z)): across(w,jnp.clip(o,0,Z-1),here)
    def finish(w):
        for o,here in ((z-Z+1,z-Z+1>=0),(z+Z-1,z+Z-1<Z)): across(w,jnp.clip(o,0,Z-1),here)
    def from_sibling(w):
        for o in range(Z):
            for q in range(2):
                ref=wall.at[o,y if q==0 else 1-y,:,1-c,:,cut[w]]
                pltpu.make_async_copy(ref,ref,cr.at[w,q,o]).wait()
    def project(jj,cc,k):
        g=(jj*2+cc)*NCH+k
        r=dot(wt[...],tokb[jj,cc,chunk(k),:],1,1)
        col=pl.ds(al(g*rows,rows),rows)
        qkvt[:,col]=jnp.concatenate([r[:W]*(math.log2(math.e)/8),r[W:]],0).astype(bf)
        out=pltpu.make_async_copy(qkvt.at[:,col],qkvt_out.at[:,col],qsem.at[g])
        out.start()
        return out
    for k in range(Z):
        step(0,k)
        if k>=1: step(1,k-1)
    finish(0)
    from_sibling(0)
    keep=[]
    parts=[]
    for t in range(3):
        cols=pl.ds(al(t*2*W+c*W,W),W)
        part=wall[:,:,:,:,:,cols].reshape(D,W)
        wt[t*W:(t+1)*W,:]=part.T
        parts.append(part)
    wmine_out[...]=jnp.concatenate(parts,1)
    mine.wait()
    for k in range(NCH): keep.append(project(j,c,k))
    step(1,Z-1)
    for k in range(NCH):
        ref=tokb.at[j,1-c,chunk(k)]
        pltpu.make_async_copy(ref,ref,tr.at[1,k]).wait()
        keep.append(project(j,1-c,k))
    finish(1)
    for k in range(NCH):
        ref=tokb.at[1-j,c,chunk(k)]
        pltpu.make_async_copy(ref,ref,tr.at[0,k]).wait()
        net.send(ref,ref,ts.at[2,k],tr.at[2,k],sib)
        keep.append(project(1-j,c,k))
        if k==0:
            pltpu.make_async_copy(infob.at[1-j,c],infob.at[1-j,c],isr.at[0]).wait()
            net.send(infob.at[1-j,c],infob.at[1-j,c],iss.at[2],isr.at[2],sib)
    from_sibling(1)
    outw=pltpu.make_async_copy(wall,wall_out,lsem.at[1]); outw.start()
    for k in range(NCH):
        ref=tokb.at[1-j,1-c,chunk(k)]
        pltpu.make_async_copy(ref,ref,tr.at[2,k]).wait()
        keep.append(project(1-j,1-c,k))
    outt=pltpu.make_async_copy(tokb,tok_out,lsem.at[2]); outt.start()
    pltpu.make_async_copy(infob.at[j,1-c],infob.at[j,1-c],isr.at[1]).wait()
    pltpu.make_async_copy(infob.at[1-j,1-c],infob.at[1-j,1-c],isr.at[2]).wait()
    info_out[...]=infob[...]
    net.drain()
    for x in keep: x.wait()
    outw.wait(); outt.wait()

def gather(tok,info,pack,Z,W):
    _,block,E=tok.shape; R,C=pack.shape
    rows=256; NCH=block//rows; L=4*block
    V=pl.BlockSpec(memory_space=pltpu.VMEM); A=pl.BlockSpec(memory_space=pl.ANY)
    S=jax.ShapeDtypeStruct; M=pltpu.VMEM; D=pltpu.SemaphoreType.DMA
    waves=((0,6*W),(6*W,C))
    return pl.pallas_call(functools.partial(gather_kernel,Z,block,E,W,waves,rows),
        out_shape=[S((2,2,block,E),bf),S((2,2,1,block),jnp.int32),S((Z,2,2,2,R,C),bf),S((E,3*W),bf),S((3*W,L),bf)],
        in_specs=[A,V,V],out_specs=[A,V,A,V,A],
        scratch_shapes=[M((2,2,block,E),bf),M((2,2,1,block),jnp.int32),M((Z,2,2,2,R,C),bf),M((3*W,E),bf),M((3*W,L),bf),
            D((3,)),D((4*NCH,)),D((2,)),D((2,)),D((2,2,Z)),D((2,Z)),D((2,Z)),D((2,Z)),D((2,2,Z)),D((2,2,Z)),D((3,NCH)),D((3,NCH)),D((3,)),D((3,))],
        compiler_params=pltpu.CompilerParams(collective_id=0,has_side_effects=True,vmem_limit_bytes=48<<20))(tok,info,pack)
def reduce_kernel(Z,block,E,W,F,rows,cuts,tg_hbm,r1_hbm,gq_ref,go_ref,gu_ref,gd_ref,gg_ref,tok_out,grad_out,
                  own,r1,tgr,tgs,ob,s0,r0,g0,s1,r1b,su,ru,sd,rd,sx,rx,
                  lsem,ts,tr,xs,xr,cs,cr,ys,yr,us,ur,ds,dr,fs,fr):
    net=Net(Z); z,y,j,c=net.z,net.y,net.j,net.c
    NCH=block//rows; C=g0.shape[-1]; Q=3*W; NW=len(cuts)
    sib=net.at(c=1-c); xd=net.at(j=1-j); yd=net.at(y=1-y)
    loads=[pltpu.make_async_copy(tg_hbm.at[:,c],own,lsem.at[0]),pltpu.make_async_copy(r1_hbm,r1,lsem.at[1])]
    for x in loads: x.start()
    net.greet()
    def chunk(k): return pl.ds(k*rows,rows)
    def landed(ref,sem): pltpu.make_async_copy(ref,ref,sem).wait()
    for t in range(2):
        jj=1-j if t==0 else j
        for k in range(NCH): net.send(tg_hbm.at[jj,1-c,chunk(k)],tgr.at[jj,chunk(k)],ts.at[t,k],tr.at[t,k],sib)
    ggt=jnp.concatenate([gg_ref[...],jnp.zeros((120,E),f32)],0).T
    def split(x,n): return x.reshape(Z,2,2,2,16,n)
    s0[:,:,:,:,0:Q]=split(gq_ref[...],Q)[:,:,:,0]
    @pl.when(c==0)
    def _(): s0[:,:,:,:,0:Q]=split(gq_ref[...],Q)[:,:,:,1]
    at=Q
    places=[]
    for x in (go_ref[...],gu_ref[...],gd_ref[...],ggt):
        n=x.shape[1]
        v=split(x,n)
        @pl.when(c==0)
        def _(): s0[:,:,:,:,at:at+n]=v[:,:,:,1].astype(bf)
        @pl.when(c==1)
        def _(): s0[:,:,:,:,at:at+n]=v[:,:,:,0].astype(bf)
        places.append((v,at,n))
        at+=n
    net.send(s0.at[:,:,:,:,0:Q],r0.at[:,:,:,:,0:Q],cs.at[0],cr.at[0],sib)
    net.send(s0.at[:,:,:,:,Q:at],r0.at[:,:,:,:,Q:at],cs.at[1],cr.at[1],sib)
    for x in loads: x.wait()
    def total(jj,k): return (own[jj,chunk(k),:].astype(f32)+tgr[jj,chunk(k),:].astype(f32)+r1[jj,chunk(k),:].astype(f32)).astype(bf)
    for k in range(NCH):
        landed(tgr.at[1-j,chunk(k)],tr.at[0,k])
        tgs[chunk(k),:]=total(1-j,k)
        net.send(tgs.at[chunk(k)],ob.at[j,chunk(k)],xs.at[k],xr.at[k],xd)
    landed(r0.at[:,:,:,:,0:Q],cr.at[0])
    landed(r0.at[:,:,:,:,Q:at],cr.at[1])
    mine=split(gq_ref[...],Q)
    for cc in range(2):
        @pl.when(c==cc)
        def _():
            for t in range(3):
                for other in range(2):
                    src=mine[:,:,:,cc,:,t*W:(t+1)*W] if other==cc else r0[:,:,:,:,t*W:(t+1)*W]
                    g0[:,:,:,:,(2*t+other)*W:(2*t+other+1)*W]=src.astype(f32)
            for v,a,n in places:
                g0[:,:,:,:,Q+a:Q+a+n]=v[:,:,:,cc]+r0[:,:,:,:,a:a+n].astype(f32)
    cut=[pl.ds(a,b-a) for a,b in cuts]
    for w in range(NW):
        s1[:,:,:,cut[w]]=g0[:,1-y,:,:,cut[w]].astype(bf)
        net.send(s1.at[:,:,:,cut[w]],r1b.at[:,:,:,cut[w]],ys.at[w],yr.at[w],yd)
    for k in range(NCH):
        landed(tgr.at[j,chunk(k)],tr.at[1,k])
        ob[j,chunk(k),:]=total(j,k)
    def lines(w):
        landed(r1b.at[:,:,:,cut[w]],yr.at[w])
        def base(o): return g0[o,y,:,:,cut[w]]+r1b[o,:,:,cut[w]].astype(f32)
        for t in range(Z-1):
            up=Z-1-t
            @pl.when(z<up)
            def _():
                @pl.when(z>0)
                def _():
                    landed(ru.at[up,:,:,cut[w]],ur.at[w,up])
                    su[up,:,:,cut[w]]=(base(up)+ru[up,:,:,cut[w]].astype(f32)).astype(bf)
                @pl.when(z==0)
                def _(): su[up,:,:,cut[w]]=base(up).astype(bf)
            net.send(su.at[up,:,:,cut[w]],ru.at[up,:,:,cut[w]],us.at[w,up],ur.at[w,up],net.at(z=z+1),z<up)
            down=t
            @pl.when(z>down)
            def _():
                @pl.when(z<Z-1)
                def _():
                    landed(rd.at[down,:,:,cut[w]],dr.at[w,down])
                    sd[down,:,:,cut[w]]=(base(down)+rd[down,:,:,cut[w]].astype(f32)).astype(bf)
                @pl.when(z==Z-1)
                def _(): sd[down,:,:,cut[w]]=base(down).astype(bf)
            net.send(sd.at[down,:,:,cut[w]],rd.at[down,:,:,cut[w]],ds.at[w,down],dr.at[w,down],net.at(z=z-1),z>down)
        for o in range(Z):
            @pl.when(z==o)
            def _():
                sum_=base(o)
                if o>0:
                    landed(ru.at[o,:,:,cut[w]],ur.at[w,o])
                    sum_=sum_+ru[o,:,:,cut[w]].astype(f32)
                if o<Z-1:
                    landed(rd.at[o,:,:,cut[w]],dr.at[w,o])
                    sum_=sum_+rd[o,:,:,cut[w]].astype(f32)
                g0[o,y,:,:,cut[w]]=sum_
        sx[:,cut[w]]=g0[z,y,1-j,:,cut[w]].astype(bf)
        net.send(sx.at[:,cut[w]],rx.at[:,cut[w]],fs.at[w],fr.at[w],xd)
    for w in range(NW): lines(w)
    for w in range(NW):
        landed(rx.at[:,cut[w]],fr.at[w])
        grad_out[:,cut[w]]=g0[z,y,j,:,cut[w]]+rx[:,cut[w]].astype(f32)
    for k in range(NCH): landed(ob.at[1-j,chunk(k)],xr.at[k])
    last=pltpu.make_async_copy(ob,tok_out,lsem.at[2])
    last.start()
    net.drain()
    last.wait()

def reduce(tg,r1,gq,go,gu,gd,gg,Z,W):
    _,_,block,E=tg.shape; F=gu.shape[1]; C=6*W+2*F+E+128; Q=3*W
    rows=256; NCH=block//rows
    steps=C//128; n=4
    edges=[128*((steps*t+n-1)//n) for t in range(n+1)]
    cuts=tuple(zip(edges[:-1],edges[1:])); NW=len(cuts)
    V=pl.BlockSpec(memory_space=pltpu.VMEM); A=pl.BlockSpec(memory_space=pl.ANY)
    S=jax.ShapeDtypeStruct; M=pltpu.VMEM; D=pltpu.SemaphoreType.DMA
    return pl.pallas_call(functools.partial(reduce_kernel,Z,block,E,W,F,rows,cuts),
        out_shape=[S((2,block,E),bf),S((16,C),f32)],
        in_specs=[A,A,V,V,V,V,V],out_specs=[A,V],
        scratch_shapes=[M((2,block,E),bf),M((2,block,E),r1.dtype),M((2,block,E),bf),M((block,E),bf),M((2,block,E),bf),
            M((Z,2,2,16,C-Q),bf),M((Z,2,2,16,C-Q),bf),M((Z,2,2,16,C),f32),M((Z,2,16,C),bf),M((Z,2,16,C),bf),
            M((Z,2,16,C),bf),M((Z,2,16,C),bf),M((Z,2,16,C),bf),M((Z,2,16,C),bf),M((16,C),bf),M((16,C),bf),
            D((3,)),D((2,NCH)),D((2,NCH)),D((NCH,)),D((NCH,)),D((2,)),D((2,)),D((NW,)),D((NW,)),D((NW,Z)),D((NW,Z)),D((NW,Z)),D((NW,Z)),D((NW,)),D((NW,))],
        compiler_params=pltpu.CompilerParams(collective_id=1,has_side_effects=True,vmem_limit_bytes=56<<20))(tg,r1,gq,go,gu,gd,gg)
def shards(tokens,cotangent,segments,padding,known,w_qkv,w_out,w_up,w_down,norm_gains,norm_shifts):
    micro,rows,block,D=tokens.shape
    J=lax.axis_size("blk")//2; dps=lax.axis_size("dp")
    units=micro*rows
    assert units==J
    H=HEADS//2; W=H*HEAD; L=2*J*block; F=w_up.shape[1]
    quick=J==2 and dps%2==0 and w_qkv.shape[0]%16==0 and block%256==0
    me=lax.axis_index("blk"); chip=me//2; core=me%2
    def to_chip(s): return [(2*a+c,2*((a+s)%J)+c) for a in range(J) for c in range(2)]
    swap=[(b,b^1) for b in range(2*J)]
    def other(x): return lax.ppermute(x,"blk",swap)
    def scatter_units(x):
        got=[]
        for s in range(J):
            mine=lax.dynamic_index_in_dim(x,(chip+s)%J,0,keepdims=False)
            got.append(mine if s==0 else lax.ppermute(mine,"blk",to_chip(s)))
        return jnp.stack([lax.select_n((chip-j)%J,*got) if J==2 else lax.dynamic_index_in_dim(jnp.stack(got),(chip-j)%J,0,keepdims=False) for j in range(J)])
    def both(mine,his):
        return jnp.stack([jnp.where(core==0,mine,his),jnp.where(core==0,his,mine)],1)
    def part(x,axis,index): return lax.dynamic_index_in_dim(x,index,axis,keepdims=False)
    flat=lambda x:x.reshape((units,)+x.shape[2:])
    info=flat(segments*4+padding*2+known)
    if quick:
        gs=jnp.pad(jnp.concatenate([norm_gains,norm_shifts],0),((0,12),(0,112)))
        pack=jnp.concatenate([w_qkv,w_out,w_up,w_down,gs],1)
        all_tok,all_info,wall,w_mine,qkvt=gather(flat(tokens),info[:,None,:],pack,dps//2,W)
        own_tok=part(all_tok,1,core); all_tok=all_tok.reshape(L,D); all_info=all_info.reshape(L)
        N=lax.axis_size("blk")*dps
        wall=wall.reshape(N,16,-1)
        gs=wall[:,:4,6*W+2*D+F:6*W+2*D+F+16].transpose(1,0,2).reshape(4,D).astype(f32)
        wall=wall.reshape(D,-1)
        full_out,full_up,full_down=wall[:,6*W:6*W+D],wall[:,6*W+D:6*W+D+F],wall[:,6*W+D+F:6*W+2*D+F]
    else:
        own_info=scatter_units(info); all_info=both(own_info,other(own_info)).reshape(L)
        own_tok=scatter_units(flat(tokens)); all_tok=both(own_tok,other(own_tok)).reshape(L,D)
        full_qkv,full_out,full_up,full_down=[lax.all_gather(w,("dp","blk"),axis=0,tiled=True) for w in (w_qkv,w_out,w_up,w_down)]
        gs=lax.all_gather(jnp.concatenate([norm_gains,norm_shifts],0),("dp","blk"),axis=1,tiled=True).astype(f32)
        w_mine=part(full_qkv.reshape(D,3,2,W),2,core).reshape(D,3*W)
        scale=jnp.where(jnp.arange(3*W)<W,math.log2(math.e)/8,1.0).astype(f32)
        qkvt=(jnp.einsum("ld,de->el",all_tok,w_mine,preferred_element_type=f32)*scale[:,None]).astype(bf)
    gs=jnp.concatenate([gs,jnp.zeros_like(gs)],0)
    qkvt,cotangent=lax.optimization_barrier((qkvt,cotangent))
    own_cot=scatter_units(flat(cotangent)).reshape(L//2,D)
    cnt,codet,meta=flags(all_info//4,(all_info//2)%2,all_info%2)
    p,att,ot,inv,kaug,vaug=attend(cnt,qkvt,codet,meta,H)
    att=att.reshape(H//2,J,2,block,128)
    mine=part(att,2,core).reshape(H//2,J*block,128); his=other(part(att,2,1-core)).reshape(H//2,J*block,128)
    a0=jnp.where(core==0,mine,his); a1=jnp.where(core==0,his,mine)
    out,r1,da,go,gu,gd,gg=middle(a0,a1,own_tok.reshape(L//2,D),own_cot,full_out,full_up,full_down,gs)
    da=da.reshape(2,H//2,J,block,128)
    dmine=part(da,0,core); dhis=other(part(da,0,1-core))
    datt=jnp.stack([jnp.where(core==0,dmine,dhis),jnp.where(core==0,dhis,dmine)],2).reshape(H//2,L,128)
    tg,gq=back(cnt,datt,p,ot,inv,kaug,vaug,qkvt,meta,all_tok,w_mine,H)
    tg=tg.reshape(J,2,block,D)
    layer_out=scatter_units(out.reshape(J,block,D)).reshape(tokens.shape)
    a,b,e=6*W,6*W+D,6*W+D+F
    if quick:
        token_grad,grads=reduce(tg,r1.reshape(J,block,D),gq.T.astype(bf),go,gu,gd,gg,dps//2,W)
        token_grad=token_grad.reshape(tokens.shape)
        gg=grads[:,e+D:e+D+4].T
        return (layer_out,token_grad,grads[:,:a],grads[:,a:b],grads[:,b:e],grads[:,e:e+D],gg[:2],gg[2:])
    own_tg=(part(tg,1,core).astype(f32)+other(part(tg,1,1-core)).astype(f32)+r1.reshape(J,block,D)).astype(bf)
    token_grad=scatter_units(own_tg).reshape(tokens.shape)
    gq=gq.T.reshape(D,3,1,W)
    gq=jnp.where(core==0,jnp.concatenate([gq,jnp.zeros_like(gq)],2),jnp.concatenate([jnp.zeros_like(gq),gq],2)).reshape(D,6*W)
    grads=lax.psum_scatter(jnp.concatenate([gq,go,gu,gd],1),("dp","blk"),scatter_dimension=0,tiled=True)
    gg=lax.psum_scatter(gg[:4],("dp","blk"),scatter_dimension=1,tiled=True)
    return (layer_out,token_grad,grads[:,:a],grads[:,a:b],grads[:,b:e],grads[:,e:],gg[:2],gg[2:])

def solution(mesh):
    in_specs = (
        P(None, "dp", "blk", None),
        P(None, "dp", "blk", None),
        P(None, "dp", "blk"),
        P(None, "dp", "blk"),
        P(None, "dp", "blk"),
        P(("dp", "blk"), None),
        P(("dp", "blk"), None),
        P(("dp", "blk"), None),
        P(("dp", "blk"), None),
        P(None, ("dp", "blk")),
        P(None, ("dp", "blk")),
    )
    out_specs = (
        P(None, "dp", "blk", None),
        P(None, "dp", "blk", None),
        P(("dp", "blk"), None),
        P(("dp", "blk"), None),
        P(("dp", "blk"), None),
        P(("dp", "blk"), None),
        P(None, ("dp", "blk")),
        P(None, ("dp", "blk")),
    )
    return jax.shard_map(shards, mesh=mesh, in_specs=in_specs, out_specs=out_specs, check_vma=False)
```

time: 1940 us -> 412 us (0.21)
  waiting for transfers between devices: 857 us -> 0.01 us
  matrix products: 530 us -> 0 us
  Pallas kernels: 0 us -> 358 us
  blocking collectives: 213 us -> 0 us
  local copies, waits for them, and re-layouts: 187 us -> 29.5 us
  other arithmetic: 110 us -> 12.6 us
    dot_general x108 -> x0, matrix products: 530 us -> none  [the longest x12 99.6 us: attend_one(): jnp.einsum('rqhk,rkhd->rqhd', exps.astype(jnp.bfloat16), value_h, preferr...]
    reduce_scatter x7 -> x0, waiting for transfers between devices: 435 us -> none  [the longest x1 134 us: shards(): lax.psum_scatter(acc_up, ('dp', 'blk'), scatter_dimension=0, tiled=True)]
    unnamed x18 -> x0, waiting for transfers between devices: 362 us -> none
    pallas_call x0 -> x5, Pallas kernels: none -> 358 us  [the longest x1 152 us: attend(): pl.pallas_call(functools.partial(attend_kernel, L, H), out_shape=[S((cap,...]
    all_gather x8 -> x0, blocking collectives: 213 us -> none  [the longest x1 42.1 us: shards(): lax.all_gather(w_down, ('dp', 'blk'), axis=0, tiled=True)]
    while x192 -> x0, local copies, waits for them, and re-layouts: 64.1 us -> none
    all_gather x5 -> x0, waiting for transfers between devices: 60.6 us -> none  [the longest x1 60.6 us: shards(): lax.all_gather(w_qkv, ('dp', 'blk'), axis=0, tiled=True)]
    dynamic_slice x72 -> x1, local copies, waits for them, and re-layouts: 53.2 us -> 1.25 us  [part(): return lax.dynamic_index_in_dim(x, index, axis, keepdims=False)]
  transfers between devices with their start and end apart: 15 -> 4, of which waited for: 9 -> 0; matrix products, arithmetic and copies ran while one was open for 20% -> 6% of each run, Pallas kernels for 0% -> 73%
where the time goes in v1:
time: 412 us; the launch traced here: 409 us
  Pallas kernels  358 us (87%)
  local copies, waits for them, and re-layouts  29.5 us (7%)
  other arithmetic  12.6 us (3%)
  starting transfers between devices  7.97 us (2%)
    pallas_call x1, Pallas kernels, attend(): pl.pallas_call(functools.partial(attend_kernel, L, H), out_shape=[S((cap,...  152 us
    pallas_call x1, Pallas kernels, reduce(): pl.pallas_call(functools.partial(reduce_kernel, Z, block, E, W, F, rows,...  86.3 us
    pallas_call x1, Pallas kernels, back(): pl.pallas_call(functools.partial(back_kernel, L, H), out_shape=[S((L, E),...  60.6 us
    pallas_call x1, Pallas kernels, gather(): pl.pallas_call(functools.partial(gather_kernel, Z, block, E, W, waves, ro...  36.5 us
    pallas_call x1, Pallas kernels, middle(): pl.pallas_call(middle_kernel, grid=(N // T,), in_specs=[pairs(P2), pairs(...  22.6 us
    unnamed x25, local copies, waits for them, and re-layouts  8.57 us
  transfers between devices with their start and end apart: 4, of which 0 were waited for; matrix products, arithmetic and copies ran while one was open for 6% of the time, Pallas kernels for 73%

profile of v1, /device:TPU:0, one launch (start us, length us, event | category | flops | bytes accessed | tf_op | source)
XLA Modules:
  0.0 409.5 jit_solution(10665279780311894378)
XLA Ops:
  0.7 0.8 constant_dynamic-update-slice_fusion.4
  1.5 0.7 constant_dynamic-update-slice_fusion.3
  2.2 0.7 constant_dynamic-update-slice_fusion.2
  2.9 0.7 constant_dynamic-update-slice_fusion.1
  3.6 0.7 add_add_fusion.2.info_ref
  4.4 0.7 constant_dynamic-update-slice_fusion.pack_ref
  5.1 1.4 copy-done.1
  6.5 36.5 %shard_map.170 = (bf16[2,2,768,512]{3,2,1,0:T(8,128)(2,1)S(1)}, s32[2,2,1,768]{3,2,1,0:T(1,128)S(1)}, bf16[4,2,2,2,16,3200]{5,4,3,2,1,0:T(8,128)(2,1)}, bf16[512,768]{1,0:T(8,128)(2,1)S(1)}, bf16[768,3072]{1,0:T(8,128)(2,1)}) custom-call(bf16[2,768,512]{2,1,0:T(8,128)(2,1)S(1)} %bitcast.98, s32[2,1,768]{2,1,0:T(1,128)S(1)} %add_add_fusion.2.info_ref, ...), custom_call_target="tpu_custom_call" | custom-call | tf_op jit(solution)/shard_map/pallas_call | solution.py:489
  42.9 0.9 copy-done.2
  43.9 2.6 dynamic-slice_bitcast_fusion.2
  46.5 0.7 collective-permute-start.1
  47.3 0.3 reduce-window.9
  47.7 0.1 slice_reduce_fusion
  48.2 0.1 copy.52
  48.8 0.6 slice.90
  49.4 0.1 copy.54
  49.5 0.1 add_select_fusion
  49.7 0.1 and_select_fusion
  50.0 0.2 convert_reduce_fusion
  50.4 0.7 add_add_fusion.meta_ref
  51.1 0.7 select_convert_fusion.codet_ref
  52.1 1.2 concatenate.23.cnt_ref
  53.3 152.4 %shard_map.171 = (bf16[42,4,512,512]{3,2,1,0:T(8,128)(2,1)}, bf16[2,3072,128]{2,1,0:T(8,128)(2,1)}, f32[6,256,512]{2,1,0:T(8,128)}, f32[4,8,3072]{2,1,0:T(8,128)...) custom-call(s32[49]{0:T(128)} %concatenate.23.cnt_ref, bf16[768,3072]{1,0:T(8,128)(2,1)} %get-tuple-element.34.qkvt_ref, ...), custom_call_target="tpu_custom_call" | custom-call | tf_op jit(solution)/shard_map/pallas_call | solution.py:160
  205.7 2.7 dynamic-slice_bitcast_fusion.3
  208.4 0.9 slice.100
  209.4 1.3 constant_dynamic-slice_fusion
  210.7 0.6 pad_convert_fusion.gs_ref
  211.3 2.7 fusion.30
  214.0 1.2 fusion.4
  215.3 1.3 pad_maximum_fusion
  216.6 2.4 bitcast_select_fusion
  219.0 22.6 %shard_map.172 = (bf16[1536,512]{1,0:T(8,128)(2,1)}, f32[1536,512]{1,0:T(8,128)}, bf16[4,1536,128]{2,1,0:T(8,128)(2,1)}, f32[512,512]{1,0:T(8,128)}, f32[512,512...) custom-call(bf16[2,1536,128]{2,1,0:T(8,128)(2,1)} %get-tuple-element.97.a0_ref, ...), custom_call_target="tpu_custom_call" | custom-call | tf_op jit(solution)/shard_map/pallas_call | solution.py:346
  241.6 1.3 dynamic-slice_bitcast_fusion
  243.0 0.6 collective-permute-start.3
  243.6 6.7 %collective-permute-start.2 = (bf16[768,512]{1,0:T(8,128)(2,1)S(1)}, bf16[768,512]{1,0:T(8,128)(2,1)S(1)}, u32[]{:S(2)}, u32[]{:S(2)}) collective-permute-start(bf16[768,512]{1,0:T(8,128)(2,1)S(1)} %dynamic-slice_bitcast_fusion.1), channel_id=1, source_target_pairs={{0,2},{1,3},{2,0},{3,1},{4,6},{5,7},{6,4},{7,5},{8,10},{9,11},{10,... | collective-permute-start | bytes 2359304 | tf_op jit(solution)/shard_map/ppermute | solution.py:630
  250.4 1.3 pad_maximum_fusion.1
  251.7 60.6 %shard_map.173 = (bf16[3072,512]{1,0:T(8,128)(2,1)}, f32[768,512]{1,0:T(8,128)}) custom-call(s32[49]{0:T(128)} %concatenate.23.cnt_ref, bf16[2,3072,128]{2,1,0:T(8,128)(2,1)} %bitcast.105, bf16[42,4,512,512]{3,2,1,0:T(8,128)(2,1)} %get-tuple-element.41.p_hbm, f32[6,256,512]{2,1,0:T(8,128)} %get-tuple-element.42.ot_ref, ...), custom_call_target="tpu_custom_call" | custom-call | tf_op jit(solution)/shard_map/pallas_call | solution.py:285
  312.4 2.6 copy.63
  314.9 86.3 %shard_map.174 = (bf16[2,768,512]{2,1,0:T(8,128)(2,1)}, f32[16,3200]{1,0:T(8,128)}) custom-call(bf16[2,2,768,512]{3,2,1,0:T(8,128)(2,1)} %bitcast.108, f32[2,768,512]{2,1,0:T(8,128)} %bitcast.107, bf16[512,768]{1,0:T(8,128)(2,1)} %bitcast.106, f32[512,512]{1,0:T(8,128)} %get-tuple-element.50.go_ref, f32[512,512]{1,0:T(8,128)} %get-tuple-element.51.gu_ref, ...), custom_call_target="tpu_custom_call" | custom-call | tf_op jit(solution)/shard_map/pallas_call | solution.py:607
  401.2 1.5 slice.81
  402.7 0.7 slice_bitcast_fusion
  403.5 0.6 copy.66
  404.2 0.6 copy.65
  404.8 1.4 fusion.31
  406.2 0.1 fusion.2
  406.3 1.3 maximum_bitcast_fusion
  407.6 0.7 copy-done.4
  408.3 1.1 copy.77
  (59 shorter events, 1.9 us)
Async XLA Ops:
  5.1 1.4 copy-start.1
  42.9 1.0 copy-start.2
  43.9 165.5 %copy-start = (bf16[2,2,768,512]{3,2,1,0:T(8,128)(2,1)}, bf16[2,2,768,512]{3,2,1,0:T(8,128)(2,1)S(1)}, u32[]{:S(2)}) copy-start(bf16[2,2,768,512]{3,2,1,0:T(8,128)(2,1)S(1)} %get-tuple-element.36) | copy-start | bytes 9437188
  46.5 167.5 %collective-permute-start.1 = (bf16[768,512]{1,0:T(8,128)(2,1)}, bf16[768,512]{1,0:T(8,128)(2,1)}, u32[]{:S(2)}, u32[]{:S(2)}) collective-permute-start(bf16[768,512]{1,0:T(8,128)(2,1)} %dynamic-slice_bitcast_fusion.2), channel_id=1, source_target_pairs={{0,2},{1,3},{2,0},{3,1},{4,6},{5,7},{6,4},{7,5},{8,10},{9,11},{10,... | collective-permute-start | bytes 2359304 | tf_op jit(solution)/shard_map/ppermute | solution.py:630
  208.4 8.1 %collective-permute-start = (bf16[2,2,768,128]{3,2,1,0:T(8,128)(2,1)}, bf16[2,2,768,128]{3,2,1,0:T(8,128)(2,1)}, u32[]{:S(2)}, u32[]{:S(2)}) collective-permute-start(bf16[2,2,768,128]{3,2,1,0:T(8,128)(2,1)} %get-tuple-element.98), channel_id=1, source_target_pairs={{0,1},{1,0},{2,3},{3,2},{4,5},{5,4},{6,7},{7,6},{8,9},{9,8},{10,11... | collective-permute-start | bytes 2359304 | tf_op jit(solution)/shard_map/ppermute | solution.py:625
  211.3 2.7 copy-start.5
  215.2 1.3 copy-start.3
  241.6 1.9 copy-start.6
  241.6 8.7 %copy-start.7 = (bf16[4,1536,128]{2,1,0:T(8,128)(2,1)S(1)}, bf16[4,1536,128]{2,1,0:T(8,128)(2,1)}, u32[]{:S(2)}) copy-start(bf16[4,1536,128]{2,1,0:T(8,128)(2,1)} %get-tuple-element.40) | copy-start | bytes 4718596
  243.0 7.4 %collective-permute-start.3 = (bf16[2,2,768,128]{3,2,1,0:T(8,128)(2,1)S(1)}, bf16[2,2,768,128]{3,2,1,0:T(8,128)(2,1)S(1)}, u32[]{:S(2)}, u32[]{:S(2)}) collective-permute-start(bf16[2,2,768,128]{3,2,1,0:T(8,128)(2,1)S(1)} %dynamic-slice_bitcast_fusion), channel_id=1, source_target_pairs={{0,1},{1,0},{2,3},{3,2},{4,5},{5,4},{6,7},{7,6},{8,9},{9,8},{10,11... | collective-permute-start | bytes 2359304 | tf_op jit(solution)/shard_map/ppermute | solution.py:625
  243.6 162.6 %collective-permute-start.2 = (bf16[768,512]{1,0:T(8,128)(2,1)S(1)}, bf16[768,512]{1,0:T(8,128)(2,1)S(1)}, u32[]{:S(2)}, u32[]{:S(2)}) collective-permute-start(bf16[768,512]{1,0:T(8,128)(2,1)S(1)} %dynamic-slice_bitcast_fusion.1), channel_id=1, source_target_pairs={{0,2},{1,3},{2,0},{3,1},{4,6},{5,7},{6,4},{7,5},{8,10},{9,11},{10,... | collective-permute-start | bytes 2359304 | tf_op jit(solution)/shard_map/ppermute | solution.py:630
  406.3 2.0 copy-start.4

commit v2 on v1

v2 whole, which is shorter than its diff:
```python
import functools, math
import jax, jax.numpy as jnp
from jax import lax
from jax.experimental import pallas as pl
from jax.experimental.pallas import tpu as pltpu
from jax.sharding import PartitionSpec as P

HEADS = 8
bf=jnp.bfloat16; f32=jnp.float32
HEAD=64
QB=512
KB=512
SRC=512
SAFE=60.0
CODE=16
VMEM=(64<<20)-(128<<10)
SLOTS=3
def dot(a,b,ca,cb): return lax.dot_general(a,b,(((ca,),(cb,)),((),())),preferred_element_type=f32)
def al(x,n): return pl.multiple_of(x,n)
def iota(shape,axis): return lax.broadcasted_iota(jnp.int32,shape,axis)

def begin(base_ref,b):
    return base_ref[b,0]

def window(win_ref,i):
    start=win_ref[i,0]//128*128
    groups=(win_ref[8+i,0]-start+127)//128
    full=(groups-1)//(KB//128)
    return start,full,groups-full*(KB//128),groups

def by_piece(first,full,rest,g,fn):
    def body(j,g):
        fn(al(first+j*KB,128),KB,g)
        return g+1
    g=lax.fori_loop(0,full,body,g)
    for r in range(1,KB//128+1):
        @pl.when(rest==r)
        def _(): fn(al(first+full*KB,128),r*128,g)
    return g+1

def attend_kernel(L,H,base_ref,win_ref,qkvt_ref,codet_ref,meta_ref,p_hbm,att_hbm,ot_hbm,inv_ref,kaug_hbm,vaug_hbm,
                  kaug_ref,vaug_ref,kvt,vct,acc,pbuf,obuf,abuf,top_ref,psem,osem,asem,ksem):
    W=H*HEAD; nq=L//QB
    total=begin(base_ref,L//256)
    for h in range(H):
        kvt[h*128:h*128+HEAD,:]=qkvt_ref[W+h*HEAD:W+(h+1)*HEAD,:]
        kvt[h*128+HEAD:h*128+HEAD+CODE,:]=codet_ref[...]
        kvt[h*128+HEAD+CODE:(h+1)*128,:]=jnp.zeros((HEAD-CODE,L),bf)
    lane=iota((256,128),1)
    down=iota((256,SRC),0)
    def dest(d,c):
        def src(s,a):
            ssl=pl.ds(al(s*SRC,SRC),SRC)
            oh=(meta_ref[0:1,ssl]==(down+d*256)).astype(f32).astype(bf)
            ka=a[0]+dot(oh,kvt[:,ssl],1,1)
            va=a[1]+dot(oh,qkvt_ref[2*W:3*W,ssl],1,1)
            return ka,va
        lo=hi=0
        for t in range(L//SRC):
            lo=lo+(begin(base_ref,(t+1)*(SRC//256))<=d*256).astype(jnp.int32)
            hi=hi+(begin(base_ref,t*(SRC//256))<d*256+256).astype(jnp.int32)
        ka,va=lax.fori_loop(lo,hi,src,(jnp.zeros((256,H*128),f32),jnp.zeros((256,W),f32)))
        dsl=pl.ds(al(d*256,256),256)
        vat=va.T
        for h in range(H):
            k1=ka[:,h*128:(h+1)*128]
            kaug_ref[h,dsl,:]=jnp.where(lane==HEAD+10,-2560.0,k1).astype(bf)
            pair=va[:,(h//2)*128:(h//2+1)*128]
            if h%2: pair=jnp.concatenate([pair[:,HEAD:],pair[:,:HEAD]],1)
            vaug_ref[h,dsl,:]=jnp.where(lane<HEAD,pair,jnp.where(lane<HEAD+3,-1.0,0.0)).astype(bf)
            vct[h,:HEAD,dsl]=vat[h*HEAD:(h+1)*HEAD,:].astype(bf)
            vct[h,HEAD:HEAD+16,dsl]=jnp.ones((16,256),bf)
        return c
    lax.fori_loop(0,(total+255)//256,dest,0)
    keep=[pltpu.make_async_copy(kaug_ref,kaug_hbm,ksem.at[0]),pltpu.make_async_copy(vaug_ref,vaug_hbm,ksem.at[1])]
    for x in keep: x.start()
    bound=jnp.float32(0)
    for h in range(H):
        q=qkvt_ref[h*HEAD:(h+1)*HEAD,:].astype(f32); k=qkvt_ref[W+h*HEAD:W+(h+1)*HEAD,:].astype(f32)
        bound=jnp.maximum(bound,jnp.max(jnp.sum(q*q,0,keepdims=True))*jnp.max(jnp.sum(k*k,0,keepdims=True)))
    safe=bound<SAFE*SAFE

    def pcopy(g):
        slot=lax.rem(g,SLOTS)
        return pltpu.make_async_copy(pbuf.at[slot],p_hbm.at[g],psem.at[slot])
    def ocopy(i):
        slot=lax.rem(i,2)
        return pltpu.make_async_copy(obuf.at[slot],ot_hbm.at[i],osem.at[slot])
    def acopy(i):
        slot=lax.rem(i,2)
        return pltpu.make_async_copy(abuf.at[slot],att_hbm.at[:,pl.ds(al(i*QB,QB),QB),:],asem.at[slot])
    def block(i,g):
        slot=lax.rem(i,2)
        qsl=pl.ds(al(i*QB,QB),QB)
        first,full,rest,groups=window(win_ref,i)
        qa=[jnp.concatenate([qkvt_ref[h*HEAD:(h+1)*HEAD,qsl],codet_ref[:,qsl],jnp.zeros((HEAD-CODE,QB),bf)],0) for h in range(H)]
        own=meta_ref[1:2,qsl]>0
        sself=[]
        for h in range(H):
            x=qkvt_ref[h*HEAD:(h+1)*HEAD,qsl].astype(f32)*qkvt_ref[W+h*HEAD:W+(h+1)*HEAD,qsl].astype(f32)
            sself.append(jnp.where(own,jnp.sum(x,0,keepdims=True),-1e30))
        acc[...]=jnp.zeros_like(acc)
        top_ref[...]=jnp.zeros_like(top_ref)
        row=iota((128,QB),0)
        def strict(h,osl):
            k=kaug_ref[h,osl,:]
            x=qa[h].astype(f32)
            plain=dot(k,jnp.where(row<HEAD,x,0.0).astype(bf),1,0)
            return jnp.where(dot(k,jnp.where(row<HEAD,0.0,x).astype(bf),1,0)>-1.0,plain,-1e30)
        @pl.when(jnp.logical_not(safe))
        def _():
            for h in range(H):
                def more(j,m): return jnp.maximum(m,jnp.max(strict(h,pl.ds(al(first+j*128,128),128)),0,keepdims=True))
                top_ref[h:h+1,:]=lax.fori_loop(0,groups,more,sself[h])
        def piece(off,size,g):
            ps=lax.rem(g,SLOTS)
            osl=pl.ds(off,size)
            @pl.when(g>=SLOTS)
            def _(): pcopy(g-SLOTS).wait()
            @pl.when(safe)
            def _():
                keepp=[]
                for h in range(H):
                    p=jnp.exp2(dot(kaug_ref[h,osl,:],qa[h],1,0)).astype(bf)
                    pbuf[ps,h,:size,:]=p
                    keepp.append(p)
                for h in range(H): acc[h]+=dot(vct[h,:,osl],keepp[h],1,0)
            @pl.when(jnp.logical_not(safe))
            def _():
                for h in range(H):
                    def put(j,c):
                        jsl=pl.ds(al(off+j*128,128),128)
                        p=jnp.exp2(strict(h,jsl)-top_ref[h:h+1,:]).astype(bf)
                        pbuf[ps,h,pl.ds(al(j*128,128),128),:]=p
                        acc[h]+=dot(vct[h,:,jsl],p,1,0)
                        return c
                    lax.fori_loop(0,size//128,put,0)
            pcopy(g).start()
        g=by_piece(first,full,rest,g,piece)
        @pl.when(i>=2)
        def _(): ocopy(i-2).wait(); acopy(i-2).wait()
        for h in range(H):
            ps=jnp.exp2(sself[h]-top_ref[h:h+1,:])
            inv=1.0/(acc[h,HEAD:HEAD+1,:]+ps)
            obuf[slot,h*HEAD:(h+1)*HEAD,:]=(acc[h,:HEAD,:]+ps*qkvt_ref[2*W+h*HEAD:2*W+(h+1)*HEAD,qsl].astype(f32))*inv
            inv_ref[h,0:1,qsl]=inv
            inv_ref[h,1:2,qsl]=ps
        for hp in range(H//2): abuf[slot,hp]=obuf[slot,hp*128:(hp+1)*128,:].T.astype(bf)
        ocopy(i).start(); acopy(i).start()
        return g
    g=lax.fori_loop(0,nq,block,0)
    for s in range(SLOTS):
        last=g-1-s
        @pl.when(last>=0)
        def _(): pcopy(last).wait()
    for i in range(max(nq-2,0),nq): ocopy(i).wait(); acopy(i).wait()
    for x in keep: x.wait()

def attend(base,win,qkvt,codet,meta,H):
    L=qkvt.shape[1]; W=H*HEAD; nq=L//QB; cap=nq*(L//KB+1)
    V=pl.BlockSpec(memory_space=pltpu.VMEM); A=pl.BlockSpec(memory_space=pl.ANY)
    S=jax.ShapeDtypeStruct; M=pltpu.VMEM; D=pltpu.SemaphoreType.DMA
    return pl.pallas_call(functools.partial(attend_kernel,L,H),
        out_shape=[S((cap,H,KB,QB),bf),S((H//2,L,128),bf),S((nq,W,QB),f32),S((H,8,L),f32),S((H,L,128),bf),S((H,L,128),bf)],
        in_specs=[pl.BlockSpec(memory_space=pltpu.SMEM)]*2+[V,V,V],
        out_specs=[A,A,A,V,A,A],
        scratch_shapes=[M((H,L,128),bf),M((H,L,128),bf),M((H*128,L),bf),M((H,HEAD+16,L),bf),M((H,HEAD+16,QB),f32),M((SLOTS,H,KB,QB),bf),
            M((2,W,QB),f32),M((2,H//2,QB,128),bf),M((8,QB),f32),D((SLOTS,)),D((2,)),D((2,)),D((2,))],
        compiler_params=pltpu.CompilerParams(vmem_limit_bytes=VMEM))(base,win,qkvt,codet,meta)

def flags(row):
    L=row.shape[1]; nb=L//256; nq=L//QB
    seg=row//4
    pad=row//2-2*seg
    known=row-2*(row//2)
    use=(pad==0)&(known==1)
    usef=use.astype(f32)
    x=jnp.concatenate([usef[:,b*256:(b+1)*256] for b in range(nb)]+[jnp.zeros((16-nb,256),f32)],0)
    incl=dot(x.astype(bf),(iota((256,256),0)<=iota((256,256),1)).astype(f32).astype(bf),1,0)
    tot=jnp.broadcast_to(incl[:,255:256],(16,256)).astype(bf)
    base=dot((iota((16,16),0)>iota((16,16),1)).astype(f32).astype(bf),tot,1,0)
    rank=(incl+base).astype(jnp.int32)-1
    rank=jnp.concatenate([rank[b:b+1] for b in range(nb)],1)
    rank=jnp.where(use,rank,-1)
    own=((pad==0)&(known!=1)).astype(jnp.int32)
    bits=iota((CODE,L),0)
    bit=lax.shift_right_logical(jnp.broadcast_to(seg,(CODE,L)),jnp.minimum(bits,9))&1
    codet=jnp.where(bits<10,jnp.where(bit==1,16.0,-16.0),jnp.where(bits==10,1.0,0.0)).astype(bf)
    meta=jnp.concatenate([rank,own,jnp.zeros((6,L),jnp.int32)],0)
    def edge(at): return jnp.concatenate([seg[:,i*QB+at:i*QB+at+1] for i in range(nq)]+[jnp.zeros((8-nq,1),jnp.int32)],0)
    low=jnp.sum(jnp.where(seg<edge(0),usef,0.0),1,keepdims=True)
    high=jnp.sum(jnp.where(seg<=edge(QB-1),usef,0.0),1,keepdims=True)
    win=jnp.broadcast_to(jnp.concatenate([low,high],0),(16,128)).astype(jnp.int32)
    return base[:,:128].astype(jnp.int32),win,codet,meta
LN2=math.log(2.0)
def back_kernel(L,H,base_ref,win_ref,datt_ref,p_hbm,ot_ref,inv_ref,kaug_ref,vaug_ref,qkvt_ref,meta_ref,tok_hbm,w_ref,
                tg_hbm,grad_ref,kct,dkv,dkvt,dq_ref,pbuf,qacc,tok_ref,tbuf,psem,tsem,ksem):
    W=H*HEAD; nq=L//QB; nd=L//256
    total=begin(base_ref,nd); groups=(total+127)//128
    pieces=lax.fori_loop(0,nq,lambda i,s:s+window(win_ref,i)[1]+1,0)
    def pcopy(g):
        slot=lax.rem(g,SLOTS)
        return pltpu.make_async_copy(p_hbm.at[g],pbuf.at[slot],psem.at[slot])
    for s in range(SLOTS-1):
        @pl.when(s<pieces)
        def _(): pcopy(s).start()
    tcopy=pltpu.make_async_copy(tok_hbm,tok_ref,ksem.at[0])
    tcopy.start()
    def prep(j,c):
        jsl=pl.ds(al(j*128,128),128)
        for h in range(H): kct[h,:,jsl]=kaug_ref[h,jsl,:].T[:HEAD]
        dkv[jsl,:]=jnp.zeros((128,2*W),f32)
        return c
    lax.fori_loop(0,groups,prep,0)
    def block(i,g):
        qsl=pl.ds(al(i*QB,QB),QB)
        first,full,rest,_=window(win_ref,i)
        dt=jnp.concatenate([datt_ref[hp,qsl,:].astype(f32).T for hp in range(H//2)],0)
        prod=dt*ot_ref[i]
        daug=[];dz=[];qz=[];deltas=[];d1s=[]
        zero=jnp.zeros((HEAD,QB),bf)
        row=iota((16,QB),0)
        for h in range(H):
            hsl=slice(h*HEAD,(h+1)*HEAD)
            inv=inv_ref[h,0:1,qsl]
            delta=jnp.sum(prod[hsl],0,keepdims=True)*inv
            d1=dt[hsl]*inv
            low=d1.astype(bf)
            a=delta.astype(bf).astype(f32); b=(delta-a).astype(bf).astype(f32)
            extra=jnp.where(row==0,a,jnp.where(row==1,b,jnp.where(row==2,delta-a-b,0.0))).astype(bf)
            daug.append(jnp.concatenate([low,extra,jnp.zeros((HEAD-16,QB),bf)],0))
            q=qkvt_ref[hsl,qsl]
            dz.append(jnp.concatenate([zero,low] if h%2 else [low,zero],0))
            qz.append(jnp.concatenate([zero,q] if h%2 else [q,zero],0))
            deltas.append(delta); d1s.append(d1)
        qacc[...]=jnp.zeros_like(qacc)
        def piece(off,size,g):
            slot=lax.rem(g,SLOTS)
            osl=pl.ds(off,size)
            @pl.when(g+SLOTS-1<pieces)
            def _(): pcopy(g+SLOTS-1).start()
            pcopy(g).wait()
            dss=[]
            for h in range(H):
                dss.append((pbuf[slot,h,:size,:].astype(f32)*dot(vaug_ref[h,osl,:],daug[h],1,0)).astype(bf))
            for h in range(H): qacc[h*HEAD:(h+1)*HEAD,:]+=dot(kct[h,:,osl],dss[h],1,0)
            for h in range(0,H,2):
                dkv[osl,h*HEAD:(h+2)*HEAD]+=dot(dss[h],qz[h],1,1)+dot(dss[h+1],qz[h+1],1,1)
                dkv[osl,W+h*HEAD:W+(h+2)*HEAD]+=dot(pbuf[slot,h,:size,:],dz[h],1,1)+dot(pbuf[slot,h+1,:size,:],dz[h+1],1,1)
        g=by_piece(first,full,rest,g,piece)
        for h in range(H):
            hsl=slice(h*HEAD,(h+1)*HEAD); ksl=slice(W+h*HEAD,W+(h+1)*HEAD); vsl=slice(2*W+h*HEAD,2*W+(h+1)*HEAD)
            ps=inv_ref[h,1:2,qsl]
            ds=ps*(jnp.sum(qkvt_ref[vsl,qsl].astype(f32)*d1s[h],0,keepdims=True)-deltas[h])
            dq_ref[hsl,qsl]=((qacc[hsl,:]+ds*qkvt_ref[ksl,qsl].astype(f32))*0.125).astype(bf)
            dq_ref[ksl,qsl]=(ds*qkvt_ref[hsl,qsl].astype(f32)*LN2).astype(bf)
            dq_ref[vsl,qsl]=(ps*d1s[h]).astype(bf)
        return g
    lax.fori_loop(0,nq,block,0)
    lanes=iota((128,2*W),1)
    def turn(j,c):
        jsl=pl.ds(al(j*128,128),128)
        x=jnp.where(j<groups,dkv[jsl,:],0.0)
        dkvt[:,jsl]=jnp.where(lanes<W,x*LN2,x).astype(bf).T
        return c
    lax.fori_loop(0,groups+3,turn,0)
    deep=iota((384,256),0)
    def tgcopy(s):
        slot=lax.rem(s,2)
        return pltpu.make_async_copy(tbuf.at[slot],tg_hbm.at[pl.ds(al(s*256,256),256),:],tsem.at[slot])
    def place(s,c):
        ssl=pl.ds(al(s*256,256),256)
        r0=begin(base_ref,s)//128*128
        oh=(meta_ref[0:1,ssl]==deep+r0).astype(f32).astype(bf)
        g=dot(dkvt[:,pl.ds(al(r0,128),384)],oh,1,0)+dq_ref[W:3*W,ssl].astype(f32)
        dq_ref[W:3*W,ssl]=g.astype(bf)
        @pl.when(s>=2)
        def _(): tgcopy(s-2).wait()
        tbuf[lax.rem(s,2)]=dot(dq_ref[:,ssl],w_ref[...],0,1).astype(bf)
        tgcopy(s).start()
        return c
    lax.fori_loop(0,nd,place,0)
    tcopy.wait()
    grad_ref[...]=dot(dq_ref[...],tok_ref[...],1,0).T.astype(bf)
    for s in range(nd-2,nd): tgcopy(s).wait()

def back(base,win,datt,p,ot,inv,kaug,vaug,qkvt,meta,tok,w,H):
    L=qkvt.shape[1]; W=H*HEAD; E=tok.shape[1]
    V=pl.BlockSpec(memory_space=pltpu.VMEM); A=pl.BlockSpec(memory_space=pl.ANY)
    S=jax.ShapeDtypeStruct; M=pltpu.VMEM; D=pltpu.SemaphoreType.DMA
    return pl.pallas_call(functools.partial(back_kernel,L,H),
        out_shape=[S((L,E),bf),S((E,3*W),bf)],
        in_specs=[pl.BlockSpec(memory_space=pltpu.SMEM)]*2+[V,A]+[V]*6+[A,V],
        out_specs=[A,V],
        scratch_shapes=[M((H,HEAD,L),bf),M((L,2*W),f32),M((2*W,L+384),bf),M((3*W,L),bf),M((SLOTS,H,KB,QB),bf),M((W,QB),f32),
            M((L,E),bf),M((2,256,E),bf),D((SLOTS,)),D((2,)),D((1,))],
        compiler_params=pltpu.CompilerParams(vmem_limit_bytes=VMEM))(base,win,datt,p,ot,inv,kaug,vaug,qkvt,meta,tok,w)
EPSILON=1e-05
def erf(x):
    x=jnp.clip(x,-3.832506856900711,3.832506856900711)
    x2=x*x
    top=0.00022905065861350646
    for c in (0.0034082910107109506,0.050955695062380861,0.18520832239976145,1.128379143519084): top=top*x2+c
    low=-1.1791602954361697e-7
    for c in (0.000023547966471313185,0.0010179625278914885,0.014070470171167667,0.11098505178285362,0.49746925110067538,1.0): low=low*x2+c
    return x*top/low
def norm(x):
    center=x-jnp.mean(x,-1,keepdims=True)
    inverse=lax.rsqrt(jnp.mean(center*center,-1,keepdims=True)+EPSILON)
    return center*inverse,inverse
def norm_back(e,n,inverse):
    return inverse*(e-jnp.mean(e,-1,keepdims=True)-n*jnp.mean(e*n,-1,keepdims=True))
def middle_kernel(a0_ref,a1_ref,tok_ref,cot_ref,wo_ref,wu_ref,wd_ref,gs_ref,out_ref,r1_ref,da_ref,go_ref,gu_ref,gd_ref,gg_ref):
    @pl.when(pl.program_id(0)==0)
    def _():
        for r in (go_ref,gu_ref,gd_ref,gg_ref): r[...]=jnp.zeros_like(r)
    P2=a0_ref.shape[0]
    att=jnp.concatenate([a0_ref[p] for p in range(P2)]+[a1_ref[p] for p in range(P2)],1)
    g0,g1,b0,b1=[gs_ref[r:r+1,:] for r in range(4)]
    n1,inv1=norm(tok_ref[...].astype(f32)+dot(att,wo_ref[...],1,0))
    first=(n1*g0+b0).astype(bf)
    hidden=dot(first,wu_ref[...],1,0)
    cdf=0.5*(1.0+erf(hidden*math.sqrt(0.5)))
    act=(hidden*cdf).astype(bf)
    slope=cdf+hidden*jnp.exp(-0.5*hidden*hidden)*(1.0/math.sqrt(2.0*math.pi))
    n2,inv2=norm(first.astype(f32)+dot(act,wd_ref[...],1,0))
    out_ref[...]=(n2*g1+b1).astype(bf)
    cot=cot_ref[...].astype(f32)
    r2=norm_back(cot*g1,n2,inv2)
    feed=r2.astype(bf)
    gd_ref[...]+=dot(act,feed,0,0)
    dh=(dot(feed,wd_ref[...],1,1)*slope).astype(bf)
    gu_ref[...]+=dot(first,dh,0,0)
    df=r2+dot(dh,wu_ref[...],1,1)
    r1=norm_back(df*g0,n1,inv1)
    r1_ref[...]=r1
    db=r1.astype(bf)
    go_ref[...]+=dot(att,db,0,0)
    da=dot(db,wo_ref[...],1,1).astype(bf)
    for p in range(2*P2): da_ref[p]=da[:,p*128:(p+1)*128]
    gg_ref[0:1,:]+=jnp.sum(df*n1,0,keepdims=True)
    gg_ref[1:2,:]+=jnp.sum(cot*n2,0,keepdims=True)
    gg_ref[2:3,:]+=jnp.sum(df,0,keepdims=True)
    gg_ref[3:4,:]+=jnp.sum(cot,0,keepdims=True)

def middle(a0,a1,tok,cot,wo,wu,wd,gs):
    P2,N,_=a0.shape; D=tok.shape[1]; F=wu.shape[1]
    T=max(t for t in (256,192,128,64,32,16) if N%t==0)
    tile=pl.BlockSpec((T,D),lambda i:(i,0))
    def pairs(k): return pl.BlockSpec((k,T,128),lambda i:(0,i,0))
    def whole(s): return pl.BlockSpec(s,lambda i:(0,)*len(s))
    return pl.pallas_call(middle_kernel,grid=(N//T,),
        in_specs=[pairs(P2),pairs(P2),tile,tile,whole((D,D)),whole((D,F)),whole((F,D)),whole((8,D))],
        out_specs=[tile,tile,pairs(2*P2),whole((D,D)),whole((D,F)),whole((F,D)),whole((8,D))],
        out_shape=[jax.ShapeDtypeStruct((N,D),bf),jax.ShapeDtypeStruct((N,D),f32),jax.ShapeDtypeStruct((2*P2,N,128),bf),
            jax.ShapeDtypeStruct((D,D),f32),jax.ShapeDtypeStruct((D,F),f32),jax.ShapeDtypeStruct((F,D),f32),jax.ShapeDtypeStruct((8,D),f32)],
        compiler_params=pltpu.CompilerParams(vmem_limit_bytes=60<<20))(a0,a1,tok,cot,wo,wu,wd,gs)
MESH=pl.DeviceIdType.MESH
class Net:
    def __init__(self,Z):
        dp=lax.axis_index("dp"); blk=lax.axis_index("blk")
        self.Z=Z; self.z=dp//2; self.y=dp%2; self.j=blk//2; self.c=blk%2
        self.sent=[]
    def at(self,z=None,y=None,j=None,c=None):
        z=self.z if z is None else z; y=self.y if y is None else y; j=self.j if j is None else j; c=self.c if c is None else c
        return (z*2+y,j*2+c)
    def greet(self):
        barrier=pltpu.get_barrier_semaphore()
        def signal(d): pl.semaphore_signal(barrier,inc=1,device_id=d,device_id_type=MESH)
        signal(self.at(j=1-self.j)); signal(self.at(y=1-self.y)); signal(self.at(c=1-self.c))
        for k in range(1,self.Z): signal(self.at(z=lax.rem(self.z+k,self.Z)))
        pl.semaphore_wait(barrier,2+self.Z)
    def copy(self,src,dst,ssem,rsem,device):
        return pltpu.make_async_remote_copy(src_ref=src,dst_ref=dst,send_sem=ssem,recv_sem=rsem,device_id=device,device_id_type=MESH)
    def send(self,src,dst,ssem,rsem,device,when=None):
        c=self.copy(src,dst,ssem,rsem,device)
        if when is None: c.start()
        else: pl.when(when)(c.start)
        self.sent.append((c,when))
    def drain(self):
        for c,when in self.sent:
            if when is None: c.wait_send()
            else: pl.when(when)(c.wait_send)

def gather_kernel(Z,block,E,W,rows,tok_hbm,seg_ref,pad_ref,known_ref,wq_ref,wo_ref,wu_ref,wd_ref,gain_ref,shift_ref,
                  tok_out,bund_out,wmine_out,qkvt_out,base_out,win_out,code_out,meta_out,
                  tokb,info_ref,infob,pack_ref,wall,bund,wt,qkvt,lsem,qsem,xs,xr,zs,zr,ys,yr,cs,cr,ts,tr,iss,isr):
    net=Net(Z); z,y,j,c=net.z,net.y,net.j,net.c
    NCH=block//rows; D=E
    sib=net.at(c=1-c); xd=net.at(j=1-j); yd=net.at(y=1-y)
    mine=pltpu.make_async_copy(tok_hbm.at[j],tokb.at[j,c],lsem.at[0]); mine.start()
    at=0
    for ref in (wq_ref,wo_ref,wu_ref,wd_ref):
        n=ref.shape[1]
        pack_ref[:,at:at+n]=ref[...]
        at+=n
    R=gain_ref.shape[1]
    place=(iota((R,128),1)==iota((R,128),0)+R*lax.rem(lax.axis_index("dp")*4+lax.axis_index("blk"),128//R)).astype(f32).astype(bf)
    pack_ref[:,at:]=jnp.concatenate([dot(gain_ref[...],place,1,0),dot(shift_ref[...],place,1,0),jnp.zeros((12,128),f32)],0).astype(bf)
    split=6*W
    wall[z,y,j,c]=pack_ref[:,:split]
    bund[y,j]=pack_ref[:,split:]
    info_ref[...]=seg_ref[...]*4+pad_ref[...]*2+known_ref[...]
    infob[j,c]=info_ref[j]
    net.greet()
    net.send(pack_ref.at[:,:split],wall.at[z,y,j,c],xs.at[0],xr.at[0],xd)
    net.send(pack_ref.at[:,split:],bund.at[y,j],xs.at[1],xr.at[1],xd)
    net.send(info_ref.at[1-j],infob.at[j,c],iss.at[0],isr.at[0],xd)
    net.send(info_ref.at[j],infob.at[j,c],iss.at[1],isr.at[1],sib)
    def chunk(k): return pl.ds(k*rows,rows)
    for k in range(NCH):
        net.send(tok_hbm.at[1-j,chunk(k)],tokb.at[j,c,chunk(k)],ts.at[0,k],tr.at[0,k],xd)
        net.send(tok_hbm.at[j,chunk(k)],tokb.at[j,c,chunk(k)],ts.at[1,k],tr.at[1,k],sib)
    def piece(o,y_): return wall.at[o,y_,:,c]
    def landed(ref,sem): pltpu.make_async_copy(ref,ref,sem).wait()
    def pass_on(o):
        net.send(piece(o,y),piece(o,y),ys.at[o],yr.at[o],yd)
        net.send(piece(o,y),piece(o,y),cs.at[0,o],cr.at[0,o],sib)
    landed(wall.at[z,y,1-j,c],xr.at[0])
    for k in range(1,Z):
        net.send(piece(z,y),piece(z,y),zs.at[k],zr.at[k],net.at(z=lax.rem(z+k,Z)))
    pass_on(z)
    landed(bund.at[y,1-j],xr.at[1])
    net.send(bund.at[y],bund.at[y],ys.at[Z],yr.at[Z],yd)
    for k in range(1,Z):
        o=lax.rem(z+Z-k,Z)
        landed(piece(o,y),zr.at[k])
        pass_on(o)
    for k in range(Z):
        o=lax.rem(z+Z-k,Z)
        landed(piece(o,1-y),yr.at[o])
        net.send(piece(o,1-y),piece(o,1-y),cs.at[1,o],cr.at[1,o],sib)
    for o in range(Z):
        for q in range(2): landed(wall.at[o,y if q==0 else 1-y,:,1-c],cr.at[q,o])
    landed(bund.at[1-y],yr.at[Z])
    outb=pltpu.make_async_copy(bund,bund_out,lsem.at[1]); outb.start()
    def project(jj,cc,k):
        g=(jj*2+cc)*NCH+k
        r=dot(wt[...],tokb[jj,cc,chunk(k),:],1,1)
        col=pl.ds(al(g*rows,rows),rows)
        qkvt[:,col]=jnp.concatenate([r[:W]*(math.log2(math.e)/8),r[W:]],0).astype(bf)
        out=pltpu.make_async_copy(qkvt.at[:,col],qkvt_out.at[:,col],qsem.at[g])
        out.start()
        return out
    keep=[]
    parts=[]
    for t in range(3):
        cols=pl.ds(al(t*2*W+c*W,W),W)
        part=wall[:,:,:,:,:,cols].reshape(D,W)
        wt[t*W:(t+1)*W,:]=part.T
        parts.append(part)
    wmine_out[...]=jnp.concatenate(parts,1)
    mine.wait()
    for k in range(NCH): keep.append(project(j,c,k))
    for k in range(NCH):
        ref=tokb.at[j,1-c,chunk(k)]
        pltpu.make_async_copy(ref,ref,tr.at[1,k]).wait()
        keep.append(project(j,1-c,k))
    for k in range(NCH):
        ref=tokb.at[1-j,c,chunk(k)]
        pltpu.make_async_copy(ref,ref,tr.at[0,k]).wait()
        net.send(ref,ref,ts.at[2,k],tr.at[2,k],sib)
        keep.append(project(1-j,c,k))
        if k==0:
            pltpu.make_async_copy(infob.at[1-j,c],infob.at[1-j,c],isr.at[0]).wait()
            net.send(infob.at[1-j,c],infob.at[1-j,c],iss.at[2],isr.at[2],sib)
    pltpu.make_async_copy(infob.at[j,1-c],infob.at[j,1-c],isr.at[1]).wait()
    pltpu.make_async_copy(infob.at[1-j,1-c],infob.at[1-j,1-c],isr.at[2]).wait()
    base_out[...],win_out[...],code_out[...],meta_out[...]=flags(jnp.concatenate([infob[0,0],infob[0,1],infob[1,0],infob[1,1]],1))
    for k in range(NCH):
        ref=tokb.at[1-j,1-c,chunk(k)]
        pltpu.make_async_copy(ref,ref,tr.at[2,k]).wait()
        keep.append(project(1-j,1-c,k))
    outt=pltpu.make_async_copy(tokb,tok_out,lsem.at[2]); outt.start()
    net.drain()
    for x in keep: x.wait()
    outb.wait(); outt.wait()

def gather(tok,seg,pad,known,wq,wo,wu,wd,gain,shift,Z,W):
    _,block,E=tok.shape; R=wq.shape[0]; C=6*W+wo.shape[1]+wu.shape[1]+wd.shape[1]+128
    rows=256; NCH=block//rows; L=4*block
    V=pl.BlockSpec(memory_space=pltpu.VMEM); A=pl.BlockSpec(memory_space=pl.ANY)
    S=jax.ShapeDtypeStruct; M=pltpu.VMEM; D=pltpu.SemaphoreType.DMA; I=jnp.int32
    return pl.pallas_call(functools.partial(gather_kernel,Z,block,E,W,rows),
        out_shape=[S((2,2,block,E),bf),S((2,2,R,C-6*W),bf),S((E,3*W),bf),S((3*W,L),bf),S((16,128),I),S((16,128),I),S((CODE,L),bf),S((8,L),I)],
        in_specs=[A]+[V]*9,out_specs=[A,A,V,A,V,V,V,V],
        scratch_shapes=[M((2,2,block,E),bf),M((2,1,block),I),M((2,2,1,block),I),M((R,C),bf),M((Z,2,2,2,R,6*W),bf),M((2,2,R,C-6*W),bf),M((3*W,E),bf),M((3*W,L),bf),
            D((3,)),D((4*NCH,)),D((2,)),D((2,)),D((Z,)),D((Z,)),D((Z+1,)),D((Z+1,)),D((2,Z)),D((2,Z)),D((3,NCH)),D((3,NCH)),D((3,)),D((3,))],
        compiler_params=pltpu.CompilerParams(collective_id=0,has_side_effects=True,vmem_limit_bytes=VMEM))(tok,seg,pad,known,wq,wo,wu,wd,gain,shift)
def middle_net_kernel(Z,block,E,F,W,T,att_hbm,tok_hbm,cot_hbm,cotx_hbm,*rest):
    bunds=rest[:Z]; lay_out,r1_out,datt_out=rest[Z:Z+3]; parts=rest[Z+3]
    (go_ref,gu_ref,gd_ref,gg_ref,gt_ref,aown,aget,tok,cot,wall,lay,r1,da,lsem,wsem,osem,asend,aget_sem,dsend,dget,xsend,xget,bsend,bget)=rest[Z+4:]
    net=Net(Z); z,y,j,c=net.z,net.y,net.j,net.c
    NCH=block//T; n=2*NCH; P2=att_hbm.shape[0]; D=E
    sib=net.at(c=1-c); xd=net.at(j=1-j)
    def place(t):
        jj=jnp.where(t<NCH,1-j,j)
        return jj,pl.ds(al(lax.rem(t,NCH)*T,T),T)
    def load(t):
        jj,rows=place(t)
        return [pltpu.make_async_copy(att_hbm.at[:,jj,c,rows],aown.at[t],lsem.at[0,t]),pltpu.make_async_copy(tok_hbm.at[jj,c,rows],tok.at[t],lsem.at[1,t])]
    def load_cot(t,near):
        rows=place(t)[1]
        return pltpu.make_async_copy((cot_hbm.at[j,rows] if near else cotx_hbm.at[rows]),cot.at[t],lsem.at[2,t])
    cols=[(0,E),(E,F),(E+F,E),(2*E+F,128)]
    loadw=[pltpu.make_async_copy(bunds[k],wall.at[lax.rem(z+Z-k,Z),:,:,c],wsem.at[k]) for k in range(Z)]
    for x in loadw: x.start()
    def start(t,near):
        for x in load(t): x.start()
        load_cot(t,near).start()
    for t in range(n): start(t,t>=NCH)
    barrier=pltpu.get_barrier_semaphore()
    for d in (sib,xd): pl.semaphore_signal(barrier,inc=1,device_id=d,device_id_type=MESH)
    pl.semaphore_wait(barrier,2)
    def ship(t):
        jj,rows=place(t)
        return net.copy(att_hbm.at[:,jj,1-c,rows],aget.at[t],asend.at[t],aget_sem.at[t],sib)
    ship(0).start()
    weights=[net.copy(bunds[k],wall.at[lax.rem(z+Z-k,Z),:,:,c],bsend.at[k],bget.at[k],sib) for k in range(Z)]
    for x in weights: x.start()
    for t in range(1,n): ship(t).start()
    for x in loadw: x.wait()
    for k in range(Z):
        ref=wall.at[lax.rem(z+Z-k,Z),:,:,1-c]
        pltpu.make_async_copy(ref,ref,bget.at[k]).wait()
    def whole(a,b): return wall[:,:,:,:,:,a:a+b].reshape(E,b)
    gs=wall[:,:,:,:,:,cols[3][0]:].reshape(E//16,16,128).astype(f32)
    gsr=jnp.concatenate([jnp.sum(gs[q*8:(q+1)*8],0) for q in range(E//128)],1)
    g0,g1,b0,b1=[gsr[r:r+1,:] for r in range(4)]
    for r in (go_ref,gu_ref,gd_ref,gg_ref): r[...]=jnp.zeros_like(r)
    def out_near(t):
        jj,rows=place(t)
        return pltpu.make_async_copy(lay.at[t],lay_out.at[j,rows],osem.at[0,t])
    def out_far(t):
        jj,rows=place(t)
        return net.copy(lay.at[t],lay_out.at[j,rows],xsend.at[t],xget.at[t],xd)
    def out_r1(t):
        jj,rows=place(t)
        return pltpu.make_async_copy(r1.at[t],r1_out.at[jj,rows],osem.at[1,t])
    def out_da(t):
        jj,rows=place(t)
        return pltpu.make_async_copy(da.at[0,t],datt_out.at[:,jj,c,rows],osem.at[2,t])
    def ship_da(t):
        jj,rows=place(t)
        return net.copy(da.at[1,t],datt_out.at[:,jj,c,rows],dsend.at[t],dget.at[t],sib)
    def tile(t,carry):
        for x in load(t): x.wait()
        pltpu.make_async_copy(cotx_hbm.at[place(t)[1]],cot.at[t],lsem.at[2,t]).wait()
        ship(t).wait_recv()
        mine=[aown[t,p] for p in range(P2)]; his=[aget[t,p] for p in range(P2)]
        att=jnp.where(c==0,jnp.concatenate(mine+his,1),jnp.concatenate(his+mine,1))
        wo=whole(*cols[0]); wu=whole(*cols[1]); wd=whole(*cols[2])
        n1,inv1=norm(tok[t].astype(f32)+dot(att,wo,1,0))
        first=(n1*g0+b0).astype(bf)
        hidden=dot(first,wu,1,0)
        cdf=0.5*(1.0+erf(hidden*math.sqrt(0.5)))
        act=(hidden*cdf).astype(bf)
        slope=cdf+hidden*jnp.exp(-0.5*hidden*hidden)*(1.0/math.sqrt(2.0*math.pi))
        n2,inv2=norm(first.astype(f32)+dot(act,wd,1,0))
        lay[t]=(n2*g1+b1).astype(bf)
        @pl.when(t<NCH)
        def _(): out_far(t).start()
        @pl.when(t>=NCH)
        def _(): out_near(t).start()
        ct=cot[t].astype(f32)
        r2=norm_back(ct*g1,n2,inv2)
        feed=r2.astype(bf)
        gd_ref[...]+=dot(act,feed,0,0)
        dh=(dot(feed,wd,1,1)*slope).astype(bf)
        gu_ref[...]+=dot(first,dh,0,0)
        df=r2+dot(dh,wu,1,1)
        dr=norm_back(df*g0,n1,inv1)
        r1[t]=dr.astype(r1.dtype)
        out_r1(t).start()
        db=dr.astype(bf)
        go_ref[...]+=dot(att,db,0,0)
        d=dot(db,wo,1,1).astype(bf)
        for p in range(P2):
            lo=d[:,p*128:(p+1)*128]; hi=d[:,W+p*128:W+(p+1)*128]
            da[0,t,p]=jnp.where(c==0,lo,hi)
            da[1,t,p]=jnp.where(c==0,hi,lo)
        out_da(t).start(); ship_da(t).start()
        gg_ref[0:1,:]+=jnp.sum(df*n1,0,keepdims=True)
        gg_ref[1:2,:]+=jnp.sum(ct*n2,0,keepdims=True)
        gg_ref[2:3,:]+=jnp.sum(df,0,keepdims=True)
        gg_ref[3:4,:]+=jnp.sum(ct,0,keepdims=True)
        return carry
    lax.fori_loop(0,n,tile,0)
    ggt=jnp.concatenate([gg_ref[...],jnp.zeros((120,E),f32)],0).T
    gt_ref[...]=ggt
    R=E//(2*Z)
    at=0
    for ref in (go_ref,gu_ref,gd_ref,gt_ref):
        parts[:,:,at:at+ref.shape[1]]=ref[...].astype(bf).reshape(2*Z,R,ref.shape[1])
        at+=ref.shape[1]
    for x in weights: x.wait_send()
    for t in range(n):
        ship(t).wait_send(); out_r1(t).wait(); out_da(t).wait(); ship_da(t).wait()
        if t<NCH: out_far(t).wait()
        else: out_near(t).wait()

def middle_net(att,tok,cot,cotx,bunds,Z,W,F):
    P2,_,_,block,_=att.shape; E=tok.shape[-1]; C=bunds[0].shape[-1]
    T=256; NCH=block//T; n=2*NCH
    V=pl.BlockSpec(memory_space=pltpu.VMEM); A=pl.BlockSpec(memory_space=pl.ANY)
    S=jax.ShapeDtypeStruct; M=pltpu.VMEM; D=pltpu.SemaphoreType.DMA
    return pl.pallas_call(functools.partial(middle_net_kernel,Z,block,E,F,W,T),
        out_shape=[S((2,block,E),bf),S((2,block,E),f32),S((P2,2,2,block,128),bf)]+[S((2*Z,E//(2*Z),C),bf)],
        in_specs=[A]*(4+Z),out_specs=[A,A,A,V],
        scratch_shapes=[M((E,E),f32),M((E,F),f32),M((F,E),f32),M((8,E),f32),M((E,128),f32),
            M((n,P2,T,128),bf),M((n,P2,T,128),bf),M((n,T,E),bf),M((n,T,E),bf),M((Z,2,2,2,16,C),bf),M((n,T,E),bf),M((n,T,E),f32),M((2,n,P2,T,128),bf),
            D((3,n)),D((Z,)),D((3,n)),D((n,)),D((n,)),D((n,)),D((n,)),D((n,)),D((n,)),D((Z,)),D((Z,))],
        compiler_params=pltpu.CompilerParams(collective_id=2,has_side_effects=True,vmem_limit_bytes=VMEM))(att,tok,cot,cotx,*bunds)
def reduce_kernel(Z,block,E,W,C1,rows,cuts,tg_hbm,r1_hbm,gq_ref,parts,tok_out,grad_out,*rest):
    (own,r1,tgr,tgs,ob,s0,r0,g0,s1,r1b,su,ru,fin,sx,rx,se,re,sxe,rxe,
     lsem,ts,tr,xs,xr,cs,cr,ys,yr,us,ur,fs,fr)=rest
    net=Net(Z); z,y,j,c=net.z,net.y,net.j,net.c
    NCH=block//rows; Q=3*W; NW=len(cuts)
    sib=net.at(c=1-c); xd=net.at(j=1-j); yd=net.at(y=1-y)
    loads=[pltpu.make_async_copy(tg_hbm.at[:,c],own,lsem.at[0]),pltpu.make_async_copy(r1_hbm,r1,lsem.at[1])]
    for x in loads: x.start()
    net.greet()
    def chunk(k): return pl.ds(k*rows,rows)
    def landed(ref,sem): pltpu.make_async_copy(ref,ref,sem).wait()
    def to_sibling(t):
        jj=1-j if t==0 else j
        for k in range(NCH): net.send(tg_hbm.at[jj,1-c,chunk(k)],tgr.at[jj,chunk(k)],ts.at[t,k],tr.at[t,k],sib)
    to_sibling(0)
    def split(x,n): return x.reshape(Z,2,2,2,16,n)
    s0[...]=split(gq_ref[...],Q)[:,:,:,0]
    @pl.when(c==0)
    def _(): s0[...]=split(gq_ref[...],Q)[:,:,:,1]
    net.send(s0,r0,cs.at[0],cr.at[0],sib)
    early=parts[0].astype(f32)
    for k in range(1,2*Z): early=early+parts[k].astype(f32)
    early=early.reshape(2,2,16,C1)
    early0=jnp.where(c==0,early[:,0],early[:,1])
    se[...]=jnp.where(c==0,early[:,1],early[:,0]).astype(bf)
    net.send(se,re,cs.at[1],cr.at[1],sib)
    to_sibling(1)
    for x in loads: x.wait()
    def total(jj,k): return (own[jj,chunk(k),:].astype(f32)+tgr[jj,chunk(k),:].astype(f32)+r1[jj,chunk(k),:].astype(f32)).astype(bf)
    for k in range(NCH):
        landed(tgr.at[1-j,chunk(k)],tr.at[0,k])
        tgs[chunk(k),:]=total(1-j,k)
        net.send(tgs.at[chunk(k)],ob.at[j,chunk(k)],xs.at[k],xr.at[k],xd)
    landed(r0,cr.at[0])
    mine=split(gq_ref[...],Q)
    for cc in range(2):
        @pl.when(c==cc)
        def _():
            for t in range(3):
                for other in range(2):
                    src=mine[:,:,:,cc,:,t*W:(t+1)*W] if other==cc else r0[:,:,:,:,t*W:(t+1)*W]
                    g0[:,:,:,:,(2*t+other)*W:(2*t+other+1)*W]=src
    cut=[pl.ds(a,b-a) for a,b in cuts]
    for w in range(NW):
        s1[:,:,:,cut[w]]=g0[:,1-y,:,:,cut[w]]
        net.send(s1.at[:,:,:,cut[w]],r1b.at[:,:,:,cut[w]],ys.at[w],yr.at[w],yd)
    landed(re,cr.at[1])
    early0=early0+re[...].astype(f32)
    early1=jnp.where(j==0,early0[0],early0[1])
    sxe[...]=jnp.where(j==0,early0[1],early0[0]).astype(bf)
    net.send(sxe,rxe,fs.at[NW],fr.at[NW],xd)
    for k in range(NCH):
        landed(tgr.at[j,chunk(k)],tr.at[1,k])
        ob[j,chunk(k),:]=total(j,k)
    def to_z(w):
        landed(r1b.at[:,:,:,cut[w]],yr.at[w])
        for k in range(1,Z):
            o=lax.rem(z+k,Z)
            su[k,:,:,cut[w]]=(g0[o,y,:,:,cut[w]].astype(f32)+r1b[o,:,:,cut[w]].astype(f32)).astype(bf)
            net.send(su.at[k,:,:,cut[w]],ru.at[k,:,:,cut[w]],us.at[w,k],ur.at[w,k],net.at(z=o))
    def to_x(w):
        sum_=g0[z,y,:,:,cut[w]].astype(f32)+r1b[z,:,:,cut[w]].astype(f32)
        for k in range(1,Z):
            landed(ru.at[k,:,:,cut[w]],ur.at[w,k])
            sum_=sum_+ru[k,:,:,cut[w]].astype(f32)
        fin[:,:,cut[w]]=sum_
        sx[:,cut[w]]=fin[1-j,:,cut[w]].astype(bf)
        net.send(sx.at[:,cut[w]],rx.at[:,cut[w]],fs.at[w],fr.at[w],xd)
    for w in range(NW):
        to_z(w)
        if w>0: to_x(w-1)
    to_x(NW-1)
    landed(rxe,fr.at[NW])
    grad_out[:,2*Q:]=early1+rxe[...].astype(f32)
    for w in range(NW):
        landed(rx.at[:,cut[w]],fr.at[w])
        grad_out[:,cut[w]]=fin[j,:,cut[w]]+rx[:,cut[w]].astype(f32)
    for k in range(NCH): landed(ob.at[1-j,chunk(k)],xr.at[k])
    last=pltpu.make_async_copy(ob,tok_out,lsem.at[2])
    last.start()
    net.drain()
    last.wait()

def reduce(tg,r1,gq,parts,Z,W):
    _,_,block,E=tg.shape; Q=3*W; C1=parts.shape[2]; C=2*Q
    rows=256; NCH=block//rows
    cuts=((0,Q),(Q,C)); NW=len(cuts)
    V=pl.BlockSpec(memory_space=pltpu.VMEM); A=pl.BlockSpec(memory_space=pl.ANY)
    S=jax.ShapeDtypeStruct; M=pltpu.VMEM; D=pltpu.SemaphoreType.DMA
    return pl.pallas_call(functools.partial(reduce_kernel,Z,block,E,W,C1,rows,cuts),
        out_shape=[S((2,block,E),bf),S((16,C+C1),f32)],
        in_specs=[A,A,V,V],out_specs=[A,V],
        scratch_shapes=[M((2,block,E),bf),M((2,block,E),r1.dtype),M((2,block,E),bf),M((block,E),bf),M((2,block,E),bf),
            M((Z,2,2,16,Q),bf),M((Z,2,2,16,Q),bf),M((Z,2,2,16,C),bf),M((Z,2,16,C),bf),M((Z,2,16,C),bf),
            M((Z,2,16,C),bf),M((Z,2,16,C),bf),M((2,16,C),f32),M((16,C),bf),M((16,C),bf),M((2,16,C1),bf),M((2,16,C1),bf),M((16,C1),bf),M((16,C1),bf),
            D((3,)),D((2,NCH)),D((2,NCH)),D((NCH,)),D((NCH,)),D((2,)),D((2,)),D((NW,)),D((NW,)),D((NW,Z)),D((NW,Z)),D((NW+1,)),D((NW+1,))],
        compiler_params=pltpu.CompilerParams(collective_id=1,has_side_effects=True,vmem_limit_bytes=VMEM))(tg,r1,gq,parts)
def shards(tokens,cotangent,segments,padding,known,w_qkv,w_out,w_up,w_down,norm_gains,norm_shifts):
    micro,rows,block,D=tokens.shape
    J=lax.axis_size("blk")//2; dps=lax.axis_size("dp")
    units=micro*rows
    assert units==J
    H=HEADS//2; W=H*HEAD; L=2*J*block; F=w_up.shape[1]
    quick=J==2 and dps%2==0 and w_qkv.shape[0]==16 and block%256==0
    me=lax.axis_index("blk"); chip=me//2; core=me%2
    flat=lambda x:x.reshape((units,)+x.shape[2:])
    if quick:
        Z=dps//2
        tok,bund,w_mine,qkvt,base,win,codet,meta=gather(flat(tokens),*[flat(x)[:,None,:] for x in (segments,padding,known)],w_qkv,w_out,w_up,w_down,norm_gains,norm_shifts,Z,W)
        cot=flat(cotangent)
        def move(x,k,b): return lax.ppermute(x,"dp",[(d,(d//2+k)%Z*2+(d%2^b)) for d in range(dps)])
        far,base=lax.optimization_barrier((jnp.where(chip==0,cot[1],cot[0]),base))
        bunds=[bund]+[move(bund,k,0) for k in range(1,Z)]
        cotx=lax.ppermute(far,"blk",[(b,b^2) for b in range(4)])
        p,att,ot,inv,kaug,vaug=attend(base,win,qkvt,codet,meta,H)
        layer_out,r1,datt,parts=middle_net(att.reshape(H//2,2,2,block,128),tok,cot,cotx,bunds,Z,W,F)
        parts=lax.all_to_all(parts,"dp",0,0,tiled=True)
        tg,gq=back(base,win,datt.reshape(H//2,L,128),p,ot,inv,kaug,vaug,qkvt,meta,tok.reshape(L,D),w_mine,H)
        token_grad,grads=reduce(tg.reshape(2,2,block,D),r1,gq,parts,Z,W)
        a,b,e=6*W,6*W+D,6*W+D+F
        gg=grads[:,e+D:e+D+4].T
        return (layer_out.reshape(tokens.shape),token_grad.reshape(tokens.shape),grads[:,:a],grads[:,a:b],grads[:,b:e],grads[:,e:e+D],gg[:2],gg[2:])
    def to_chip(s): return [(2*a+c,2*((a+s)%J)+c) for a in range(J) for c in range(2)]
    swap=[(b,b^1) for b in range(2*J)]
    def other(x): return lax.ppermute(x,"blk",swap)
    def scatter_units(x):
        got=[]
        for s in range(J):
            mine=lax.dynamic_index_in_dim(x,(chip+s)%J,0,keepdims=False)
            got.append(mine if s==0 else lax.ppermute(mine,"blk",to_chip(s)))
        return jnp.stack([lax.dynamic_index_in_dim(jnp.stack(got),(chip-j)%J,0,keepdims=False) for j in range(J)])
    def both(mine,his):
        return jnp.stack([jnp.where(core==0,mine,his),jnp.where(core==0,his,mine)],1)
    def part(x,axis,index): return lax.dynamic_index_in_dim(x,index,axis,keepdims=False)
    own_info=scatter_units(flat(segments*4+padding*2+known)); info=both(own_info,other(own_info)).reshape(1,L)
    own_tok=scatter_units(flat(tokens)); all_tok=both(own_tok,other(own_tok)).reshape(L,D)
    own_cot=scatter_units(flat(cotangent)).reshape(L//2,D)
    full_qkv,full_out,full_up,full_down=[lax.all_gather(w,("dp","blk"),axis=0,tiled=True) for w in (w_qkv,w_out,w_up,w_down)]
    gs=lax.all_gather(jnp.concatenate([norm_gains,norm_shifts],0),("dp","blk"),axis=1,tiled=True).astype(f32)
    gs=jnp.concatenate([gs,jnp.zeros_like(gs)],0)
    w_mine=part(full_qkv.reshape(D,3,2,W),2,core).reshape(D,3*W)
    scale=jnp.where(jnp.arange(3*W)<W,math.log2(math.e)/8,1.0).astype(f32)
    qkvt=(jnp.einsum("ld,de->el",all_tok,w_mine,preferred_element_type=f32)*scale[:,None]).astype(bf)
    base,win,codet,meta=flags(info)
    p,att,ot,inv,kaug,vaug=attend(base,win,qkvt,codet,meta,H)
    att=att.reshape(H//2,J,2,block,128)
    mine=part(att,2,core).reshape(H//2,J*block,128); his=other(part(att,2,1-core)).reshape(H//2,J*block,128)
    a0=jnp.where(core==0,mine,his); a1=jnp.where(core==0,his,mine)
    out,r1,da,go,gu,gd,gg=middle(a0,a1,own_tok.reshape(L//2,D),own_cot,full_out,full_up,full_down,gs)
    da=da.reshape(2,H//2,J,block,128)
    dmine=part(da,0,core); dhis=other(part(da,0,1-core))
    datt=jnp.stack([jnp.where(core==0,dmine,dhis),jnp.where(core==0,dhis,dmine)],2).reshape(H//2,L,128)
    tg,gq=back(base,win,datt,p,ot,inv,kaug,vaug,qkvt,meta,all_tok,w_mine,H)
    tg=tg.reshape(J,2,block,D)
    layer_out=scatter_units(out.reshape(J,block,D)).reshape(tokens.shape)
    own_tg=(part(tg,1,core).astype(f32)+other(part(tg,1,1-core)).astype(f32)+r1.reshape(J,block,D)).astype(bf)
    token_grad=scatter_units(own_tg).reshape(tokens.shape)
    gq=gq.astype(f32).reshape(D,3,1,W)
    gq=jnp.where(core==0,jnp.concatenate([gq,jnp.zeros_like(gq)],2),jnp.concatenate([jnp.zeros_like(gq),gq],2)).reshape(D,6*W)
    grads=lax.psum_scatter(jnp.concatenate([gq,go,gu,gd],1),("dp","blk"),scatter_dimension=0,tiled=True)
    gg=lax.psum_scatter(gg[:4],("dp","blk"),scatter_dimension=1,tiled=True)
    a,b,e=6*W,6*W+D,6*W+D+F
    return (layer_out,token_grad,grads[:,:a],grads[:,a:b],grads[:,b:e],grads[:,e:],gg[:2],gg[2:])

def solution(mesh):
    in_specs = (
        P(None, "dp", "blk", None),
        P(None, "dp", "blk", None),
        P(None, "dp", "blk"),
        P(None, "dp", "blk"),
        P(None, "dp", "blk"),
        P(("dp", "blk"), None),
        P(("dp", "blk"), None),
        P(("dp", "blk"), None),
        P(("dp", "blk"), None),
        P(None, ("dp", "blk")),
        P(None, ("dp", "blk")),
    )
    out_specs = (
        P(None, "dp", "blk", None),
        P(None, "dp", "blk", None),
        P(("dp", "blk"), None),
        P(("dp", "blk"), None),
        P(("dp", "blk"), None),
        P(("dp", "blk"), None),
        P(None, ("dp", "blk")),
        P(None, ("dp", "blk")),
    )
    return jax.shard_map(shards, mesh=mesh, in_specs=in_specs, out_specs=out_specs, check_vma=False)
```

time: 412 us -> 343 us (0.83)
  Pallas kernels: 358 us -> 183 us
  starting transfers between devices: 7.97 us -> 148 us
  local copies, waits for them, and re-layouts: 29.5 us -> 8.93 us
  other arithmetic: 12.6 us -> 2.33 us
    all_to_all x0 -> x1, starting transfers between devices: none -> 143 us  [shards(): parts = lax.all_to_all(parts, 'dp', 0, 0, tiled=True)]
    pallas_call x1, Pallas kernels: 152 us -> 31.7 us  [attend(): pl.pallas_call(functools.partial(attend_kernel, L, H), out_shape=[S((cap,...]
    pallas_call x3, Pallas kernels: 145 us -> 91 us  [the longest x1 33.6 us: gather(): pl.pallas_call(functools.partial(gather_kernel, Z, block, E, W, rows), ou...]
    squeeze x4 -> x0, local copies, waits for them, and re-layouts: 6.69 us -> none  [the longest x2 4.03 us: part(): return lax.dynamic_index_in_dim(x, index, axis, keepdims=False)]
    another operation x9 -> x0, other arithmetic: 4.38 us -> none  [the longest x3 2.63 us: scatter_units(): jnp.stack([lax.select_n((chip - j) % J, *got) if J == 2 else lax.dynamic_...]
    slice x6 -> x0, local copies, waits for them, and re-layouts: 4.3 us -> none  [the longest x1 2.71 us: shards(): wall[:, 6 * W + D + F:6 * W + 2 * D + F]]
    unnamed x25 -> x6, local copies, waits for them, and re-layouts: 8.57 us -> 5.07 us
  transfers between devices with their start and end apart: 4 -> 5, of which waited for: 0 -> 0; matrix products, arithmetic and copies ran while one was open for 6% -> 0% of each run, Pallas kernels for 73% -> 27%
where the time goes in v2:
time: 343 us
  Pallas kernels  183 us (53%)
  starting transfers between devices  148 us (43%)
  local copies, waits for them, and re-layouts  8.93 us (3%)
    all_to_all x1, starting transfers between devices, shards(): parts = lax.all_to_all(parts, 'dp', 0, 0, tiled=True)  143 us
    pallas_call x1, Pallas kernels, back(): pl.pallas_call(functools.partial(back_kernel, L, H), out_shape=[S((L, E),...  60.5 us
    pallas_call x1, Pallas kernels, gather(): pl.pallas_call(functools.partial(gather_kernel, Z, block, E, W, rows), ou...  33.6 us
    pallas_call x1, Pallas kernels, reduce(): pl.pallas_call(functools.partial(reduce_kernel, Z, block, E, W, C1, rows,...  31.8 us
    pallas_call x1, Pallas kernels, attend(): pl.pallas_call(functools.partial(attend_kernel, L, H), out_shape=[S((cap,...  31.7 us
    pallas_call x1, Pallas kernels, middle_net(): pl.pallas_call(functools.partial(middle_net_kernel, Z, block, E, F, W, T)...  25.6 us
  transfers between devices with their start and end apart: 5, of which 0 were waited for; matrix products, arithmetic and copies ran while one was open for 0% of the time, Pallas kernels for 27%

profile of v2, /device:TPU:0, one launch (start us, length us, event | category | flops | bytes accessed | tf_op | source)
XLA Modules:
  0.0 342.9 jit_solution(17576730313369254422)
XLA Ops:
  0.6 2.3 select_bitcast_fusion
  3.0 33.6 %shard_map.170 = (bf16[2,2,768,512]{3,2,1,0:T(8,128)(2,1)}, bf16[2,2,16,1664]{3,2,1,0:T(8,128)(2,1)}, bf16[512,768]{1,0:T(8,128)(2,1)}, bf16[768,3072]{1,0:T(8,1...) custom-call(bf16[2,768,512]{2,1,0:T(8,128)(2,1)} %bitcast.21, ...), custom_call_target="tpu_custom_call" | custom-call | tf_op jit(solution)/shard_map/pallas_call | solution.py:484
  36.6 0.2 collective-permute-start
  36.8 3.4 collective-permute-start.3
  40.2 0.0 collective-permute-start.2
  40.2 1.1 collective-permute-start.1
  41.3 31.7 %shard_map.171 = (bf16[42,4,512,512]{3,2,1,0:T(8,128)(2,1)}, bf16[2,3072,128]{2,1,0:T(8,128)(2,1)}, f32[6,256,512]{2,1,0:T(8,128)}, f32[4,8,3072]{2,1,0:T(8,128)...) custom-call(s32[16,128]{1,0:T(8,128)} %get-tuple-element.33.base_ref, ...), custom_call_target="tpu_custom_call" | custom-call | tf_op jit(solution)/shard_map/pallas_call | solution.py:163
  73.0 0.0 collective-permute-done.3.rest_3_
  73.0 0.0 collective-permute-done.2.rest_2_
  73.0 0.0 collective-permute-done.1.rest_1_
  73.1 0.0 collective-permute-done.cotx_hbm
  73.1 25.6 %shard_map.172 = (bf16[2,768,512]{2,1,0:T(8,128)(2,1)}, f32[2,768,512]{2,1,0:T(8,128)}, bf16[2,2,2,768,128]{4,3,2,1,0:T(8,128)(2,1)}, bf16[8,64,1664]{2,1,0:T(8,128)(2,1)}) custom-call(bf16[2,2,2,768,128]{4,3,2,1,0:T(8,128)(2,1)} %bitcast.22, bf16[2,2,768,512]{3,2,1,0:T(8,128)(2,1)} %get-tuple-element.39.tok_hbm, bf16[2,768,512]{2,1,0:T(8,128)(2,1)} %bitcast.17, ...), custom_call_target="tpu_custom_call" | custom-call | tf_op jit(solution)/shard_map/pallas_call | solution.py:607
  98.7 142.9 %all-to-all-start = ((bf16[8,64,1664]{2,1,0:T(8,128)(2,1)}), bf16[8,64,1664]{2,1,0:T(8,128)(2,1)}, u32[]{:S(2)}, u32[]{:S(2)}) async-start(bf16[8,64,1664]{2,1,0:T(8,128)(2,1)} %get-tuple-element.53), calls=%async_computation | async-start | bytes 3407872 | tf_op jit(solution)/shard_map/all_to_all | solution.py:730
  241.6 60.5 %shard_map.173 = (bf16[3072,512]{1,0:T(8,128)(2,1)}, bf16[512,768]{1,0:T(8,128)(2,1)}) custom-call(s32[16,128]{1,0:T(8,128)} %get-tuple-element.33.base_ref, s32[16,128]{1,0:T(8,128)} %get-tuple-element.34.win_ref, bf16[2,3072,128]{2,1,0:T(8,128)(2,1)} %bitcast.23, bf16[42,4,512,512]{3,2,1,0:T(8,128)(2,1)} %get-tuple-element.44.p_hbm, ...), custom_call_target="tpu_custom_call" | custom-call | tf_op jit(solution)/shard_map/pallas_call | solution.py:291
  302.1 0.0 all-to-all-done.parts
  302.1 31.8 %shard_map.174 = (bf16[2,768,512]{2,1,0:T(8,128)(2,1)}, f32[16,3200]{1,0:T(8,128)}) custom-call(bf16[2,2,768,512]{3,2,1,0:T(8,128)(2,1)} %bitcast.18, f32[2,768,512]{2,1,0:T(8,128)} %get-tuple-element.51.r1_hbm, bf16[512,768]{1,0:T(8,128)(2,1)} %get-tuple-element.52.gq_ref, bf16[8,64,1664]{2,1,0:T(8,128)(2,1)} %all-to-all-done.parts), custom_call_target="tpu_custom_call" | custom-call | tf_op jit(solution)/shard_map/pallas_call | solution.py:703
  333.9 0.7 slice_bitcast_fusion
  334.6 1.5 slice.31
  336.2 0.0 copy-start
  336.2 1.5 fusion
  337.7 0.1 fusion.1
  337.8 0.6 copy.22
  338.4 0.6 copy.21
  339.1 2.7 copy.25
  341.7 0.0 copy-done
  341.7 1.1 copy.26
Async XLA Ops:
  36.6 36.4 %collective-permute-start = (bf16[768,512]{1,0:T(8,128)(2,1)}, bf16[768,512]{1,0:T(8,128)(2,1)}, u32[]{:S(2)}, u32[]{:S(2)}) collective-permute-start(bf16[768,512]{1,0:T(8,128)(2,1)} %select_bitcast_fusion), channel_id=1, source_target_pairs={{0,2},{1,3},{2,0},{3,1},{4,6},{5,7},{6,4},{7,5},{8,10},{9,11},{10,... | collective-permute-start | bytes 2359304 | tf_op jit(solution)/shard_map/ppermute | solution.py:727
  36.8 36.2 %collective-permute-start.3 = (bf16[2,2,16,1664]{3,2,1,0:T(8,128)(2,1)}, bf16[2,2,16,1664]{3,2,1,0:T(8,128)(2,1)}, u32[]{:S(2)}, u32[]{:S(2)}) collective-permute-start(bf16[2,2,16,1664]{3,2,1,0:T(8,128)(2,1)} %get-tuple-element.41.rest_0_), channel_id=1, source_target_pairs={{0,24},{4,28},{8,0},{12,4},{16,8},{20,12},{24,16},{28,20},{1,25},{... | collective-permute-start | bytes 638984 | tf_op jit(solution)/shard_map/ppermute | solution.py:724
  40.2 32.9 %collective-permute-start.2 = (bf16[2,2,16,1664]{3,2,1,0:T(8,128)(2,1)}, bf16[2,2,16,1664]{3,2,1,0:T(8,128)(2,1)}, u32[]{:S(2)}, u32[]{:S(2)}) collective-permute-start(bf16[2,2,16,1664]{3,2,1,0:T(8,128)(2,1)} %get-tuple-element.41.rest_0_), channel_id=1, source_target_pairs={{0,16},{4,20},{8,24},{12,28},{16,0},{20,4},{24,8},{28,12},{1,17},{... | collective-permute-start | bytes 638984 | tf_op jit(solution)/shard_map/ppermute | solution.py:724
  40.2 32.9 %collective-permute-start.1 = (bf16[2,2,16,1664]{3,2,1,0:T(8,128)(2,1)}, bf16[2,2,16,1664]{3,2,1,0:T(8,128)(2,1)}, u32[]{:S(2)}, u32[]{:S(2)}) collective-permute-start(bf16[2,2,16,1664]{3,2,1,0:T(8,128)(2,1)} %get-tuple-element.41.rest_0_), channel_id=1, source_target_pairs={{0,8},{4,12},{8,16},{12,20},{16,24},{20,28},{24,0},{28,4},{1,9},{5... | collective-permute-start | bytes 638984 | tf_op jit(solution)/shard_map/ppermute | solution.py:724
  98.7 203.5 %all-to-all-start = ((bf16[8,64,1664]{2,1,0:T(8,128)(2,1)}), bf16[8,64,1664]{2,1,0:T(8,128)(2,1)}, u32[]{:S(2)}, u32[]{:S(2)}) async-start(bf16[8,64,1664]{2,1,0:T(8,128)(2,1)} %get-tuple-element.53), calls=%async_computation | async-start | bytes 3407872 | tf_op jit(solution)/shard_map/all_to_all | solution.py:730
  336.2 5.6 %copy-start = (bf16[2,768,512]{2,1,0:T(8,128)(2,1)S(1)}, bf16[2,768,512]{2,1,0:T(8,128)(2,1)}, u32[]{:S(2)}) copy-start(bf16[2,768,512]{2,1,0:T(8,128)(2,1)} %get-tuple-element.54) | copy-start | bytes 4718596

commit v3 on v2

v3 whole, which is shorter than its diff:
```python
import functools, math
import jax, jax.numpy as jnp
from jax import lax
from jax.experimental import pallas as pl
from jax.experimental.pallas import tpu as pltpu
from jax.sharding import PartitionSpec as P

HEADS = 8
bf=jnp.bfloat16; f32=jnp.float32
HEAD=64
QB=512
KB=512
SRC=1024
SAFE=60.0
CODE=16
VMEM=(64<<20)-(128<<10)
SLOTS=3
def dot(a,b,ca,cb): return lax.dot_general(a,b,(((ca,),(cb,)),((),())),preferred_element_type=f32)
def al(x,n): return pl.multiple_of(x,n)
def iota(shape,axis): return lax.broadcasted_iota(jnp.int32,shape,axis)

def begin(base_ref,b):
    return base_ref[b,0]

def window(win_ref,i):
    start=win_ref[i,0]//128*128
    groups=(win_ref[8+i,0]-start+127)//128
    full=(groups-1)//(KB//128)
    return start,full,groups-full*(KB//128),groups

def by_piece(first,full,rest,g,fn):
    def body(j,g):
        fn(al(first+j*KB,128),KB,g)
        return g+1
    g=lax.fori_loop(0,full,body,g)
    for r in range(1,KB//128+1):
        @pl.when(rest==r)
        def _(): fn(al(first+full*KB,128),r*128,g)
    return g+1

def attend_kernel(L,H,base_ref,win_ref,qkvt_hbm,codet_ref,meta_ref,p_hbm,att_hbm,ot_hbm,inv_ref,kct_hbm,vaug_hbm,
                  kaug_ref,kct_ref,vaug_ref,kvt,q_ref,v_ref,vct,acc,pbuf,obuf,abuf,top_ref,psem,osem,asem,ksem,lsem):
    W=H*HEAD; nq=L//QB
    total=begin(base_ref,L//256)
    come=[pltpu.make_async_copy(qkvt_hbm.at[W+h*HEAD:W+(h+1)*HEAD],kvt.at[h*128:h*128+HEAD],lsem.at[h]) for h in range(H)]
    come+=[pltpu.make_async_copy(qkvt_hbm.at[2*W:],v_ref,lsem.at[H]),pltpu.make_async_copy(qkvt_hbm.at[:W],q_ref,lsem.at[H+1])]
    for x in come: x.start()
    for h in range(H):
        kvt[h*128+HEAD:h*128+HEAD+CODE,:]=codet_ref[...]
        kvt[h*128+HEAD+CODE:(h+1)*128,:]=jnp.zeros((HEAD-CODE,L),bf)
    vct[:,HEAD:,:]=jnp.ones((H,16,L),bf)
    for x in come[:H+1]: x.wait()
    row=iota((256,256),0)
    down=iota((256,SRC),0)
    def dest(d,c):
        first=jnp.minimum(win_ref[16+d,0]//128*128,L-SRC)
        last=win_ref[17+d,0]
        def src(t,a):
            ssl=pl.ds(al(jnp.minimum(first+t*SRC,L-SRC),128),SRC)
            oh=((meta_ref[0:1,ssl]==down+d*256)&(lane>=first+t*SRC-jnp.minimum(first+t*SRC,L-SRC))).astype(f32).astype(bf)
            return a[0]+dot(kvt[:,ssl],oh,1,1),a[1]+dot(v_ref[:,ssl],oh,1,1)
        lane=iota((256,SRC),1)
        ka,va=src(0,(jnp.zeros((H*128,256),f32),jnp.zeros((W,256),f32)))
        ka,va=lax.fori_loop(1,(last-first+SRC-1)//SRC,src,(ka,va))
        dsl=pl.ds(al(d*256,256),256)
        for h in range(H):
            k1=jnp.where(row[:128]==HEAD+10,-2560.0,ka[h*128:(h+1)*128])
            kaug_ref[h,dsl,:]=k1.astype(bf).T
            kct_ref[h,:,dsl]=k1[:HEAD].astype(bf)
            v1=va[h*HEAD:(h+1)*HEAD]
            vct[h,:HEAD,dsl]=v1.astype(bf)
            vaug_ref[h,dsl,:]=jnp.concatenate([v1,jnp.where(row[:HEAD]<3,-1.0,0.0)],0).astype(bf).T
        return c
    lax.fori_loop(0,(total+255)//256,dest,0)
    keep=[pltpu.make_async_copy(kct_ref,kct_hbm,ksem.at[0]),pltpu.make_async_copy(vaug_ref,vaug_hbm,ksem.at[1])]
    for x in keep: x.start()
    come[H+1].wait()
    bound=jnp.float32(0)
    for h in range(H):
        q=q_ref[h*HEAD:(h+1)*HEAD,:].astype(f32); k=kvt[h*128:h*128+HEAD,:].astype(f32)
        bound=jnp.maximum(bound,jnp.max(jnp.sum(q*q,0,keepdims=True))*jnp.max(jnp.sum(k*k,0,keepdims=True)))
    safe=bound<SAFE*SAFE

    def pcopy(g):
        slot=lax.rem(g,SLOTS)
        return pltpu.make_async_copy(pbuf.at[slot],p_hbm.at[g],psem.at[slot])
    def ocopy(i):
        slot=lax.rem(i,2)
        return pltpu.make_async_copy(obuf.at[slot],ot_hbm.at[i],osem.at[slot])
    def acopy(i):
        slot=lax.rem(i,2)
        return pltpu.make_async_copy(abuf.at[slot],att_hbm.at[:,pl.ds(al(i*QB,QB),QB),:],asem.at[slot])
    def block(i,g):
        slot=lax.rem(i,2)
        qsl=pl.ds(al(i*QB,QB),QB)
        first,full,rest,groups=window(win_ref,i)
        qa=[jnp.concatenate([q_ref[h*HEAD:(h+1)*HEAD,qsl],codet_ref[:,qsl],jnp.zeros((HEAD-CODE,QB),bf)],0) for h in range(H)]
        own=meta_ref[1:2,qsl]>0
        sself=[]
        for h in range(H):
            x=q_ref[h*HEAD:(h+1)*HEAD,qsl].astype(f32)*kvt[h*128:h*128+HEAD,qsl].astype(f32)
            sself.append(jnp.where(own,jnp.sum(x,0,keepdims=True),-1e30))
        acc[...]=jnp.zeros_like(acc)
        top_ref[...]=jnp.zeros_like(top_ref)
        row=iota((128,QB),0)
        def strict(h,osl):
            k=kaug_ref[h,osl,:]
            x=qa[h].astype(f32)
            plain=dot(k,jnp.where(row<HEAD,x,0.0).astype(bf),1,0)
            return jnp.where(dot(k,jnp.where(row<HEAD,0.0,x).astype(bf),1,0)>-1.0,plain,-1e30)
        @pl.when(jnp.logical_not(safe))
        def _():
            for h in range(H):
                def more(j,m): return jnp.maximum(m,jnp.max(strict(h,pl.ds(al(first+j*128,128),128)),0,keepdims=True))
                top_ref[h:h+1,:]=lax.fori_loop(0,groups,more,sself[h])
        def piece(off,size,g):
            ps=lax.rem(g,SLOTS)
            osl=pl.ds(off,size)
            @pl.when(g>=SLOTS)
            def _(): pcopy(g-SLOTS).wait()
            @pl.when(safe)
            def _():
                keepp=[]
                for h in range(H):
                    p=jnp.exp2(dot(kaug_ref[h,osl,:],qa[h],1,0)).astype(bf)
                    pbuf[ps,h,:size,:]=p
                    keepp.append(p)
                for h in range(H): acc[h]+=dot(vct[h,:,osl],keepp[h],1,0)
            @pl.when(jnp.logical_not(safe))
            def _():
                for h in range(H):
                    def put(j,c):
                        jsl=pl.ds(al(off+j*128,128),128)
                        p=jnp.exp2(strict(h,jsl)-top_ref[h:h+1,:]).astype(bf)
                        pbuf[ps,h,pl.ds(al(j*128,128),128),:]=p
                        acc[h]+=dot(vct[h,:,jsl],p,1,0)
                        return c
                    lax.fori_loop(0,size//128,put,0)
            pcopy(g).start()
        g=by_piece(first,full,rest,g,piece)
        @pl.when(i>=2)
        def _(): ocopy(i-2).wait(); acopy(i-2).wait()
        for h in range(H):
            ps=jnp.exp2(sself[h]-top_ref[h:h+1,:])
            inv=1.0/(acc[h,HEAD:HEAD+1,:]+ps)
            obuf[slot,h*HEAD:(h+1)*HEAD,:]=(acc[h,:HEAD,:]+ps*v_ref[h*HEAD:(h+1)*HEAD,qsl].astype(f32))*inv
            inv_ref[h,0:1,qsl]=inv
            inv_ref[h,1:2,qsl]=ps
        for hp in range(H//2): abuf[slot,hp]=obuf[slot,hp*128:(hp+1)*128,:].T.astype(bf)
        ocopy(i).start(); acopy(i).start()
        return g
    g=lax.fori_loop(0,nq,block,0)
    for s in range(SLOTS):
        last=g-1-s
        @pl.when(last>=0)
        def _(): pcopy(last).wait()
    for i in range(max(nq-2,0),nq): ocopy(i).wait(); acopy(i).wait()
    for x in keep: x.wait()

def attend(base,win,qkvt,codet,meta,H):
    L=qkvt.shape[1]; W=H*HEAD; nq=L//QB; cap=nq*(L//KB+1)
    V=pl.BlockSpec(memory_space=pltpu.VMEM); A=pl.BlockSpec(memory_space=pl.ANY)
    S=jax.ShapeDtypeStruct; M=pltpu.VMEM; D=pltpu.SemaphoreType.DMA
    return pl.pallas_call(functools.partial(attend_kernel,L,H),
        out_shape=[S((cap,H,KB,QB),bf),S((H//2,L,128),bf),S((nq,W,QB),f32),S((H,8,L),f32),S((H,HEAD,L),bf),S((H,L,128),bf)],
        in_specs=[pl.BlockSpec(memory_space=pltpu.SMEM)]*2+[A,V,V],
        out_specs=[A,A,A,V,A,A],
        scratch_shapes=[M((H,L,128),bf),M((H,HEAD,L),bf),M((H,L,128),bf),M((H*128,L),bf),M((W,L),bf),M((W,L),bf),M((H,HEAD+16,L),bf),M((H,HEAD+16,QB),f32),M((SLOTS,H,KB,QB),bf),
            M((2,W,QB),f32),M((2,H//2,QB,128),bf),M((8,QB),f32),D((SLOTS,)),D((2,)),D((2,)),D((2,)),D((H+2,))],
        compiler_params=pltpu.CompilerParams(vmem_limit_bytes=VMEM))(base,win,qkvt,codet,meta)

def flags(row):
    L=row.shape[1]; nb=L//256; nq=L//QB
    seg=row//4
    pad=row//2-2*seg
    known=row-2*(row//2)
    use=(pad==0)&(known==1)
    usef=use.astype(f32)
    x=jnp.concatenate([usef[:,b*256:(b+1)*256] for b in range(nb)]+[jnp.zeros((16-nb,256),f32)],0)
    incl=dot(x.astype(bf),(iota((256,256),0)<=iota((256,256),1)).astype(f32).astype(bf),1,0)
    tot=jnp.broadcast_to(incl[:,255:256],(16,256)).astype(bf)
    base=dot((iota((16,16),0)>iota((16,16),1)).astype(f32).astype(bf),tot,1,0)
    rank=(incl+base).astype(jnp.int32)-1
    rank=jnp.concatenate([rank[b:b+1] for b in range(nb)],1)
    rank=jnp.where(use,rank,-1)
    own=((pad==0)&(known!=1)).astype(jnp.int32)
    bits=iota((CODE,L),0)
    bit=lax.shift_right_logical(jnp.broadcast_to(seg,(CODE,L)),jnp.minimum(bits,9))&1
    codet=jnp.where(bits<10,jnp.where(bit==1,16.0,-16.0),jnp.where(bits==10,1.0,0.0)).astype(bf)
    meta=jnp.concatenate([rank,own,jnp.zeros((6,L),jnp.int32)],0)
    def edge(at): return jnp.concatenate([seg[:,i*QB+at:i*QB+at+1] for i in range(nq)]+[jnp.zeros((8-nq,1),jnp.int32)],0)
    low=jnp.sum(jnp.where(seg<edge(0),usef,0.0),1,keepdims=True)
    high=jnp.sum(jnp.where(seg<=edge(QB-1),usef,0.0),1,keepdims=True)
    csum=jnp.concatenate([(incl+base)[b:b+1] for b in range(nb)],1)
    starts=jnp.sum((csum<=(256*iota((16,1),0)).astype(f32)).astype(f32),1,keepdims=True)
    win=jnp.broadcast_to(jnp.concatenate([low,high,starts],0),(32,128)).astype(jnp.int32)
    return base[:,:128].astype(jnp.int32),win,codet,meta
LN2=math.log(2.0)
SPAN=384
def back_kernel(L,H,base_ref,win_ref,datt_hbm,p_hbm,ot_hbm,inv_ref,kct_hbm,vaug_hbm,qkvt_hbm,dq_hbm,dkvw_hbm,
                vaug_ref,kct,dkv,dkvt,pbuf,qacc,qkv,datt,ot,dq,psem,lsem,qsem,osem,tsem):
    W=H*HEAD; nq=L//QB
    groups=(begin(base_ref,L//256)+127)//128
    pieces=lax.fori_loop(0,nq,lambda i,s:s+window(win_ref,i)[1]+1,0)
    def pcopy(g):
        slot=lax.rem(g,SLOTS)
        return pltpu.make_async_copy(p_hbm.at[g],pbuf.at[slot],psem.at[slot])
    def keys(t):
        rows=pl.ds(al(t*KB,KB),KB)
        return [pltpu.make_async_copy(kct_hbm.at[:,:,rows],kct.at[:,:,rows],lsem.at[0,t]),pltpu.make_async_copy(vaug_hbm.at[:,rows],vaug_ref.at[:,rows],lsem.at[1,t])]
    def queries(i):
        slot=lax.rem(i,2); qsl=pl.ds(al(i*QB,QB),QB)
        return [pltpu.make_async_copy(a,b.at[slot],qsem.at[k,slot]) for k,(a,b) in enumerate(((qkvt_hbm.at[:,qsl],qkv),(datt_hbm.at[:,qsl],datt),(ot_hbm.at[i],ot)))]
    def each_key(fn):
        def body(t,c):
            for x in keys(t): fn(x)
            return c
        lax.fori_loop(0,(groups+KB//128-1)//(KB//128),body,0)
    each_key(lambda x:x.start())
    for x in queries(0): x.start()
    for s in range(SLOTS-1):
        @pl.when(s<pieces)
        def _(): pcopy(s).start()
    def clear(j,c):
        dkv[pl.ds(al(j*128,128),128),:]=jnp.zeros((128,2*W),f32)
        return c
    lax.fori_loop(0,groups,clear,0)
    each_key(lambda x:x.wait())
    def ocopy(i):
        slot=lax.rem(i,2)
        return pltpu.make_async_copy(dq.at[slot],dq_hbm.at[:,pl.ds(al(i*QB,QB),QB)],osem.at[slot])
    def block(i,g):
        slot=lax.rem(i,2)
        qsl=pl.ds(al(i*QB,QB),QB)
        first,full,rest,_=window(win_ref,i)
        for x in queries(i): x.wait()
        @pl.when(i+1<nq)
        def _():
            for x in queries(i+1): x.start()
        dt=jnp.concatenate([datt[slot,hp].astype(f32).T for hp in range(H//2)],0)
        prod=dt*ot[slot]
        daug=[];dz=[];qz=[];deltas=[];d1s=[]
        zero=jnp.zeros((HEAD,QB),bf)
        row=iota((16,QB),0)
        for h in range(H):
            hsl=slice(h*HEAD,(h+1)*HEAD)
            inv=inv_ref[h,0:1,qsl]
            delta=jnp.sum(prod[hsl],0,keepdims=True)*inv
            d1=dt[hsl]*inv
            low=d1.astype(bf)
            a=delta.astype(bf).astype(f32); b=(delta-a).astype(bf).astype(f32)
            extra=jnp.where(row==0,a,jnp.where(row==1,b,jnp.where(row==2,delta-a-b,0.0))).astype(bf)
            daug.append(jnp.concatenate([low,extra,jnp.zeros((HEAD-16,QB),bf)],0))
            q=qkv[slot,hsl,:]
            dz.append(jnp.concatenate([zero,low] if h%2 else [low,zero],0))
            qz.append(jnp.concatenate([zero,q] if h%2 else [q,zero],0))
            deltas.append(delta); d1s.append(d1)
        qacc[...]=jnp.zeros_like(qacc)
        def piece(off,size,g):
            ps=lax.rem(g,SLOTS)
            osl=pl.ds(off,size)
            @pl.when(g+SLOTS-1<pieces)
            def _(): pcopy(g+SLOTS-1).start()
            pcopy(g).wait()
            dss=[]
            for h in range(H):
                dss.append((pbuf[ps,h,:size,:].astype(f32)*dot(vaug_ref[h,osl,:],daug[h],1,0)).astype(bf))
            for h in range(H): qacc[h*HEAD:(h+1)*HEAD,:]+=dot(kct[h,:,osl],dss[h],1,0)
            for h in range(0,H,2):
                dkv[osl,h*HEAD:(h+2)*HEAD]+=dot(dss[h],qz[h],1,1)+dot(dss[h+1],qz[h+1],1,1)
                dkv[osl,W+h*HEAD:W+(h+2)*HEAD]+=dot(pbuf[ps,h,:size,:],dz[h],1,1)+dot(pbuf[ps,h+1,:size,:],dz[h+1],1,1)
        g=by_piece(first,full,rest,g,piece)
        @pl.when(i>=2)
        def _(): ocopy(i-2).wait()
        for h in range(H):
            hsl=slice(h*HEAD,(h+1)*HEAD); ksl=slice(W+h*HEAD,W+(h+1)*HEAD); vsl=slice(2*W+h*HEAD,2*W+(h+1)*HEAD)
            ps=inv_ref[h,1:2,qsl]
            ds=ps*(jnp.sum(qkv[slot,vsl,:].astype(f32)*d1s[h],0,keepdims=True)-deltas[h])
            dq[slot,hsl,:]=((qacc[hsl,:]+ds*qkv[slot,ksl,:].astype(f32))*0.125).astype(bf)
            dq[slot,ksl,:]=(ds*qkv[slot,hsl,:].astype(f32)*LN2).astype(bf)
            dq[slot,vsl,:]=(ps*d1s[h]).astype(bf)
        ocopy(i).start()
        return g
    lax.fori_loop(0,nq,block,0)
    lanes=iota((128,2*W),1)
    def turn(j,c):
        jsl=pl.ds(al(j*128,128),128)
        x=jnp.where(j<groups,dkv[jsl,:],0.0)
        dkvt[:,jsl]=jnp.where(lanes<W,x*LN2,x).astype(bf).T
        return c
    lax.fori_loop(0,groups+3,turn,0)
    def tcopy(s): return pltpu.make_async_copy(dkvt.at[:,pl.ds(al(begin(base_ref,s)//128*128,128),SPAN)],dkvw_hbm.at[s],tsem.at[s])
    for s in range(L//256): tcopy(s).start()
    for i in range(max(nq-2,0),nq): ocopy(i).wait()
    for s in range(L//256): tcopy(s).wait()

def back(base,win,datt,p,ot,inv,kct,vaug,qkvt,H):
    L=qkvt.shape[1]; W=H*HEAD
    V=pl.BlockSpec(memory_space=pltpu.VMEM); A=pl.BlockSpec(memory_space=pl.ANY); N=pl.BlockSpec(memory_space=pltpu.SMEM)
    S=jax.ShapeDtypeStruct; M=pltpu.VMEM; D=pltpu.SemaphoreType.DMA
    return pl.pallas_call(functools.partial(back_kernel,L,H),
        out_shape=[S((3*W,L),bf),S((L//256,2*W,SPAN),bf)],
        in_specs=[N,N,A,A,A,V,A,A,A],
        out_specs=[A,A],
        scratch_shapes=[M((H,L,128),bf),M((H,HEAD,L),bf),M((L+384,2*W),f32),M((2*W,L+384),bf),M((SLOTS,H,KB,QB),bf),M((W,QB),f32),
            M((2,3*W,QB),bf),M((2,H//2,QB,128),bf),M((2,W,QB),f32),M((2,3*W,QB),bf),
            D((SLOTS,)),D((2,L//KB)),D((3,2)),D((2,)),D((L//256,))],
        compiler_params=pltpu.CompilerParams(vmem_limit_bytes=VMEM))(base,win,datt,p,ot,inv,kct,vaug,qkvt)

def placed(base_ref,rank_row,span,own,s):
    r0=begin(base_ref,s)//128*128
    oh=(rank_row==iota((SPAN,256),0)+r0).astype(f32).astype(bf)
    return dot(span,oh,1,0)+own.astype(f32)

def place_kernel(L,W,base_ref,meta_ref,dq_in,dkvw_ref,tok_ref,w_ref,tg_ref,grad_ref,dq_ref):
    dq_ref[...]=dq_in[...]
    def place(s,c):
        ssl=pl.ds(al(s*256,256),256)
        dq_ref[W:3*W,ssl]=placed(base_ref,meta_ref[0:1,ssl],dkvw_ref[s],dq_ref[W:3*W,ssl],s).astype(bf)
        tg_ref[ssl,:]=dot(dq_ref[:,ssl],w_ref[...],0,1).astype(bf)
        return c
    lax.fori_loop(0,L//256,place,0)
    grad_ref[...]=dot(dq_ref[...],tok_ref[...],1,0).T.astype(bf)

def place_all(base,meta,dq,dkvw,tok,w,H):
    L,E=tok.shape; W=H*HEAD
    V=pl.BlockSpec(memory_space=pltpu.VMEM); S=jax.ShapeDtypeStruct
    return pl.pallas_call(functools.partial(place_kernel,L,W),out_shape=[S((L,E),bf),S((E,3*W),bf)],
        in_specs=[pl.BlockSpec(memory_space=pltpu.SMEM)]+[V]*5,out_specs=[V,V],scratch_shapes=[pltpu.VMEM((3*W,L),bf)],
        compiler_params=pltpu.CompilerParams(vmem_limit_bytes=VMEM))(base,meta,dq,dkvw,tok,w)
EPSILON=1e-05
def erf(x):
    x=jnp.clip(x,-3.832506856900711,3.832506856900711)
    x2=x*x
    top=0.00022905065861350646
    for c in (0.0034082910107109506,0.050955695062380861,0.18520832239976145,1.128379143519084): top=top*x2+c
    low=-1.1791602954361697e-7
    for c in (0.000023547966471313185,0.0010179625278914885,0.014070470171167667,0.11098505178285362,0.49746925110067538,1.0): low=low*x2+c
    return x*top/low
def norm(x):
    center=x-jnp.mean(x,-1,keepdims=True)
    inverse=lax.rsqrt(jnp.mean(center*center,-1,keepdims=True)+EPSILON)
    return center*inverse,inverse
def norm_back(e,n,inverse):
    return inverse*(e-jnp.mean(e,-1,keepdims=True)-n*jnp.mean(e*n,-1,keepdims=True))
def middle_kernel(a0_ref,a1_ref,tok_ref,cot_ref,wo_ref,wu_ref,wd_ref,gs_ref,out_ref,r1_ref,da_ref,go_ref,gu_ref,gd_ref,gg_ref):
    @pl.when(pl.program_id(0)==0)
    def _():
        for r in (go_ref,gu_ref,gd_ref,gg_ref): r[...]=jnp.zeros_like(r)
    P2=a0_ref.shape[0]
    att=jnp.concatenate([a0_ref[p] for p in range(P2)]+[a1_ref[p] for p in range(P2)],1)
    g0,g1,b0,b1=[gs_ref[r:r+1,:] for r in range(4)]
    n1,inv1=norm(tok_ref[...].astype(f32)+dot(att,wo_ref[...],1,0))
    first=(n1*g0+b0).astype(bf)
    hidden=dot(first,wu_ref[...],1,0)
    cdf=0.5*(1.0+erf(hidden*math.sqrt(0.5)))
    act=(hidden*cdf).astype(bf)
    slope=cdf+hidden*jnp.exp(-0.5*hidden*hidden)*(1.0/math.sqrt(2.0*math.pi))
    n2,inv2=norm(first.astype(f32)+dot(act,wd_ref[...],1,0))
    out_ref[...]=(n2*g1+b1).astype(bf)
    cot=cot_ref[...].astype(f32)
    r2=norm_back(cot*g1,n2,inv2)
    feed=r2.astype(bf)
    gd_ref[...]+=dot(act,feed,0,0)
    dh=(dot(feed,wd_ref[...],1,1)*slope).astype(bf)
    gu_ref[...]+=dot(first,dh,0,0)
    df=r2+dot(dh,wu_ref[...],1,1)
    r1=norm_back(df*g0,n1,inv1)
    r1_ref[...]=r1
    db=r1.astype(bf)
    go_ref[...]+=dot(att,db,0,0)
    da=dot(db,wo_ref[...],1,1).astype(bf)
    for p in range(2*P2): da_ref[p]=da[:,p*128:(p+1)*128]
    gg_ref[0:1,:]+=jnp.sum(df*n1,0,keepdims=True)
    gg_ref[1:2,:]+=jnp.sum(cot*n2,0,keepdims=True)
    gg_ref[2:3,:]+=jnp.sum(df,0,keepdims=True)
    gg_ref[3:4,:]+=jnp.sum(cot,0,keepdims=True)

def middle(a0,a1,tok,cot,wo,wu,wd,gs):
    P2,N,_=a0.shape; D=tok.shape[1]; F=wu.shape[1]
    T=max(t for t in (256,192,128,64,32,16) if N%t==0)
    tile=pl.BlockSpec((T,D),lambda i:(i,0))
    def pairs(k): return pl.BlockSpec((k,T,128),lambda i:(0,i,0))
    def whole(s): return pl.BlockSpec(s,lambda i:(0,)*len(s))
    return pl.pallas_call(middle_kernel,grid=(N//T,),
        in_specs=[pairs(P2),pairs(P2),tile,tile,whole((D,D)),whole((D,F)),whole((F,D)),whole((8,D))],
        out_specs=[tile,tile,pairs(2*P2),whole((D,D)),whole((D,F)),whole((F,D)),whole((8,D))],
        out_shape=[jax.ShapeDtypeStruct((N,D),bf),jax.ShapeDtypeStruct((N,D),f32),jax.ShapeDtypeStruct((2*P2,N,128),bf),
            jax.ShapeDtypeStruct((D,D),f32),jax.ShapeDtypeStruct((D,F),f32),jax.ShapeDtypeStruct((F,D),f32),jax.ShapeDtypeStruct((8,D),f32)],
        compiler_params=pltpu.CompilerParams(vmem_limit_bytes=60<<20))(a0,a1,tok,cot,wo,wu,wd,gs)
MESH=pl.DeviceIdType.MESH
class Net:
    def __init__(self,Z):
        dp=lax.axis_index("dp"); blk=lax.axis_index("blk")
        self.Z=Z; self.z=dp//2; self.y=dp%2; self.j=blk//2; self.c=blk%2
        self.sent=[]
    def at(self,z=None,y=None,j=None,c=None):
        z=self.z if z is None else z; y=self.y if y is None else y; j=self.j if j is None else j; c=self.c if c is None else c
        return (z*2+y,j*2+c)
    def signal(self):
        barrier=pltpu.get_barrier_semaphore()
        for d in [self.at(j=1-self.j),self.at(y=1-self.y),self.at(c=1-self.c)]+[self.at(z=lax.rem(self.z+k,self.Z)) for k in range(1,self.Z)]:
            pl.semaphore_signal(barrier,inc=1,device_id=d,device_id_type=MESH)
    def wait(self): pl.semaphore_wait(pltpu.get_barrier_semaphore(),2+self.Z)
    def greet(self):
        self.signal()
        self.wait()
    def copy(self,src,dst,ssem,rsem,device):
        return pltpu.make_async_remote_copy(src_ref=src,dst_ref=dst,send_sem=ssem,recv_sem=rsem,device_id=device,device_id_type=MESH)
    def send(self,src,dst,ssem,rsem,device,when=None):
        c=self.copy(src,dst,ssem,rsem,device)
        if when is None: c.start()
        else: pl.when(when)(c.start)
        self.sent.append((c,when))
    def drain(self):
        for c,when in self.sent:
            if when is None: c.wait_send()
            else: pl.when(when)(c.wait_send)

def gather_kernel(Z,block,E,W,rows,tok_hbm,cot_hbm,seg_ref,pad_ref,known_ref,wq_ref,wo_ref,wu_ref,wd_ref,gain_ref,shift_ref,
                  tok_out,bund_out,wmine_out,qkvt_out,base_out,win_out,code_out,meta_out,far_out,
                  tokb,farb,info_ref,infob,pack_ref,wall,bund,wt,qkvt,lsem,qsem,xs,xr,zs,zr,ys,yr,cs,cr,ts,tr,iss,isr):
    net=Net(Z); z,y,j,c=net.z,net.y,net.j,net.c
    NCH=block//rows; D=E
    sib=net.at(c=1-c); xd=net.at(j=1-j); yd=net.at(y=1-y)
    net.signal()
    mine=pltpu.make_async_copy(tok_hbm.at[j],tokb.at[j,c],lsem.at[0]); mine.start()
    far=pltpu.make_async_copy(cot_hbm.at[1-j],farb,lsem.at[3]); far.start()
    at=0
    for ref in (wq_ref,wo_ref,wu_ref,wd_ref):
        n=ref.shape[1]
        pack_ref[:,at:at+n]=ref[...]
        at+=n
    R=gain_ref.shape[1]
    place=(iota((R,128),1)==iota((R,128),0)+R*lax.rem(lax.axis_index("dp")*4+lax.axis_index("blk"),128//R)).astype(f32).astype(bf)
    pack_ref[:,at:]=jnp.concatenate([dot(gain_ref[...],place,1,0),dot(shift_ref[...],place,1,0),jnp.zeros((12,128),f32)],0).astype(bf)
    split=6*W
    wall[z,y,j,c]=pack_ref[:,:split]
    bund[y,j]=pack_ref[:,split:]
    info_ref[...]=seg_ref[...]*4+pad_ref[...]*2+known_ref[...]
    infob[j,c]=info_ref[j]
    net.wait()
    net.send(pack_ref.at[:,:split],wall.at[z,y,j,c],xs.at[0],xr.at[0],xd)
    net.send(pack_ref.at[:,split:],bund.at[y,j],xs.at[1],xr.at[1],xd)
    net.send(info_ref.at[1-j],infob.at[j,c],iss.at[0],isr.at[0],xd)
    net.send(info_ref.at[j],infob.at[j,c],iss.at[1],isr.at[1],sib)
    def chunk(k): return pl.ds(k*rows if type(k) is int else al(k*rows,rows),rows)
    for k in range(NCH):
        net.send(tok_hbm.at[1-j,chunk(k)],tokb.at[j,c,chunk(k)],ts.at[0,k],tr.at[0,k],xd)
        net.send(tok_hbm.at[j,chunk(k)],tokb.at[j,c,chunk(k)],ts.at[1,k],tr.at[1,k],sib)
    def piece(o,y_): return wall.at[o,y_,:,c]
    def landed(ref,sem): pltpu.make_async_copy(ref,ref,sem).wait()
    def pass_on(o):
        net.send(piece(o,y),piece(o,y),ys.at[o],yr.at[o],yd)
        net.send(piece(o,y),piece(o,y),cs.at[0,o],cr.at[0,o],sib)
    far.wait()
    far=pltpu.make_async_copy(farb,far_out,lsem.at[3]); far.start()
    landed(wall.at[z,y,1-j,c],xr.at[0])
    for k in range(1,Z):
        net.send(piece(z,y),piece(z,y),zs.at[k],zr.at[k],net.at(z=lax.rem(z+k,Z)))
    pass_on(z)
    landed(bund.at[y,1-j],xr.at[1])
    net.send(bund.at[y],bund.at[y],ys.at[Z],yr.at[Z],yd)
    for k in range(1,Z):
        o=lax.rem(z+Z-k,Z)
        landed(piece(o,y),zr.at[k])
        pass_on(o)
    for k in range(Z):
        o=lax.rem(z+Z-k,Z)
        landed(piece(o,1-y),yr.at[o])
        net.send(piece(o,1-y),piece(o,1-y),cs.at[1,o],cr.at[1,o],sib)
    for o in range(Z):
        for q in range(2): landed(wall.at[o,y if q==0 else 1-y,:,1-c],cr.at[q,o])
    landed(bund.at[1-y],yr.at[Z])
    outb=pltpu.make_async_copy(bund,bund_out,lsem.at[1]); outb.start()
    def qcopy(g):
        col=pl.ds(al(g*rows,rows),rows)
        return pltpu.make_async_copy(qkvt.at[:,col],qkvt_out.at[:,col],qsem.at[g])
    def project(jj,cc,come=None,onward=False):
        def body(k,carry):
            ref=tokb.at[jj,cc,chunk(k)]
            if come is not None: landed(ref,tr.at[come,k])
            if onward: net.copy(ref,ref,ts.at[2,k],tr.at[2,k],sib).start()
            g=(jj*2+cc)*NCH+k
            r=dot(wt[...],ref[...],1,1)
            qkvt[:,pl.ds(al(g*rows,rows),rows)]=jnp.concatenate([r[:W]*(math.log2(math.e)/8),r[W:]],0).astype(bf)
            qcopy(g).start()
            return carry
        lax.fori_loop(0,NCH,body,0)
    parts=[]
    for t in range(3):
        cols=pl.ds(al(t*2*W+c*W,W),W)
        part=wall[:,:,:,:,:,cols].reshape(D,W)
        wt[t*W:(t+1)*W,:]=part.T
        parts.append(part)
    wmine_out[...]=jnp.concatenate(parts,1)
    mine.wait()
    project(j,c)
    project(j,1-c,1)
    landed(infob.at[1-j,c],isr.at[0])
    net.send(infob.at[1-j,c],infob.at[1-j,c],iss.at[2],isr.at[2],sib)
    project(1-j,c,0,True)
    landed(infob.at[j,1-c],isr.at[1])
    landed(infob.at[1-j,1-c],isr.at[2])
    base_out[...],win_out[...],code_out[...],meta_out[...]=flags(jnp.concatenate([infob[0,0],infob[0,1],infob[1,0],infob[1,1]],1))
    project(1-j,1-c,2)
    outt=pltpu.make_async_copy(tokb,tok_out,lsem.at[2]); outt.start()
    net.drain()
    for k in range(NCH):
        ref=tokb.at[1-j,c,chunk(k)]
        net.copy(ref,ref,ts.at[2,k],tr.at[2,k],sib).wait_send()
    lax.fori_loop(0,4*NCH,lambda g,c:(qcopy(g).wait(),c)[1],0)
    outb.wait(); outt.wait(); far.wait()

def gather(tok,cot,seg,pad,known,wq,wo,wu,wd,gain,shift,Z,W):
    _,block,E=tok.shape; R=wq.shape[0]; C=6*W+wo.shape[1]+wu.shape[1]+wd.shape[1]+128
    rows=256; NCH=block//rows; L=4*block
    V=pl.BlockSpec(memory_space=pltpu.VMEM); A=pl.BlockSpec(memory_space=pl.ANY)
    S=jax.ShapeDtypeStruct; M=pltpu.VMEM; D=pltpu.SemaphoreType.DMA; I=jnp.int32
    return pl.pallas_call(functools.partial(gather_kernel,Z,block,E,W,rows),
        out_shape=[S((2,2,block,E),bf),S((2,2,R,C-6*W),bf),S((E,3*W),bf),S((3*W,L),bf),S((16,128),I),S((32,128),I),S((CODE,L),bf),S((8,L),I),S((block,E),bf)],
        in_specs=[A,A]+[V]*9,out_specs=[A,A,V,A,V,V,V,V,A],
        scratch_shapes=[M((2,2,block,E),bf),M((block,E),bf),M((2,1,block),I),M((2,2,1,block),I),M((R,C),bf),M((Z,2,2,2,R,6*W),bf),M((2,2,R,C-6*W),bf),M((3*W,E),bf),M((3*W,L),bf),
            D((4,)),D((4*NCH,)),D((2,)),D((2,)),D((Z,)),D((Z,)),D((Z+1,)),D((Z+1,)),D((2,Z)),D((2,Z)),D((3,NCH)),D((3,NCH)),D((3,)),D((3,))],
        compiler_params=pltpu.CompilerParams(collective_id=0,has_side_effects=True,vmem_limit_bytes=VMEM))(tok,cot,seg,pad,known,wq,wo,wu,wd,gain,shift)
def middle_net_kernel(Z,block,E,F,W,T,att_hbm,tok_hbm,cot_hbm,cotx_hbm,*rest):
    bunds=rest[:Z]; near_out,far_out,r1_out,datt_out=rest[Z:Z+4]; parts=rest[Z+4]
    (go_ref,gu_ref,gd_ref,gg_ref,gt_ref,aown,aget,tok,cot,wall,lay,r1,da,lsem,wsem,osem,asend,aget_sem,dsend,dget,bsend,bget)=rest[Z+5:]
    net=Net(Z); z,y,j,c=net.z,net.y,net.j,net.c
    NCH=block//T; n=2*NCH; P2=att_hbm.shape[0]; G=2
    sib=net.at(c=1-c)
    def place(t):
        jj=jnp.where(t<NCH,1-j,j)
        return jj,pl.ds(al(lax.rem(t,NCH)*T,T),T)
    def load(t):
        jj,rows=place(t)
        return [pltpu.make_async_copy(att_hbm.at[:,jj,c,rows],aown.at[t],lsem.at[0,t]),pltpu.make_async_copy(tok_hbm.at[jj,c,rows],tok.at[t],lsem.at[1,t])]
    def load_cot(t,near):
        rows=place(t)[1]
        return pltpu.make_async_copy((cot_hbm.at[j,rows] if near else cotx_hbm.at[rows]),cot.at[t],lsem.at[2,t])
    cols=[(0,E),(E,F),(E+F,E),(2*E+F,128)]
    loadw=[pltpu.make_async_copy(bunds[k],wall.at[lax.rem(z+Z-k,Z),:,:,c],wsem.at[k]) for k in range(Z)]
    for x in loadw: x.start()
    def start(t,near):
        for x in load(t): x.start()
        load_cot(t,near).start()
    for t in range(n): start(t,t>=NCH)
    barrier=pltpu.get_barrier_semaphore()
    pl.semaphore_signal(barrier,inc=1,device_id=sib,device_id_type=MESH)
    pl.semaphore_wait(barrier,1)
    def ship(t):
        jj,rows=place(t)
        return net.copy(att_hbm.at[:,jj,1-c,rows],aget.at[t],asend.at[t],aget_sem.at[t],sib)
    ship(0).start()
    weights=[net.copy(bunds[k],wall.at[lax.rem(z+Z-k,Z),:,:,c],bsend.at[k],bget.at[k],sib) for k in range(Z)]
    for x in weights: x.start()
    for t in range(1,n): ship(t).start()
    for x in loadw: x.wait()
    for k in range(Z):
        ref=wall.at[lax.rem(z+Z-k,Z),:,:,1-c]
        pltpu.make_async_copy(ref,ref,bget.at[k]).wait()
    def whole(a,b): return wall[:,:,:,:,:,a:a+b].reshape(E,b)
    gs=wall[:,:,:,:,:,cols[3][0]:].reshape(E//16,16,128).astype(f32)
    gsr=jnp.concatenate([jnp.sum(gs[q*8:(q+1)*8],0) for q in range(E//128)],1)
    g0,g1,b0,b1=[gsr[r:r+1,:] for r in range(4)]
    for r in (go_ref,gu_ref,gd_ref,gg_ref): r[...]=jnp.zeros_like(r)
    def out_near(t): return pltpu.make_async_copy(lay.at[t],near_out.at[place(t)[1]],osem.at[0,t])
    def out_far(t): return pltpu.make_async_copy(lay.at[t],far_out.at[place(t)[1]],osem.at[0,t])
    def out_r1(t):
        jj,rows=place(t)
        return pltpu.make_async_copy(r1.at[t],r1_out.at[jj,rows],osem.at[1,t])
    def out_da(t):
        jj,rows=place(t)
        return pltpu.make_async_copy(da.at[0,t],datt_out.at[:,jj,c,rows],osem.at[2,t])
    def ship_da(t):
        jj,rows=place(t)
        return net.copy(da.at[1,t],datt_out.at[:,jj,c,rows],dsend.at[t],dget.at[t],sib)
    def tiles(u,carry):
        ts=[G*u+g for g in range(G)]
        def each(f,*lists): return [f(*v) for v in zip(*lists)]
        for t in ts:
            for x in load(t): x.wait()
            pltpu.make_async_copy(cotx_hbm.at[place(t)[1]],cot.at[t],lsem.at[2,t]).wait()
            ship(t).wait_recv()
        def whole_att(t):
            mine=[aown[t,p] for p in range(P2)]; his=[aget[t,p] for p in range(P2)]
            return jnp.where(c==0,jnp.concatenate(mine+his,1),jnp.concatenate(his+mine,1))
        wo=whole(*cols[0]); wu=whole(*cols[1]); wd=whole(*cols[2])
        att=each(whole_att,ts)
        branch=each(lambda a:dot(a,wo,1,0),att)
        n1,inv1=zip(*each(lambda t,b:norm(tok[t].astype(f32)+b),ts,branch))
        first=each(lambda n:(n*g0+b0).astype(bf),n1)
        hidden=each(lambda a:dot(a,wu,1,0),first)
        cdf=each(lambda h:0.5*(1.0+erf(h*math.sqrt(0.5))),hidden)
        act=each(lambda h,p:(h*p).astype(bf),hidden,cdf)
        fed=each(lambda a:dot(a,wd,1,0),act)
        slope=each(lambda h,p:p+h*jnp.exp(-0.5*h*h)*(1.0/math.sqrt(2.0*math.pi)),hidden,cdf)
        n2,inv2=zip(*each(lambda a,b:norm(a.astype(f32)+b),first,fed))
        ct=each(lambda t:cot[t].astype(f32),ts)
        r2=each(lambda x,n,i:norm_back(x*g1,n,i),ct,n2,inv2)
        feed=each(lambda x:x.astype(bf),r2)
        dact=each(lambda x:dot(x,wd,1,1),feed)
        for t,n in zip(ts,n2): lay[t]=(n*g1+b1).astype(bf)
        both=lambda v:jnp.concatenate(v,0)
        gd_ref[...]+=dot(both(act),both(feed),0,0)
        dh=each(lambda x,s:(x*s).astype(bf),dact,slope)
        df=each(lambda x,h:x+dot(h,wu,1,1),r2,dh)
        gu_ref[...]+=dot(both(first),both(dh),0,0)
        dr=each(lambda x,n,i:norm_back(x*g0,n,i),df,n1,inv1)
        db=each(lambda x:x.astype(bf),dr)
        d=each(lambda x:dot(x,wo,1,1).astype(bf),db)
        go_ref[...]+=dot(both(att),both(db),0,0)
        for t,x,e in zip(ts,dr,d):
            r1[t]=x.astype(r1.dtype)
            for p in range(P2):
                lo=e[:,p*128:(p+1)*128]; hi=e[:,W+p*128:W+(p+1)*128]
                da[0,t,p]=jnp.where(c==0,lo,hi)
                da[1,t,p]=jnp.where(c==0,hi,lo)
        down=lambda v:sum(jnp.sum(x,0,keepdims=True) for x in v)
        gg_ref[0:1,:]+=down(each(lambda x,n:x*n,df,n1))
        gg_ref[1:2,:]+=down(each(lambda x,n:x*n,ct,n2))
        gg_ref[2:3,:]+=down(df)
        gg_ref[3:4,:]+=down(ct)
        for t in ts:
            @pl.when(t<NCH)
            def _(): out_far(t).start()
            @pl.when(t>=NCH)
            def _(): out_near(t).start()
            out_r1(t).start(); out_da(t).start(); ship_da(t).start()
        return carry
    lax.fori_loop(0,n//G,tiles,0)
    ggt=jnp.concatenate([gg_ref[...],jnp.zeros((120,E),f32)],0).T
    gt_ref[...]=ggt
    R=E//(2*Z)
    at=0
    for ref in (go_ref,gu_ref,gd_ref,gt_ref):
        parts[:,:,at:at+ref.shape[1]]=ref[...].astype(bf).reshape(2*Z,R,ref.shape[1])
        at+=ref.shape[1]
    for x in weights: x.wait_send()
    for t in range(n):
        ship(t).wait_send(); out_r1(t).wait(); out_da(t).wait(); ship_da(t).wait()
        (out_far if t<NCH else out_near)(t).wait()

def middle_net(att,tok,cot,cotx,bunds,Z,W,F):
    P2,_,_,block,_=att.shape; E=tok.shape[-1]; C=bunds[0].shape[-1]
    T=256; NCH=block//T; n=2*NCH
    V=pl.BlockSpec(memory_space=pltpu.VMEM); A=pl.BlockSpec(memory_space=pl.ANY)
    S=jax.ShapeDtypeStruct; M=pltpu.VMEM; D=pltpu.SemaphoreType.DMA
    return pl.pallas_call(functools.partial(middle_net_kernel,Z,block,E,F,W,T),
        out_shape=[S((block,E),bf),S((block,E),bf),S((2,block,E),f32),S((P2,2,2,block,128),bf)]+[S((2*Z,E//(2*Z),C),bf)],
        in_specs=[A]*(4+Z),out_specs=[A,A,A,A,V],
        scratch_shapes=[M((E,E),f32),M((E,F),f32),M((F,E),f32),M((8,E),f32),M((E,128),f32),
            M((n,P2,T,128),bf),M((n,P2,T,128),bf),M((n,T,E),bf),M((n,T,E),bf),M((Z,2,2,2,16,C),bf),M((n,T,E),bf),M((n,T,E),f32),M((2,n,P2,T,128),bf),
            D((3,n)),D((Z,)),D((3,n)),D((n,)),D((n,)),D((n,)),D((n,)),D((Z,)),D((Z,))],
        compiler_params=pltpu.CompilerParams(collective_id=2,has_side_effects=True,vmem_limit_bytes=VMEM))(att,tok,cot,cotx,*bunds)
def reduce_kernel(Z,block,E,W,C1,rows,base_ref,meta_ref,dq_hbm,dkvw_hbm,tok_hbm,w_hbm,r1_hbm,parts,tok_out,grad_out,
     dq,dkvw,tok,w,r1,own,tgf,tgr,tgs,ob,s0,r0,g0,s1,r1b,su,ru,fin,sx,rx,se,re,sxe,rxe,
     lsem,osem,ts,tr,xs,xr,cs,cr,ys,yr,us,ur,fs,fr):
    net=Net(Z); z,y,j,c=net.z,net.y,net.j,net.c
    NCH=block//rows; half=2*block
    sib=net.at(c=1-c); xd=net.at(j=1-j); yd=net.at(y=1-y)
    def side(jj): return pl.ds(al(jj*half,128),half)
    def spans(jj): return pl.ds(jj*2*NCH,2*NCH)
    loads=[pltpu.make_async_copy(a,b,lsem.at[k]) for k,(a,b) in enumerate(((dkvw_hbm.at[spans(1-j)],dkvw.at[spans(1-j)]),(dq_hbm.at[:,side(1-j)],dq.at[:,side(1-j)]),(w_hbm,w),(r1_hbm,r1),
        (dq_hbm.at[:,side(j)],dq.at[:,side(j)]),(tok_hbm,tok),(dkvw_hbm.at[spans(j)],dkvw.at[spans(j)])))]
    net.signal()
    for x in loads: x.start()
    def chunk(k): return pl.ds(k*rows,rows)
    def landed(ref,sem): pltpu.make_async_copy(ref,ref,sem).wait()
    def position(jj,cc,k): return pl.ds(al(((jj*2+cc)*NCH+k)*rows,rows),rows)
    def place(jj,cc,k):
        ssl=position(jj,cc,k)
        dq[W:3*W,ssl]=placed(base_ref,meta_ref[0:1,ssl],dkvw[(jj*2+cc)*NCH+k],dq[W:3*W,ssl],(jj*2+cc)*NCH+k).astype(bf)
    def to_tokens(jj,cc,k): return dot(dq[:,position(jj,cc,k)],w[...],0,1)
    def for_sibling(t):
        jj=1-j if t==0 else j
        for k in range(NCH):
            tgf[jj,chunk(k),:]=to_tokens(jj,1-c,k).astype(bf)
            net.send(tgf.at[jj,chunk(k)],tgr.at[jj,chunk(k)],ts.at[t,k],tr.at[t,k],sib)
    def split(x,n): return x.reshape(Z,2,2,2,16,n)
    def core_sum(v,lo,n):
        x=dot(dq[lo:lo+n,:],tok[...],1,0).T.astype(bf)
        x=split(x,n)
        s0[:,:,:,:,lo:lo+n]=jnp.where(c==0,x[:,:,:,1],x[:,:,:,0])
        net.send(s0.at[:,:,:,:,lo:lo+n],r0.at[:,:,:,:,lo:lo+n],cs.at[v],cr.at[v],sib)
        mine=jnp.where(c==0,x[:,:,:,0],x[:,:,:,1])
        for t in range(lo//W,(lo+n)//W):
            part=mine[:,:,:,:,t*W-lo:(t+1)*W-lo]
            @pl.when(c==0)
            def _(): g0[:,:,:,:,2*t*W:(2*t+1)*W]=part
            @pl.when(c==1)
            def _(): g0[:,:,:,:,(2*t+1)*W:(2*t+2)*W]=part
    def core_get(v,lo,n):
        landed(r0.at[:,:,:,:,lo:lo+n],cr.at[v])
        for t in range(lo//W,(lo+n)//W):
            part=r0[:,:,:,:,t*W:(t+1)*W]
            @pl.when(c==0)
            def _(): g0[:,:,:,:,(2*t+1)*W:(2*t+2)*W]=part
            @pl.when(c==1)
            def _(): g0[:,:,:,:,2*t*W:(2*t+1)*W]=part
    cut=[pl.ds(2*t*W,2*W) for t in range(3)]
    def to_y(v):
        s1[:,:,:,cut[v]]=jnp.where(y==0,g0[:,1,:,:,cut[v]],g0[:,0,:,:,cut[v]])
        net.send(s1.at[:,:,:,cut[v]],r1b.at[:,:,:,cut[v]],ys.at[v],yr.at[v],yd)
    def to_z(v):
        landed(r1b.at[:,:,:,cut[v]],yr.at[v])
        for k in range(1,Z):
            o=lax.rem(z+k,Z)
            su[k,:,:,cut[v]]=(g0[o,y,:,:,cut[v]].astype(f32)+r1b[o,:,:,cut[v]].astype(f32)).astype(bf)
            net.send(su.at[k,:,:,cut[v]],ru.at[k,:,:,cut[v]],us.at[v,k],ur.at[v,k],net.at(z=o))
    def to_x(v):
        sum_=g0[z,y,:,:,cut[v]].astype(f32)+r1b[z,:,:,cut[v]].astype(f32)
        for k in range(1,Z):
            landed(ru.at[k,:,:,cut[v]],ur.at[v,k])
            sum_=sum_+ru[k,:,:,cut[v]].astype(f32)
        fin[:,:,cut[v]]=sum_
        sx[:,cut[v]]=jnp.where(j==0,sum_[1],sum_[0]).astype(bf)
        net.send(sx.at[:,cut[v]],rx.at[:,cut[v]],fs.at[v],fr.at[v],xd)
    for x in loads[:3]: x.wait()
    for k in range(NCH): place(1-j,1-c,k)
    net.wait()
    for_sibling(0)
    for k in range(NCH): place(1-j,c,k)
    for k in range(NCH): own[1-j,chunk(k),:]=to_tokens(1-j,c,k)
    loads[3].wait()
    def total(jj,k): return (own[jj,chunk(k),:]+tgr[jj,chunk(k),:].astype(f32)+r1[jj,chunk(k),:]).astype(bf)
    for k in range(NCH):
        landed(tgr.at[1-j,chunk(k)],tr.at[0,k])
        tgs[chunk(k),:]=total(1-j,k)
        net.send(tgs.at[chunk(k)],ob.at[j,chunk(k)],xs.at[k],xr.at[k],xd)
    for x in loads[4:]: x.wait()
    core_sum(0,0,W)
    for cc in (1-c,c):
        for k in range(NCH): place(j,cc,k)
    core_get(0,0,W)
    to_y(0)
    core_sum(1,W,W)
    core_sum(2,2*W,W)
    core_get(1,W,W)
    to_y(1)
    early=parts[0].astype(f32)
    for k in range(1,2*Z): early=early+parts[k].astype(f32)
    early=early.reshape(2,2,16,C1)
    early0=jnp.where(c==0,early[:,0],early[:,1])
    se[...]=jnp.where(c==0,early[:,1],early[:,0]).astype(bf)
    net.send(se,re,cs.at[3],cr.at[3],sib)
    core_get(2,2*W,W)
    to_y(2)
    to_z(0)
    for_sibling(1)
    to_z(1)
    landed(re,cr.at[3])
    early0=early0+re[...].astype(f32)
    early1=jnp.where(j==0,early0[0],early0[1])
    sxe[...]=jnp.where(j==0,early0[1],early0[0]).astype(bf)
    net.send(sxe,rxe,fs.at[3],fr.at[3],xd)
    to_x(0)
    for k in range(NCH): own[j,chunk(k),:]=to_tokens(j,c,k)
    to_z(2)
    to_x(1)
    for k in range(NCH):
        landed(tgr.at[j,chunk(k)],tr.at[1,k])
        ob[j,chunk(k),:]=total(j,k)
    near=pltpu.make_async_copy(ob.at[j],tok_out.at[j],osem.at[0]); near.start()
    to_x(2)
    landed(rxe,fr.at[3])
    grad_out[:,6*W:]=early1+rxe[...].astype(f32)
    for v in range(3):
        landed(rx.at[:,cut[v]],fr.at[v])
        grad_out[:,cut[v]]=jnp.where(j==0,fin[0,:,cut[v]],fin[1,:,cut[v]])+rx[:,cut[v]].astype(f32)
    for k in range(NCH): landed(ob.at[1-j,chunk(k)],xr.at[k])
    last=pltpu.make_async_copy(ob.at[1-j],tok_out.at[1-j],osem.at[1]); last.start()
    net.drain()
    near.wait(); last.wait()

def reduce(base,meta,dq,dkvw,tok,w,r1,parts,Z,W):
    _,block,E=r1.shape; L=4*block; C1=parts.shape[2]; C=6*W
    rows=256; NCH=block//rows
    V=pl.BlockSpec(memory_space=pltpu.VMEM); A=pl.BlockSpec(memory_space=pl.ANY)
    S=jax.ShapeDtypeStruct; M=pltpu.VMEM; D=pltpu.SemaphoreType.DMA
    return pl.pallas_call(functools.partial(reduce_kernel,Z,block,E,W,C1,rows),
        out_shape=[S((2,block,E),bf),S((16,C+C1),f32)],
        in_specs=[pl.BlockSpec(memory_space=pltpu.SMEM),V,A,A,A,A,A,V],out_specs=[A,V],
        scratch_shapes=[M(dq.shape,bf),M(dkvw.shape,bf),M(tok.shape,bf),M(w.shape,bf),M(r1.shape,f32),M((2,block,E),f32),M((2,block,E),bf),M((2,block,E),bf),M((block,E),bf),M((2,block,E),bf),
            M((Z,2,2,16,3*W),bf),M((Z,2,2,16,3*W),bf),M((Z,2,2,16,C),bf),M((Z,2,16,C),bf),M((Z,2,16,C),bf),
            M((Z,2,16,C),bf),M((Z,2,16,C),bf),M((2,16,C),f32),M((16,C),bf),M((16,C),bf),M((2,16,C1),bf),M((2,16,C1),bf),M((16,C1),bf),M((16,C1),bf),
            D((7,)),D((2,)),D((2,NCH)),D((2,NCH)),D((NCH,)),D((NCH,)),D((4,)),D((4,)),D((3,)),D((3,)),D((3,Z)),D((3,Z)),D((4,)),D((4,))],
        compiler_params=pltpu.CompilerParams(collective_id=1,has_side_effects=True,vmem_limit_bytes=VMEM))(base,meta,dq,dkvw,tok,w,r1,parts)

def finish_kernel(W,near,far,tg_hbm,grads,lay_out,tg_out,gq,go,gu,gd,gg,gs,lay,tg,sem):
    j=lax.axis_index("blk")//2
    come=[pltpu.make_async_copy(a,b,sem.at[k]) for k,(a,b) in enumerate(((near,lay.at[j]),(far,lay.at[1-j]),(tg_hbm.at[0],tg.at[0]),(tg_hbm.at[1],tg.at[1])))]
    go_out=[pltpu.make_async_copy(a,b,sem.at[4+k]) for k,(a,b) in enumerate(((lay.at[j],lay_out.at[j]),(lay.at[1-j],lay_out.at[1-j]),(tg.at[0],tg_out.at[0]),(tg.at[1],tg_out.at[1])))]
    for x in come: x.start()
    at=0
    for ref in (gq,go,gu,gd):
        n=ref.shape[1]
        ref[...]=grads[:,at:at+n]
        at+=n
    t=grads[:,at:].T
    gg[...]=t[0:2,:]
    gs[...]=t[2:4,:]
    for x,o in zip(come,go_out):
        x.wait(); o.start()
    for o in go_out: o.wait()

def finish(near,far,tg,grads,W,F):
    _,block,E=tg.shape
    V=pl.BlockSpec(memory_space=pltpu.VMEM); A=pl.BlockSpec(memory_space=pl.ANY); S=jax.ShapeDtypeStruct
    return pl.pallas_call(functools.partial(finish_kernel,W),
        out_shape=[S(tg.shape,bf),S(tg.shape,bf),S((16,6*W),f32),S((16,E),f32),S((16,F),f32),S((16,E),f32),S((2,16),f32),S((2,16),f32)],
        in_specs=[A,A,A,V],out_specs=[A,A]+[V]*6,scratch_shapes=[pltpu.VMEM(tg.shape,bf),pltpu.VMEM(tg.shape,bf),pltpu.SemaphoreType.DMA((8,))],
        compiler_params=pltpu.CompilerParams(vmem_limit_bytes=VMEM))(near,far,tg,grads)
def shards(tokens,cotangent,segments,padding,known,w_qkv,w_out,w_up,w_down,norm_gains,norm_shifts):
    micro,rows,block,D=tokens.shape
    J=lax.axis_size("blk")//2; dps=lax.axis_size("dp")
    units=micro*rows
    assert units==J
    H=HEADS//2; W=H*HEAD; L=2*J*block; F=w_up.shape[1]
    quick=J==2 and dps%2==0 and w_qkv.shape[0]==16 and block%256==0
    me=lax.axis_index("blk"); chip=me//2; core=me%2
    flat=lambda x:x.reshape((units,)+x.shape[2:])
    if quick:
        Z=dps//2
        cot=flat(cotangent)
        tok,bund,w_mine,qkvt,base,win,codet,meta,far=gather(flat(tokens),cot,*[flat(x)[:,None,:] for x in (segments,padding,known)],w_qkv,w_out,w_up,w_down,norm_gains,norm_shifts,Z,W)
        bunds=[bund]+[lax.ppermute(bund,"dp",[(d,(d//2+k)%Z*2+d%2) for d in range(dps)]) for k in range(1,Z)]
        across=[(b,b^2) for b in range(4)]
        cotx=lax.ppermute(far,"blk",across)
        p,att,ot,inv,kct,vaug=attend(base,win,qkvt,codet,meta,H)
        near,far,r1,datt,parts=middle_net(att.reshape(H//2,2,2,block,128),tok,cot,cotx,bunds,Z,W,F)
        parts=lax.all_to_all(parts,"dp",0,0,tiled=True)
        layx=lax.ppermute(far,"blk",across)
        dq,dkvw=back(base,win,datt.reshape(H//2,L,128),p,ot,inv,kct,vaug,qkvt,H)
        tg,grads=reduce(base,meta,dq,dkvw,tok.reshape(L,D),w_mine,r1,parts,Z,W)
        out=finish(near,layx,tg,grads,W,F)
        return (out[0].reshape(tokens.shape),out[1].reshape(tokens.shape))+tuple(out[2:])
    def to_chip(s): return [(2*a+c,2*((a+s)%J)+c) for a in range(J) for c in range(2)]
    swap=[(b,b^1) for b in range(2*J)]
    def other(x): return lax.ppermute(x,"blk",swap)
    def scatter_units(x):
        got=[]
        for s in range(J):
            mine=lax.dynamic_index_in_dim(x,(chip+s)%J,0,keepdims=False)
            got.append(mine if s==0 else lax.ppermute(mine,"blk",to_chip(s)))
        return jnp.stack([lax.dynamic_index_in_dim(jnp.stack(got),(chip-j)%J,0,keepdims=False) for j in range(J)])
    def both(mine,his):
        return jnp.stack([jnp.where(core==0,mine,his),jnp.where(core==0,his,mine)],1)
    def part(x,axis,index): return lax.dynamic_index_in_dim(x,index,axis,keepdims=False)
    own_info=scatter_units(flat(segments*4+padding*2+known)); info=both(own_info,other(own_info)).reshape(1,L)
    own_tok=scatter_units(flat(tokens)); all_tok=both(own_tok,other(own_tok)).reshape(L,D)
    own_cot=scatter_units(flat(cotangent)).reshape(L//2,D)
    full_qkv,full_out,full_up,full_down=[lax.all_gather(w,("dp","blk"),axis=0,tiled=True) for w in (w_qkv,w_out,w_up,w_down)]
    gs=lax.all_gather(jnp.concatenate([norm_gains,norm_shifts],0),("dp","blk"),axis=1,tiled=True).astype(f32)
    gs=jnp.concatenate([gs,jnp.zeros_like(gs)],0)
    w_mine=part(full_qkv.reshape(D,3,2,W),2,core).reshape(D,3*W)
    scale=jnp.where(jnp.arange(3*W)<W,math.log2(math.e)/8,1.0).astype(f32)
    qkvt=(jnp.einsum("ld,de->el",all_tok,w_mine,preferred_element_type=f32)*scale[:,None]).astype(bf)
    base,win,codet,meta=flags(info)
    p,att,ot,inv,kct,vaug=attend(base,win,qkvt,codet,meta,H)
    att=att.reshape(H//2,J,2,block,128)
    mine=part(att,2,core).reshape(H//2,J*block,128); his=other(part(att,2,1-core)).reshape(H//2,J*block,128)
    a0=jnp.where(core==0,mine,his); a1=jnp.where(core==0,his,mine)
    out,r1,da,go,gu,gd,gg=middle(a0,a1,own_tok.reshape(L//2,D),own_cot,full_out,full_up,full_down,gs)
    da=da.reshape(2,H//2,J,block,128)
    dmine=part(da,0,core); dhis=other(part(da,0,1-core))
    datt=jnp.stack([jnp.where(core==0,dmine,dhis),jnp.where(core==0,dhis,dmine)],2).reshape(H//2,L,128)
    dq,dkvw=back(base,win,datt,p,ot,inv,kct,vaug,qkvt,H)
    tg,gq=place_all(base,meta,dq,dkvw,all_tok,w_mine,H)
    tg=tg.reshape(J,2,block,D)
    layer_out=scatter_units(out.reshape(J,block,D)).reshape(tokens.shape)
    own_tg=(part(tg,1,core).astype(f32)+other(part(tg,1,1-core)).astype(f32)+r1.reshape(J,block,D)).astype(bf)
    token_grad=scatter_units(own_tg).reshape(tokens.shape)
    gq=gq.astype(f32).reshape(D,3,1,W)
    gq=jnp.where(core==0,jnp.concatenate([gq,jnp.zeros_like(gq)],2),jnp.concatenate([jnp.zeros_like(gq),gq],2)).reshape(D,6*W)
    grads=lax.psum_scatter(jnp.concatenate([gq,go,gu,gd],1),("dp","blk"),scatter_dimension=0,tiled=True)
    gg=lax.psum_scatter(gg[:4],("dp","blk"),scatter_dimension=1,tiled=True)
    a,b,e=6*W,6*W+D,6*W+D+F
    return (layer_out,token_grad,grads[:,:a],grads[:,a:b],grads[:,b:e],grads[:,e:],gg[:2],gg[2:])

def solution(mesh):
    in_specs = (
        P(None, "dp", "blk", None),
        P(None, "dp", "blk", None),
        P(None, "dp", "blk"),
        P(None, "dp", "blk"),
        P(None, "dp", "blk"),
        P(("dp", "blk"), None),
        P(("dp", "blk"), None),
        P(("dp", "blk"), None),
        P(("dp", "blk"), None),
        P(None, ("dp", "blk")),
        P(None, ("dp", "blk")),
    )
    out_specs = (
        P(None, "dp", "blk", None),
        P(None, "dp", "blk", None),
        P(("dp", "blk"), None),
        P(("dp", "blk"), None),
        P(("dp", "blk"), None),
        P(("dp", "blk"), None),
        P(None, ("dp", "blk")),
        P(None, ("dp", "blk")),
    )
    return jax.shard_map(shards, mesh=mesh, in_specs=in_specs, out_specs=out_specs, check_vma=False)
```

time: 343 us -> 315 us (0.918)
  starting transfers between devices: 148 us -> 27.9 us
  Pallas kernels: 183 us -> 286 us
  local copies, waits for them, and re-layouts: 8.93 us -> 0 us
    all_to_all x1, starting transfers between devices: 143 us -> 23.3 us  [shards(): parts = lax.all_to_all(parts, 'dp', 0, 0, tiled=True)]
    pallas_call x1, Pallas kernels: 31.7 us -> 151 us  [attend(): pl.pallas_call(functools.partial(attend_kernel, L, H), out_shape=[S((cap,...]
    pallas_call x2 -> x3, Pallas kernels: 92.3 us -> 82.8 us  [the longest x1 44 us: back(): pl.pallas_call(functools.partial(back_kernel, L, H), out_shape=[S((3 * W,...]
    pallas_call x1, Pallas kernels: 25.6 us -> 20.2 us  [middle_net(): pl.pallas_call(functools.partial(middle_net_kernel, Z, block, E, F, W, T)...]
    unnamed x6 -> x0, local copies, waits for them, and re-layouts: 5.07 us -> none
  transfers between devices with their start and end apart: 5 -> 6, of which waited for: 0 -> 0; matrix products, arithmetic and copies ran while one was open for 0% -> 0% of each run, Pallas kernels for 27% -> 73%
where the time goes in v3:
time: 315 us
  Pallas kernels  286 us (91%)
  starting transfers between devices  27.9 us (9%)
    pallas_call x1, Pallas kernels, attend(): pl.pallas_call(functools.partial(attend_kernel, L, H), out_shape=[S((cap,...  151 us
    pallas_call x1, Pallas kernels, back(): pl.pallas_call(functools.partial(back_kernel, L, H), out_shape=[S((3 * W,...  44 us
    pallas_call x1, Pallas kernels, reduce(): pl.pallas_call(functools.partial(reduce_kernel, Z, block, E, W, C1, rows)...  34.4 us
    pallas_call x1, Pallas kernels, gather(): pl.pallas_call(functools.partial(gather_kernel, Z, block, E, W, rows), ou...  32.4 us
    all_to_all x1, starting transfers between devices, shards(): parts = lax.all_to_all(parts, 'dp', 0, 0, tiled=True)  23.3 us
    pallas_call x1, Pallas kernels, middle_net(): pl.pallas_call(functools.partial(middle_net_kernel, Z, block, E, F, W, T)...  20.2 us
  transfers between devices with their start and end apart: 6, of which 0 were waited for; matrix products, arithmetic and copies ran while one was open for 0% of the time, Pallas kernels for 73%

profile of v3, /device:TPU:0, one launch (start us, length us, event | category | flops | bytes accessed | tf_op | source)
XLA Modules:
  0.0 315.3 jit_solution(10640178777549776409)
XLA Ops:
  0.6 32.4 %shard_map.170 = (bf16[2,2,768,512]{3,2,1,0:T(8,128)(2,1)}, bf16[2,2,16,1664]{3,2,1,0:T(8,128)(2,1)}, bf16[512,768]{1,0:T(8,128)(2,1)}, bf16[768,3072]{1,0:T(8,1...) custom-call(bf16[2,768,512]{2,1,0:T(8,128)(2,1)} %bitcast.14, ...), custom_call_target="tpu_custom_call" | custom-call | tf_op jit(solution)/shard_map/pallas_call | solution.py:520
  33.0 0.7 collective-permute-start
  33.7 2.8 collective-permute-start.3
  36.6 0.0 collective-permute-start.2
  36.6 1.1 collective-permute-start.1
  37.6 150.9 %shard_map.171 = (bf16[42,4,512,512]{3,2,1,0:T(8,128)(2,1)}, bf16[2,3072,128]{2,1,0:T(8,128)(2,1)}, f32[6,256,512]{2,1,0:T(8,128)}, f32[4,8,3072]{2,1,0:T(8,128)...) custom-call(s32[16,128]{1,0:T(8,128)} %get-tuple-element.40.base_ref, ...), custom_call_target="tpu_custom_call" | custom-call | tf_op jit(solution)/shard_map/pallas_call | solution.py:164
  188.6 0.0 collective-permute-done.3.rest_3_
  188.6 0.0 collective-permute-done.2.rest_2_
  188.6 0.0 collective-permute-done.1.rest_1_
  188.6 0.0 collective-permute-done.cotx_hbm
  188.6 20.2 %shard_map.172 = (bf16[768,512]{1,0:T(8,128)(2,1)}, bf16[768,512]{1,0:T(8,128)(2,1)}, f32[2,768,512]{2,1,0:T(8,128)}, bf16[2,2,2,768,128]{4,3,2,1,0:T(8,128)(2,1)}, bf16[8,64,1664]{2,1,0:T(8,128)(2,1)}) custom-call(bf16[2,2,2,768,128]{4,3,2,1,0:T(8,128)(2,1)} %bitcast.15, bf16[2,2,768,512]{3,2,1,0:T(8,128)(2,1)} %get-tuple-element.46.tok_hbm, ...), custom_call_target="tpu_custom_call" | custom-call | tf_op jit(solution)/shard_map/pallas_call | solution.py:649
  208.9 23.3 %all-to-all-start = ((bf16[8,64,1664]{2,1,0:T(8,128)(2,1)}), bf16[8,64,1664]{2,1,0:T(8,128)(2,1)}, u32[]{:S(2)}, u32[]{:S(2)}) async-start(bf16[8,64,1664]{2,1,0:T(8,128)(2,1)} %get-tuple-element.61), calls=%async_computation | async-start | bytes 3407872 | tf_op jit(solution)/shard_map/all_to_all | solution.py:832
  232.2 0.0 collective-permute-start.4
  232.2 44.0 %shard_map.173 = (bf16[768,3072]{1,0:T(8,128)(2,1)}, bf16[12,512,384]{2,1,0:T(8,128)(2,1)}) custom-call(s32[16,128]{1,0:T(8,128)} %get-tuple-element.40.base_ref, s32[32,128]{1,0:T(8,128)} %get-tuple-element.41.win_ref, bf16[2,3072,128]{2,1,0:T(8,128)(2,1)} %bitcast.16, bf16[42,4,512,512]{3,2,1,0:T(8,128)(2,1)} %get-tuple-element.52.p_hbm, ...), custom_call_target="tpu_custom_call" | custom-call | tf_op jit(solution)/shard_map/pallas_call | solution.py:301
  276.2 0.0 all-to-all-done.parts
  276.2 34.4 %shard_map.174 = (bf16[2,768,512]{2,1,0:T(8,128)(2,1)}, f32[16,3200]{1,0:T(8,128)}) custom-call(s32[16,128]{1,0:T(8,128)} %get-tuple-element.40.base_ref, s32[8,3072]{1,0:T(8,128)} %get-tuple-element.44.meta_ref, bf16[768,3072]{1,0:T(8,128)(2,1)} %get-tuple-element.57.dq_hbm, bf16[12,512,384]{2,1,0:T(8,128)(2,1)} %get-tuple-element.58.dkvw_hbm, ...), custom_call_target="tpu_custom_call" | custom-call | tf_op jit(solution)/shard_map/pallas_call | solution.py:781
  310.6 0.0 collective-permute-done.4.far
  310.6 4.5 %shard_map.175 = (bf16[2,768,512]{2,1,0:T(8,128)(2,1)}, bf16[2,768,512]{2,1,0:T(8,128)(2,1)}, f32[16,1536]{1,0:T(8,128)}, f32[16,512]{1,0:T(8,128)}, f32[16,512]...) custom-call(bf16[768,512]{1,0:T(8,128)(2,1)} %get-tuple-element.49.near, ...), custom_call_target="tpu_custom_call" | custom-call | tf_op jit(solution)/shard_map/pallas_call | solution.py:810
Async XLA Ops:
  33.0 155.6 %collective-permute-start = (bf16[768,512]{1,0:T(8,128)(2,1)}, bf16[768,512]{1,0:T(8,128)(2,1)}, u32[]{:S(2)}, u32[]{:S(2)}) collective-permute-start(bf16[768,512]{1,0:T(8,128)(2,1)} %get-tuple-element.47), channel_id=1, source_target_pairs={{0,2},{1,3},{2,0},{3,1},{4,6},{5,7},{6,4},{7,5},{8,10},{9,11},{10,... | collective-permute-start | bytes 2359304 | tf_op jit(solution)/shard_map/ppermute | solution.py:829
  33.7 154.8 %collective-permute-start.3 = (bf16[2,2,16,1664]{3,2,1,0:T(8,128)(2,1)}, bf16[2,2,16,1664]{3,2,1,0:T(8,128)(2,1)}, u32[]{:S(2)}, u32[]{:S(2)}) collective-permute-start(bf16[2,2,16,1664]{3,2,1,0:T(8,128)(2,1)} %get-tuple-element.48.rest_0_), channel_id=1, source_target_pairs={{0,24},{4,28},{8,0},{12,4},{16,8},{20,12},{24,16},{28,20},{1,25},{... | collective-permute-start | bytes 638984 | tf_op jit(solution)/shard_map/ppermute | solution.py:827
  36.6 152.0 %collective-permute-start.2 = (bf16[2,2,16,1664]{3,2,1,0:T(8,128)(2,1)}, bf16[2,2,16,1664]{3,2,1,0:T(8,128)(2,1)}, u32[]{:S(2)}, u32[]{:S(2)}) collective-permute-start(bf16[2,2,16,1664]{3,2,1,0:T(8,128)(2,1)} %get-tuple-element.48.rest_0_), channel_id=1, source_target_pairs={{0,16},{4,20},{8,24},{12,28},{16,0},{20,4},{24,8},{28,12},{1,17},{... | collective-permute-start | bytes 638984 | tf_op jit(solution)/shard_map/ppermute | solution.py:827
  36.6 152.0 %collective-permute-start.1 = (bf16[2,2,16,1664]{3,2,1,0:T(8,128)(2,1)}, bf16[2,2,16,1664]{3,2,1,0:T(8,128)(2,1)}, u32[]{:S(2)}, u32[]{:S(2)}) collective-permute-start(bf16[2,2,16,1664]{3,2,1,0:T(8,128)(2,1)} %get-tuple-element.48.rest_0_), channel_id=1, source_target_pairs={{0,8},{4,12},{8,16},{12,20},{16,24},{20,28},{24,0},{28,4},{1,9},{5... | collective-permute-start | bytes 638984 | tf_op jit(solution)/shard_map/ppermute | solution.py:827
  208.9 67.4 %all-to-all-start = ((bf16[8,64,1664]{2,1,0:T(8,128)(2,1)}), bf16[8,64,1664]{2,1,0:T(8,128)(2,1)}, u32[]{:S(2)}, u32[]{:S(2)}) async-start(bf16[8,64,1664]{2,1,0:T(8,128)(2,1)} %get-tuple-element.61), calls=%async_computation | async-start | bytes 3407872 | tf_op jit(solution)/shard_map/all_to_all | solution.py:832
  232.2 78.4 %collective-permute-start.4 = (bf16[768,512]{1,0:T(8,128)(2,1)}, bf16[768,512]{1,0:T(8,128)(2,1)}, u32[]{:S(2)}, u32[]{:S(2)}) collective-permute-start(bf16[768,512]{1,0:T(8,128)(2,1)} %get-tuple-element.50), channel_id=1, source_target_pairs={{0,2},{1,3},{2,0},{3,1},{4,6},{5,7},{6,4},{7,5},{8,10},{9,11},{10,... | collective-permute-start | bytes 2359304 | tf_op jit(solution)/shard_map/ppermute | solution.py:833

commit v4 on v3

--- a/solution.py
+++ b/solution.py
@@ -146,7 +146,7 @@
             obuf[slot,h*HEAD:(h+1)*HEAD,:]=(acc[h,:HEAD,:]+ps*v_ref[h*HEAD:(h+1)*HEAD,qsl].astype(f32))*inv
             inv_ref[h,0:1,qsl]=inv
             inv_ref[h,1:2,qsl]=ps
-        for hp in range(H//2): abuf[slot,hp]=obuf[slot,hp*128:(hp+1)*128,:].T.astype(bf)
+        for hp in range(H//2): abuf[slot,hp]=obuf[slot,hp*128:(hp+1)*128,:].astype(bf).T
         ocopy(i).start(); acopy(i).start()
         return g
     g=lax.fori_loop(0,nq,block,0)
@@ -211,13 +211,13 @@
     def queries(i):
         slot=lax.rem(i,2); qsl=pl.ds(al(i*QB,QB),QB)
         return [pltpu.make_async_copy(a,b.at[slot],qsem.at[k,slot]) for k,(a,b) in enumerate(((qkvt_hbm.at[:,qsl],qkv),(datt_hbm.at[:,qsl],datt),(ot_hbm.at[i],ot)))]
-    def each_key(fn):
+    def each_key(fn,least=0):
         def body(t,c):
             for x in keys(t): fn(x)
             return c
-        lax.fori_loop(0,(groups+KB//128-1)//(KB//128),body,0)
+        lax.fori_loop(least,(groups+KB//128-1)//(KB//128),body,0)
+    for x in queries(0): x.start()
     each_key(lambda x:x.start())
-    for x in queries(0): x.start()
     for s in range(SLOTS-1):
         @pl.when(s<pieces)
         def _(): pcopy(s).start()
@@ -225,7 +225,6 @@
         dkv[pl.ds(al(j*128,128),128),:]=jnp.zeros((128,2*W),f32)
         return c
     lax.fori_loop(0,groups,clear,0)
-    each_key(lambda x:x.wait())
     def ocopy(i):
         slot=lax.rem(i,2)
         return pltpu.make_async_copy(dq.at[slot],dq_hbm.at[:,pl.ds(al(i*QB,QB),QB)],osem.at[slot])
@@ -237,7 +236,7 @@
         @pl.when(i+1<nq)
         def _():
             for x in queries(i+1): x.start()
-        dt=jnp.concatenate([datt[slot,hp].astype(f32).T for hp in range(H//2)],0)
+        dt=datt[slot].astype(f32)
         prod=dt*ot[slot]
         daug=[];dz=[];qz=[];deltas=[];d1s=[]
         zero=jnp.zeros((HEAD,QB),bf)
@@ -256,20 +255,26 @@
             qz.append(jnp.concatenate([zero,q] if h%2 else [q,zero],0))
             deltas.append(delta); d1s.append(d1)
         qacc[...]=jnp.zeros_like(qacc)
+        def wide(v): return jnp.concatenate(v,1)
         def piece(off,size,g):
             ps=lax.rem(g,SLOTS)
             osl=pl.ds(off,size)
             @pl.when(g+SLOTS-1<pieces)
             def _(): pcopy(g+SLOTS-1).start()
+            @pl.when(i==0)
+            def _():
+                for x in keys(g): x.wait()
             pcopy(g).wait()
             dss=[]
             for h in range(H):
                 dss.append((pbuf[ps,h,:size,:].astype(f32)*dot(vaug_ref[h,osl,:],daug[h],1,0)).astype(bf))
             for h in range(H): qacc[h*HEAD:(h+1)*HEAD,:]+=dot(kct[h,:,osl],dss[h],1,0)
             for h in range(0,H,2):
-                dkv[osl,h*HEAD:(h+2)*HEAD]+=dot(dss[h],qz[h],1,1)+dot(dss[h+1],qz[h+1],1,1)
-                dkv[osl,W+h*HEAD:W+(h+2)*HEAD]+=dot(pbuf[ps,h,:size,:],dz[h],1,1)+dot(pbuf[ps,h+1,:size,:],dz[h+1],1,1)
+                dkv[osl,h*HEAD:(h+2)*HEAD]+=dot(wide(dss[h:h+2]),wide(qz[h:h+2]),1,1)
+                dkv[osl,W+h*HEAD:W+(h+2)*HEAD]+=dot(wide([pbuf[ps,h,:size,:],pbuf[ps,h+1,:size,:]]),wide(dz[h:h+2]),1,1)
         g=by_piece(first,full,rest,g,piece)
+        @pl.when(i==0)
+        def _(): each_key(lambda x:x.wait(),g)
         @pl.when(i>=2)
         def _(): ocopy(i-2).wait()
         for h in range(H):
@@ -283,14 +288,16 @@
         return g
     lax.fori_loop(0,nq,block,0)
     lanes=iota((128,2*W),1)
+    def tcopy(s): return pltpu.make_async_copy(dkvt.at[:,pl.ds(al(begin(base_ref,s)//128*128,128),SPAN)],dkvw_hbm.at[s],tsem.at[s])
     def turn(j,c):
         jsl=pl.ds(al(j*128,128),128)
         x=jnp.where(j<groups,dkv[jsl,:],0.0)
         dkvt[:,jsl]=jnp.where(lanes<W,x*LN2,x).astype(bf).T
+        for s in range(L//256):
+            @pl.when(begin(base_ref,s)//128+SPAN//128-1==j)
+            def _(): tcopy(s).start()
         return c
-    lax.fori_loop(0,groups+3,turn,0)
-    def tcopy(s): return pltpu.make_async_copy(dkvt.at[:,pl.ds(al(begin(base_ref,s)//128*128,128),SPAN)],dkvw_hbm.at[s],tsem.at[s])
-    for s in range(L//256): tcopy(s).start()
+    lax.fori_loop(0,groups+SPAN//128,turn,0)
     for i in range(max(nq-2,0),nq): ocopy(i).wait()
     for s in range(L//256): tcopy(s).wait()
 
@@ -303,7 +310,7 @@
         in_specs=[N,N,A,A,A,V,A,A,A],
         out_specs=[A,A],
         scratch_shapes=[M((H,L,128),bf),M((H,HEAD,L),bf),M((L+384,2*W),f32),M((2*W,L+384),bf),M((SLOTS,H,KB,QB),bf),M((W,QB),f32),
-            M((2,3*W,QB),bf),M((2,H//2,QB,128),bf),M((2,W,QB),f32),M((2,3*W,QB),bf),
+            M((2,3*W,QB),bf),M((2,W,QB),bf),M((2,W,QB),f32),M((2,3*W,QB),bf),
             D((SLOTS,)),D((2,L//KB)),D((3,2)),D((2,)),D((L//256,))],
         compiler_params=pltpu.CompilerParams(vmem_limit_bytes=VMEM))(base,win,datt,p,ot,inv,kct,vaug,qkvt)
 
@@ -329,14 +336,14 @@
         in_specs=[pl.BlockSpec(memory_space=pltpu.SMEM)]+[V]*5,out_specs=[V,V],scratch_shapes=[pltpu.VMEM((3*W,L),bf)],
         compiler_params=pltpu.CompilerParams(vmem_limit_bytes=VMEM))(base,meta,dq,dkvw,tok,w)
 EPSILON=1e-05
-def erf(x):
-    x=jnp.clip(x,-3.832506856900711,3.832506856900711)
-    x2=x*x
-    top=0.00022905065861350646
-    for c in (0.0034082910107109506,0.050955695062380861,0.18520832239976145,1.128379143519084): top=top*x2+c
-    low=-1.1791602954361697e-7
-    for c in (0.000023547966471313185,0.0010179625278914885,0.014070470171167667,0.11098505178285362,0.49746925110067538,1.0): low=low*x2+c
-    return x*top/low
+def gelu_parts(h):
+    bell=jnp.exp(-0.5*h*h)
+    t=1.0/(1.0+(0.3275911*math.sqrt(0.5))*jnp.abs(h))
+    tail=0.5*1.061405429
+    for c in (-1.453152027,1.421413741,-0.284496736,0.254829592): tail=tail*t+0.5*c
+    tail=tail*t*bell
+    cdf=jnp.where(h<0.0,tail,1.0-tail)
+    return cdf,cdf+h*bell*(1.0/math.sqrt(2.0*math.pi))
 def norm(x):
     center=x-jnp.mean(x,-1,keepdims=True)
     inverse=lax.rsqrt(jnp.mean(center*center,-1,keepdims=True)+EPSILON)
@@ -353,9 +360,8 @@
     n1,inv1=norm(tok_ref[...].astype(f32)+dot(att,wo_ref[...],1,0))
     first=(n1*g0+b0).astype(bf)
     hidden=dot(first,wu_ref[...],1,0)
-    cdf=0.5*(1.0+erf(hidden*math.sqrt(0.5)))
+    cdf,slope=gelu_parts(hidden)
     act=(hidden*cdf).astype(bf)
-    slope=cdf+hidden*jnp.exp(-0.5*hidden*hidden)*(1.0/math.sqrt(2.0*math.pi))
     n2,inv2=norm(first.astype(f32)+dot(act,wd_ref[...],1,0))
     out_ref[...]=(n2*g1+b1).astype(bf)
     cot=cot_ref[...].astype(f32)
@@ -532,6 +538,7 @@
     def place(t):
         jj=jnp.where(t<NCH,1-j,j)
         return jj,pl.ds(al(lax.rem(t,NCH)*T,T),T)
+    def where(t): return pl.ds(al((jnp.where(t<NCH,1-j,j)*2+c)*block+lax.rem(t,NCH)*T,T),T)
     def load(t):
         jj,rows=place(t)
         return [pltpu.make_async_copy(att_hbm.at[:,jj,c,rows],aown.at[t],lsem.at[0,t]),pltpu.make_async_copy(tok_hbm.at[jj,c,rows],tok.at[t],lsem.at[1,t])]
@@ -570,11 +577,9 @@
         jj,rows=place(t)
         return pltpu.make_async_copy(r1.at[t],r1_out.at[jj,rows],osem.at[1,t])
     def out_da(t):
-        jj,rows=place(t)
-        return pltpu.make_async_copy(da.at[0,t],datt_out.at[:,jj,c,rows],osem.at[2,t])
+        return pltpu.make_async_copy(da.at[0,t],datt_out.at[:,where(t)],osem.at[2,t])
     def ship_da(t):
-        jj,rows=place(t)
-        return net.copy(da.at[1,t],datt_out.at[:,jj,c,rows],dsend.at[t],dget.at[t],sib)
+        return net.copy(da.at[1,t],datt_out.at[:,where(t)],dsend.at[t],dget.at[t],sib)
     def tiles(u,carry):
         ts=[G*u+g for g in range(G)]
         def each(f,*lists): return [f(*v) for v in zip(*lists)]
@@ -591,10 +596,9 @@
         n1,inv1=zip(*each(lambda t,b:norm(tok[t].astype(f32)+b),ts,branch))
         first=each(lambda n:(n*g0+b0).astype(bf),n1)
         hidden=each(lambda a:dot(a,wu,1,0),first)
-        cdf=each(lambda h:0.5*(1.0+erf(h*math.sqrt(0.5))),hidden)
+        cdf,slope=zip(*each(gelu_parts,hidden))
         act=each(lambda h,p:(h*p).astype(bf),hidden,cdf)
         fed=each(lambda a:dot(a,wd,1,0),act)
-        slope=each(lambda h,p:p+h*jnp.exp(-0.5*h*h)*(1.0/math.sqrt(2.0*math.pi)),hidden,cdf)
         n2,inv2=zip(*each(lambda a,b:norm(a.astype(f32)+b),first,fed))
         ct=each(lambda t:cot[t].astype(f32),ts)
         r2=each(lambda x,n,i:norm_back(x*g1,n,i),ct,n2,inv2)
@@ -608,14 +612,12 @@
         gu_ref[...]+=dot(both(first),both(dh),0,0)
         dr=each(lambda x,n,i:norm_back(x*g0,n,i),df,n1,inv1)
         db=each(lambda x:x.astype(bf),dr)
-        d=each(lambda x:dot(x,wo,1,1).astype(bf),db)
+        d=each(lambda x:dot(wo,x,1,1).astype(bf),db)
         go_ref[...]+=dot(both(att),both(db),0,0)
         for t,x,e in zip(ts,dr,d):
             r1[t]=x.astype(r1.dtype)
-            for p in range(P2):
-                lo=e[:,p*128:(p+1)*128]; hi=e[:,W+p*128:W+(p+1)*128]
-                da[0,t,p]=jnp.where(c==0,lo,hi)
-                da[1,t,p]=jnp.where(c==0,hi,lo)
+            da[0,t]=jnp.where(c==0,e[:W],e[W:])
+            da[1,t]=jnp.where(c==0,e[W:],e[:W])
         down=lambda v:sum(jnp.sum(x,0,keepdims=True) for x in v)
         gg_ref[0:1,:]+=down(each(lambda x,n:x*n,df,n1))
         gg_ref[1:2,:]+=down(each(lambda x,n:x*n,ct,n2))
@@ -647,24 +649,30 @@
     V=pl.BlockSpec(memory_space=pltpu.VMEM); A=pl.BlockSpec(memory_space=pl.ANY)
     S=jax.ShapeDtypeStruct; M=pltpu.VMEM; D=pltpu.SemaphoreType.DMA
     return pl.pallas_call(functools.partial(middle_net_kernel,Z,block,E,F,W,T),
-        out_shape=[S((block,E),bf),S((block,E),bf),S((2,block,E),f32),S((P2,2,2,block,128),bf)]+[S((2*Z,E//(2*Z),C),bf)],
+        out_shape=[S((block,E),bf),S((block,E),bf),S((2,block,E),bf),S((W,4*block),bf)]+[S((2*Z,E//(2*Z),C),bf)],
         in_specs=[A]*(4+Z),out_specs=[A,A,A,A,V],
         scratch_shapes=[M((E,E),f32),M((E,F),f32),M((F,E),f32),M((8,E),f32),M((E,128),f32),
-            M((n,P2,T,128),bf),M((n,P2,T,128),bf),M((n,T,E),bf),M((n,T,E),bf),M((Z,2,2,2,16,C),bf),M((n,T,E),bf),M((n,T,E),f32),M((2,n,P2,T,128),bf),
+            M((n,P2,T,128),bf),M((n,P2,T,128),bf),M((n,T,E),bf),M((n,T,E),bf),M((Z,2,2,2,16,C),bf),M((n,T,E),bf),M((n,T,E),bf),M((2,n,W,T),bf),
             D((3,n)),D((Z,)),D((3,n)),D((n,)),D((n,)),D((n,)),D((n,)),D((Z,)),D((Z,))],
         compiler_params=pltpu.CompilerParams(collective_id=2,has_side_effects=True,vmem_limit_bytes=VMEM))(att,tok,cot,cotx,*bunds)
-def reduce_kernel(Z,block,E,W,C1,rows,base_ref,meta_ref,dq_hbm,dkvw_hbm,tok_hbm,w_hbm,r1_hbm,parts,tok_out,grad_out,
-     dq,dkvw,tok,w,r1,own,tgf,tgr,tgs,ob,s0,r0,g0,s1,r1b,su,ru,fin,sx,rx,se,re,sxe,rxe,
-     lsem,osem,ts,tr,xs,xr,cs,cr,ys,yr,us,ur,fs,fr):
+def reduce_kernel(Z,block,E,W,C1,rows,base_ref,meta_ref,dq_hbm,dkvw_hbm,tok_hbm,w_hbm,r1_hbm,parts_hbm,tok_out,grad_out,
+     dq,dkvw,tok,w,r1,parts,own,tgf,tgr,tgs,ob,s0,r0,g0,s1,r1b,su,ru,fin,sx,rx,se,re,sxe,rxe,
+     lsem,nsem,osem,ts,tr,xs,xr,cs,cr,ys,yr,us,ur,fs,fr):
     net=Net(Z); z,y,j,c=net.z,net.y,net.j,net.c
     NCH=block//rows; half=2*block
     sib=net.at(c=1-c); xd=net.at(j=1-j); yd=net.at(y=1-y)
     def side(jj): return pl.ds(al(jj*half,128),half)
     def spans(jj): return pl.ds(jj*2*NCH,2*NCH)
-    loads=[pltpu.make_async_copy(a,b,lsem.at[k]) for k,(a,b) in enumerate(((dkvw_hbm.at[spans(1-j)],dkvw.at[spans(1-j)]),(dq_hbm.at[:,side(1-j)],dq.at[:,side(1-j)]),(w_hbm,w),(r1_hbm,r1),
+    def need(cc,k):
+        at=((1-j)*2+cc)*NCH+k; cols=pl.ds(al(at*rows,rows),rows)
+        return [pltpu.make_async_copy(dkvw_hbm.at[at],dkvw.at[at],nsem.at[0,cc,k]),pltpu.make_async_copy(dq_hbm.at[:,cols],dq.at[:,cols],nsem.at[1,cc,k])]
+    loads=[pltpu.make_async_copy(a,b,lsem.at[k]) for k,(a,b) in enumerate(((w_hbm,w),(r1_hbm,r1),(parts_hbm,parts),
         (dq_hbm.at[:,side(j)],dq.at[:,side(j)]),(tok_hbm,tok),(dkvw_hbm.at[spans(j)],dkvw.at[spans(j)])))]
     net.signal()
-    for x in loads: x.start()
+    for x in need(1-c,0)+loads[:1]+need(c,0): x.start()
+    for k in range(1,NCH):
+        for x in need(1-c,k)+need(c,k): x.start()
+    for x in loads[1:]: x.start()
     def chunk(k): return pl.ds(k*rows,rows)
     def landed(ref,sem): pltpu.make_async_copy(ref,ref,sem).wait()
     def position(jj,cc,k): return pl.ds(al(((jj*2+cc)*NCH+k)*rows,rows),rows)
@@ -672,11 +680,10 @@
         ssl=position(jj,cc,k)
         dq[W:3*W,ssl]=placed(base_ref,meta_ref[0:1,ssl],dkvw[(jj*2+cc)*NCH+k],dq[W:3*W,ssl],(jj*2+cc)*NCH+k).astype(bf)
     def to_tokens(jj,cc,k): return dot(dq[:,position(jj,cc,k)],w[...],0,1)
-    def for_sibling(t):
+    def for_sibling(t,k):
         jj=1-j if t==0 else j
-        for k in range(NCH):
-            tgf[jj,chunk(k),:]=to_tokens(jj,1-c,k).astype(bf)
-            net.send(tgf.at[jj,chunk(k)],tgr.at[jj,chunk(k)],ts.at[t,k],tr.at[t,k],sib)
+        tgf[jj,chunk(k),:]=to_tokens(jj,1-c,k).astype(bf)
+        net.send(tgf.at[jj,chunk(k)],tgr.at[jj,chunk(k)],ts.at[t,k],tr.at[t,k],sib)
     def split(x,n): return x.reshape(Z,2,2,2,16,n)
     def core_sum(v,lo,n):
         x=dot(dq[lo:lo+n,:],tok[...],1,0).T.astype(bf)
@@ -716,20 +723,26 @@
         fin[:,:,cut[v]]=sum_
         sx[:,cut[v]]=jnp.where(j==0,sum_[1],sum_[0]).astype(bf)
         net.send(sx.at[:,cut[v]],rx.at[:,cut[v]],fs.at[v],fr.at[v],xd)
-    for x in loads[:3]: x.wait()
-    for k in range(NCH): place(1-j,1-c,k)
-    net.wait()
-    for_sibling(0)
-    for k in range(NCH): place(1-j,c,k)
-    for k in range(NCH): own[1-j,chunk(k),:]=to_tokens(1-j,c,k)
-    loads[3].wait()
-    def total(jj,k): return (own[jj,chunk(k),:]+tgr[jj,chunk(k),:].astype(f32)+r1[jj,chunk(k),:]).astype(bf)
-    for k in range(NCH):
+    def total(jj,k): return (own[jj,chunk(k),:]+tgr[jj,chunk(k),:].astype(f32)+r1[jj,chunk(k),:].astype(f32)).astype(bf)
+    def far(k):
         landed(tgr.at[1-j,chunk(k)],tr.at[0,k])
         tgs[chunk(k),:]=total(1-j,k)
         net.send(tgs.at[chunk(k)],ob.at[j,chunk(k)],xs.at[k],xr.at[k],xd)
-    for x in loads[4:]: x.wait()
+    for k in range(NCH):
+        for x in need(1-c,k): x.wait()
+        place(1-j,1-c,k)
+        if k==0:
+            loads[0].wait()
+            net.wait()
+        for_sibling(0,k)
+        for x in need(c,k): x.wait()
+        place(1-j,c,k)
+        own[1-j,chunk(k),:]=to_tokens(1-j,c,k)
+        if k==0: loads[1].wait()
+        else: far(k-1)
+    for x in loads[2:]: x.wait()
     core_sum(0,0,W)
+    far(NCH-1)
     for cc in (1-c,c):
         for k in range(NCH): place(j,cc,k)
     core_get(0,0,W)
@@ -747,7 +760,7 @@
     core_get(2,2*W,W)
     to_y(2)
     to_z(0)
-    for_sibling(1)
+    for k in range(NCH): for_sibling(1,k)
     to_z(1)
     landed(re,cr.at[3])
     early0=early0+re[...].astype(f32)
@@ -768,10 +781,13 @@
     for v in range(3):
         landed(rx.at[:,cut[v]],fr.at[v])
         grad_out[:,cut[v]]=jnp.where(j==0,fin[0,:,cut[v]],fin[1,:,cut[v]])+rx[:,cut[v]].astype(f32)
-    for k in range(NCH): landed(ob.at[1-j,chunk(k)],xr.at[k])
-    last=pltpu.make_async_copy(ob.at[1-j],tok_out.at[1-j],osem.at[1]); last.start()
+    last=[pltpu.make_async_copy(ob.at[1-j,chunk(k)],tok_out.at[1-j,chunk(k)],osem.at[1+k]) for k in range(NCH)]
+    for k in range(NCH):
+        landed(ob.at[1-j,chunk(k)],xr.at[k])
+        last[k].start()
     net.drain()
-    near.wait(); last.wait()
+    near.wait()
+    for x in last: x.wait()
 
 def reduce(base,meta,dq,dkvw,tok,w,r1,parts,Z,W):
     _,block,E=r1.shape; L=4*block; C1=parts.shape[2]; C=6*W
@@ -780,36 +796,45 @@
     S=jax.ShapeDtypeStruct; M=pltpu.VMEM; D=pltpu.SemaphoreType.DMA
     return pl.pallas_call(functools.partial(reduce_kernel,Z,block,E,W,C1,rows),
         out_shape=[S((2,block,E),bf),S((16,C+C1),f32)],
-        in_specs=[pl.BlockSpec(memory_space=pltpu.SMEM),V,A,A,A,A,A,V],out_specs=[A,V],
-        scratch_shapes=[M(dq.shape,bf),M(dkvw.shape,bf),M(tok.shape,bf),M(w.shape,bf),M(r1.shape,f32),M((2,block,E),f32),M((2,block,E),bf),M((2,block,E),bf),M((block,E),bf),M((2,block,E),bf),
+        in_specs=[pl.BlockSpec(memory_space=pltpu.SMEM),V,A,A,A,A,A,A],out_specs=[A,V],
+        scratch_shapes=[M(dq.shape,bf),M(dkvw.shape,bf),M(tok.shape,bf),M(w.shape,bf),M(r1.shape,bf),M(parts.shape,bf),M((2,block,E),f32),M((2,block,E),bf),M((2,block,E),bf),M((block,E),bf),M((2,block,E),bf),
             M((Z,2,2,16,3*W),bf),M((Z,2,2,16,3*W),bf),M((Z,2,2,16,C),bf),M((Z,2,16,C),bf),M((Z,2,16,C),bf),
             M((Z,2,16,C),bf),M((Z,2,16,C),bf),M((2,16,C),f32),M((16,C),bf),M((16,C),bf),M((2,16,C1),bf),M((2,16,C1),bf),M((16,C1),bf),M((16,C1),bf),
-            D((7,)),D((2,)),D((2,NCH)),D((2,NCH)),D((NCH,)),D((NCH,)),D((4,)),D((4,)),D((3,)),D((3,)),D((3,Z)),D((3,Z)),D((4,)),D((4,))],
+            D((6,)),D((2,2,NCH)),D((1+NCH,)),D((2,NCH)),D((2,NCH)),D((NCH,)),D((NCH,)),D((4,)),D((4,)),D((3,)),D((3,)),D((3,Z)),D((3,Z)),D((4,)),D((4,))],
         compiler_params=pltpu.CompilerParams(collective_id=1,has_side_effects=True,vmem_limit_bytes=VMEM))(base,meta,dq,dkvw,tok,w,r1,parts)
 
-def finish_kernel(W,near,far,tg_hbm,grads,lay_out,tg_out,gq,go,gu,gd,gg,gs,lay,tg,sem):
-    j=lax.axis_index("blk")//2
-    come=[pltpu.make_async_copy(a,b,sem.at[k]) for k,(a,b) in enumerate(((near,lay.at[j]),(far,lay.at[1-j]),(tg_hbm.at[0],tg.at[0]),(tg_hbm.at[1],tg.at[1])))]
-    go_out=[pltpu.make_async_copy(a,b,sem.at[4+k]) for k,(a,b) in enumerate(((lay.at[j],lay_out.at[j]),(lay.at[1-j],lay_out.at[1-j]),(tg.at[0],tg_out.at[0]),(tg.at[1],tg_out.at[1])))]
+def finish_kernel(W,E,F,near,far,tg_hbm,grads_hbm,lay_out,tg_out,gq,go,gu,gd,gg,gs,lay,tg,grads,small,isem,osem):
+    j=lax.axis_index("blk")//2; block=near.shape[0]; n=4; rows=block//n
+    gcopy=pltpu.make_async_copy(grads_hbm,grads,isem.at[4*n]); gcopy.start()
+    come=[];leave=[]
+    for k in range(n):
+        r=pl.ds(k*rows,rows)
+        for a,b,o in ((near.at[r],lay.at[j,r],lay_out.at[j,r]),(far.at[r],lay.at[1-j,r],lay_out.at[1-j,r]),(tg_hbm.at[0,r],tg.at[0,r],tg_out.at[0,r]),(tg_hbm.at[1,r],tg.at[1,r],tg_out.at[1,r])):
+            at=len(come)
+            come.append(pltpu.make_async_copy(a,b,isem.at[at])); leave.append(pltpu.make_async_copy(b,o,osem.at[at]))
     for x in come: x.start()
+    gcopy.wait()
     at=0
-    for ref in (gq,go,gu,gd):
-        n=ref.shape[1]
-        ref[...]=grads[:,at:at+n]
-        at+=n
+    for k,ref in enumerate((gq,go,gu,gd)):
+        width=ref.shape[1]
+        leave.append(pltpu.make_async_copy(grads.at[:,at:at+width],ref,osem.at[4*n+k]))
+        at+=width
+        leave[-1].start()
     t=grads[:,at:].T
-    gg[...]=t[0:2,:]
-    gs[...]=t[2:4,:]
-    for x,o in zip(come,go_out):
+    small[0]=t[0:2,:]; small[1]=t[2:4,:]
+    for k,ref in enumerate((gg,gs)):
+        leave.append(pltpu.make_async_copy(small.at[k],ref,osem.at[4*n+4+k]))
+        leave[-1].start()
+    for x,o in zip(come,leave):
         x.wait(); o.start()
-    for o in go_out: o.wait()
+    for o in leave: o.wait()
 
 def finish(near,far,tg,grads,W,F):
     _,block,E=tg.shape
-    V=pl.BlockSpec(memory_space=pltpu.VMEM); A=pl.BlockSpec(memory_space=pl.ANY); S=jax.ShapeDtypeStruct
-    return pl.pallas_call(functools.partial(finish_kernel,W),
+    A=pl.BlockSpec(memory_space=pl.ANY); S=jax.ShapeDtypeStruct; M=pltpu.VMEM; D=pltpu.SemaphoreType.DMA
+    return pl.pallas_call(functools.partial(finish_kernel,W,E,F),
         out_shape=[S(tg.shape,bf),S(tg.shape,bf),S((16,6*W),f32),S((16,E),f32),S((16,F),f32),S((16,E),f32),S((2,16),f32),S((2,16),f32)],
-        in_specs=[A,A,A,V],out_specs=[A,A]+[V]*6,scratch_shapes=[pltpu.VMEM(tg.shape,bf),pltpu.VMEM(tg.shape,bf),pltpu.SemaphoreType.DMA((8,))],
+        in_specs=[A]*4,out_specs=[A]*8,scratch_shapes=[M(tg.shape,bf),M(tg.shape,bf),M(grads.shape,f32),M((2,2,16),f32),D((17,)),D((22,))],
         compiler_params=pltpu.CompilerParams(vmem_limit_bytes=VMEM))(near,far,tg,grads)
 def shards(tokens,cotangent,segments,padding,known,w_qkv,w_out,w_up,w_down,norm_gains,norm_shifts):
     micro,rows,block,D=tokens.shape
@@ -831,7 +856,7 @@
         near,far,r1,datt,parts=middle_net(att.reshape(H//2,2,2,block,128),tok,cot,cotx,bunds,Z,W,F)
         parts=lax.all_to_all(parts,"dp",0,0,tiled=True)
         layx=lax.ppermute(far,"blk",across)
-        dq,dkvw=back(base,win,datt.reshape(H//2,L,128),p,ot,inv,kct,vaug,qkvt,H)
+        dq,dkvw=back(base,win,datt,p,ot,inv,kct,vaug,qkvt,H)
         tg,grads=reduce(base,meta,dq,dkvw,tok.reshape(L,D),w_mine,r1,parts,Z,W)
         out=finish(near,layx,tg,grads,W,F)
         return (out[0].reshape(tokens.shape),out[1].reshape(tokens.shape))+tuple(out[2:])
@@ -864,7 +889,7 @@
     out,r1,da,go,gu,gd,gg=middle(a0,a1,own_tok.reshape(L//2,D),own_cot,full_out,full_up,full_down,gs)
     da=da.reshape(2,H//2,J,block,128)
     dmine=part(da,0,core); dhis=other(part(da,0,1-core))
-    datt=jnp.stack([jnp.where(core==0,dmine,dhis),jnp.where(core==0,dhis,dmine)],2).reshape(H//2,L,128)
+    datt=jnp.stack([jnp.where(core==0,dmine,dhis),jnp.where(core==0,dhis,dmine)],2).reshape(H//2,L,128).transpose(0,2,1).reshape(W,L)
     dq,dkvw=back(base,win,datt,p,ot,inv,kct,vaug,qkvt,H)
     tg,gq=place_all(base,meta,dq,dkvw,all_tok,w_mine,H)
     tg=tg.reshape(J,2,block,D)

time: 315 us -> 309 us (0.981)
  Pallas kernels: 286 us -> 282 us
where the time goes in v4:
time: 309 us; the launch traced here: 308 us
  Pallas kernels  282 us (91%)
  starting transfers between devices  25.4 us (8%)
    pallas_call x1, Pallas kernels, attend(): pl.pallas_call(functools.partial(attend_kernel, L, H), out_shape=[S((cap,...  151 us
    pallas_call x1, Pallas kernels, back(): pl.pallas_call(functools.partial(back_kernel, L, H), out_shape=[S((3 * W,...  42.8 us
    pallas_call x1, Pallas kernels, reduce(): pl.pallas_call(functools.partial(reduce_kernel, Z, block, E, W, C1, rows)...  32.7 us
    pallas_call x1, Pallas kernels, gather(): pl.pallas_call(functools.partial(gather_kernel, Z, block, E, W, rows), ou...  32.4 us
    all_to_all x1, starting transfers between devices, shards(): parts = lax.all_to_all(parts, 'dp', 0, 0, tiled=True)  20.8 us
    pallas_call x1, Pallas kernels, middle_net(): pl.pallas_call(functools.partial(middle_net_kernel, Z, block, E, F, W, T)...  19.4 us
  transfers between devices with their start and end apart: 6, of which 0 were waited for; matrix products, arithmetic and copies ran while one was open for 0% of the time, Pallas kernels for 73%

profile of v4, /device:TPU:0, one launch (start us, length us, event | category | flops | bytes accessed | tf_op | source)
XLA Modules:
  0.0 307.9 jit_solution(12892638940296466949)
XLA Ops:
  0.6 32.4 %shard_map.170 = (bf16[2,2,768,512]{3,2,1,0:T(8,128)(2,1)}, bf16[2,2,16,1664]{3,2,1,0:T(8,128)(2,1)}, bf16[512,768]{1,0:T(8,128)(2,1)}, bf16[768,3072]{1,0:T(8,1...) custom-call(bf16[2,768,512]{2,1,0:T(8,128)(2,1)} %bitcast.13, ...), custom_call_target="tpu_custom_call" | custom-call | tf_op jit(solution)/shard_map/pallas_call | solution.py:526
  33.0 0.7 collective-permute-start
  33.7 2.8 collective-permute-start.3
  36.5 0.0 collective-permute-start.2
  36.5 1.1 collective-permute-start.1
  37.6 150.8 %shard_map.171 = (bf16[42,4,512,512]{3,2,1,0:T(8,128)(2,1)}, bf16[2,3072,128]{2,1,0:T(8,128)(2,1)}, f32[6,256,512]{2,1,0:T(8,128)}, f32[4,8,3072]{2,1,0:T(8,128)...) custom-call(s32[16,128]{1,0:T(8,128)} %get-tuple-element.40.base_ref, ...), custom_call_target="tpu_custom_call" | custom-call | tf_op jit(solution)/shard_map/pallas_call | solution.py:164
  188.4 0.0 collective-permute-done.3.rest_3_
  188.4 0.0 collective-permute-done.2.rest_2_
  188.4 0.0 collective-permute-done.1.rest_1_
  188.4 0.0 collective-permute-done.cotx_hbm
  188.5 19.4 %shard_map.172 = (bf16[768,512]{1,0:T(8,128)(2,1)}, bf16[768,512]{1,0:T(8,128)(2,1)}, bf16[2,768,512]{2,1,0:T(8,128)(2,1)}, bf16[256,3072]{1,0:T(8,128)(2,1)}, bf16[8,64,1664]{2,1,0:T(8,128)(2,1)}) custom-call(bf16[2,2,2,768,128]{4,3,2,1,0:T(8,128)(2,1)} %bitcast.14, bf16[2,2,768,512]{3,2,1,0:T(8,128)(2,1)} %get-tuple-element.46.tok_hbm, ...), custom_call_target="tpu_custom_call" | custom-call | tf_op jit(solution)/shard_map/pallas_call | solution.py:651
  207.9 20.8 %all-to-all-start = ((bf16[8,64,1664]{2,1,0:T(8,128)(2,1)}), bf16[8,64,1664]{2,1,0:T(8,128)(2,1)}, u32[]{:S(2)}, u32[]{:S(2)}) async-start(bf16[8,64,1664]{2,1,0:T(8,128)(2,1)} %get-tuple-element.61), calls=%async_computation | async-start | bytes 3407872 | tf_op jit(solution)/shard_map/all_to_all | solution.py:857
  228.6 0.0 collective-permute-start.4
  228.6 42.8 %shard_map.173 = (bf16[768,3072]{1,0:T(8,128)(2,1)}, bf16[12,512,384]{2,1,0:T(8,128)(2,1)}) custom-call(s32[16,128]{1,0:T(8,128)} %get-tuple-element.40.base_ref, s32[32,128]{1,0:T(8,128)} %get-tuple-element.41.win_ref, bf16[256,3072]{1,0:T(8,128)(2,1)} %get-tuple-element.51.datt_hbm, bf16[42,4,512,512]{3,2,1,0:T(8,128)(2,1)} %get-tuple-element.52.p_hbm, ...), custom_call_target="tpu_custom_call" | custom-call | tf_op jit(solution)/shard_map/pallas_call | solution.py:308
  271.5 0.0 all-to-all-done.parts_hbm
  271.5 32.7 %shard_map.174 = (bf16[2,768,512]{2,1,0:T(8,128)(2,1)}, f32[16,3200]{1,0:T(8,128)}) custom-call(s32[16,128]{1,0:T(8,128)} %get-tuple-element.40.base_ref, s32[8,3072]{1,0:T(8,128)} %get-tuple-element.44.meta_ref, bf16[768,3072]{1,0:T(8,128)(2,1)} %get-tuple-element.57.dq_hbm, bf16[12,512,384]{2,1,0:T(8,128)(2,1)} %get-tuple-element.58.dkvw_hbm, ...), custom_call_target="tpu_custom_call" | custom-call | tf_op jit(solution)/shard_map/pallas_call | solution.py:797
  304.2 0.0 collective-permute-done.4.far
  304.2 3.5 %shard_map.175 = (bf16[2,768,512]{2,1,0:T(8,128)(2,1)}, bf16[2,768,512]{2,1,0:T(8,128)(2,1)}, f32[16,1536]{1,0:T(8,128)}, f32[16,512]{1,0:T(8,128)}, f32[16,512]...) custom-call(bf16[768,512]{1,0:T(8,128)(2,1)} %get-tuple-element.49.near, ...), custom_call_target="tpu_custom_call" | custom-call | tf_op jit(solution)/shard_map/pallas_call | solution.py:835
Async XLA Ops:
  33.0 155.4 %collective-permute-start = (bf16[768,512]{1,0:T(8,128)(2,1)}, bf16[768,512]{1,0:T(8,128)(2,1)}, u32[]{:S(2)}, u32[]{:S(2)}) collective-permute-start(bf16[768,512]{1,0:T(8,128)(2,1)} %get-tuple-element.47), channel_id=1, source_target_pairs={{0,2},{1,3},{2,0},{3,1},{4,6},{5,7},{6,4},{7,5},{8,10},{9,11},{10,... | collective-permute-start | bytes 2359304 | tf_op jit(solution)/shard_map/ppermute | solution.py:854
  33.7 154.7 %collective-permute-start.3 = (bf16[2,2,16,1664]{3,2,1,0:T(8,128)(2,1)}, bf16[2,2,16,1664]{3,2,1,0:T(8,128)(2,1)}, u32[]{:S(2)}, u32[]{:S(2)}) collective-permute-start(bf16[2,2,16,1664]{3,2,1,0:T(8,128)(2,1)} %get-tuple-element.48.rest_0_), channel_id=1, source_target_pairs={{0,24},{4,28},{8,0},{12,4},{16,8},{20,12},{24,16},{28,20},{1,25},{... | collective-permute-start | bytes 638984 | tf_op jit(solution)/shard_map/ppermute | solution.py:852
  36.5 151.9 %collective-permute-start.2 = (bf16[2,2,16,1664]{3,2,1,0:T(8,128)(2,1)}, bf16[2,2,16,1664]{3,2,1,0:T(8,128)(2,1)}, u32[]{:S(2)}, u32[]{:S(2)}) collective-permute-start(bf16[2,2,16,1664]{3,2,1,0:T(8,128)(2,1)} %get-tuple-element.48.rest_0_), channel_id=1, source_target_pairs={{0,16},{4,20},{8,24},{12,28},{16,0},{20,4},{24,8},{28,12},{1,17},{... | collective-permute-start | bytes 638984 | tf_op jit(solution)/shard_map/ppermute | solution.py:852
  36.5 151.9 %collective-permute-start.1 = (bf16[2,2,16,1664]{3,2,1,0:T(8,128)(2,1)}, bf16[2,2,16,1664]{3,2,1,0:T(8,128)(2,1)}, u32[]{:S(2)}, u32[]{:S(2)}) collective-permute-start(bf16[2,2,16,1664]{3,2,1,0:T(8,128)(2,1)} %get-tuple-element.48.rest_0_), channel_id=1, source_target_pairs={{0,8},{4,12},{8,16},{12,20},{16,24},{20,28},{24,0},{28,4},{1,9},{5... | collective-permute-start | bytes 638984 | tf_op jit(solution)/shard_map/ppermute | solution.py:852
  207.9 63.6 %all-to-all-start = ((bf16[8,64,1664]{2,1,0:T(8,128)(2,1)}), bf16[8,64,1664]{2,1,0:T(8,128)(2,1)}, u32[]{:S(2)}, u32[]{:S(2)}) async-start(bf16[8,64,1664]{2,1,0:T(8,128)(2,1)} %get-tuple-element.61), calls=%async_computation | async-start | bytes 3407872 | tf_op jit(solution)/shard_map/all_to_all | solution.py:857
  228.6 75.6 %collective-permute-start.4 = (bf16[768,512]{1,0:T(8,128)(2,1)}, bf16[768,512]{1,0:T(8,128)(2,1)}, u32[]{:S(2)}, u32[]{:S(2)}) collective-permute-start(bf16[768,512]{1,0:T(8,128)(2,1)} %get-tuple-element.50), channel_id=1, source_target_pairs={{0,2},{1,3},{2,0},{3,1},{4,6},{5,7},{6,4},{7,5},{8,10},{9,11},{10,... | collective-permute-start | bytes 2359304 | tf_op jit(solution)/shard_map/ppermute | solution.py:858

commit v5 on v4

--- a/solution.py
+++ b/solution.py
@@ -38,8 +38,8 @@
         def _(): fn(al(first+full*KB,128),r*128,g)
     return g+1
 
-def attend_kernel(L,H,base_ref,win_ref,qkvt_hbm,codet_ref,meta_ref,p_hbm,att_hbm,ot_hbm,inv_ref,kct_hbm,vaug_hbm,
-                  kaug_ref,kct_ref,vaug_ref,kvt,q_ref,v_ref,vct,acc,pbuf,obuf,abuf,top_ref,psem,osem,asem,ksem,lsem):
+def attend_kernel(L,H,base_ref,win_ref,qkvt_hbm,codet_ref,meta_ref,p_hbm,att_hbm,ot_hbm,inv_ref,kct_hbm,vct_hbm,
+                  kaug_ref,kct_ref,kvt,q_ref,v_ref,vct,acc,pbuf,obuf,abuf,top_ref,psem,osem,asem,ksem,lsem):
     W=H*HEAD; nq=L//QB
     total=begin(base_ref,L//256)
     come=[pltpu.make_async_copy(qkvt_hbm.at[W+h*HEAD:W+(h+1)*HEAD],kvt.at[h*128:h*128+HEAD],lsem.at[h]) for h in range(H)]
@@ -67,12 +67,10 @@
             k1=jnp.where(row[:128]==HEAD+10,-2560.0,ka[h*128:(h+1)*128])
             kaug_ref[h,dsl,:]=k1.astype(bf).T
             kct_ref[h,:,dsl]=k1[:HEAD].astype(bf)
-            v1=va[h*HEAD:(h+1)*HEAD]
-            vct[h,:HEAD,dsl]=v1.astype(bf)
-            vaug_ref[h,dsl,:]=jnp.concatenate([v1,jnp.where(row[:HEAD]<3,-1.0,0.0)],0).astype(bf).T
+            vct[h,:HEAD,dsl]=va[h*HEAD:(h+1)*HEAD].astype(bf)
         return c
     lax.fori_loop(0,(total+255)//256,dest,0)
-    keep=[pltpu.make_async_copy(kct_ref,kct_hbm,ksem.at[0]),pltpu.make_async_copy(vaug_ref,vaug_hbm,ksem.at[1])]
+    keep=[pltpu.make_async_copy(kct_ref,kct_hbm,ksem.at[0]),pltpu.make_async_copy(vct,vct_hbm,ksem.at[1])]
     for x in keep: x.start()
     come[H+1].wait()
     bound=jnp.float32(0)
@@ -123,7 +121,7 @@
                 keepp=[]
                 for h in range(H):
                     p=jnp.exp2(dot(kaug_ref[h,osl,:],qa[h],1,0)).astype(bf)
-                    pbuf[ps,h,:size,:]=p
+                    pbuf[ps,h,:,:size]=p.T
                     keepp.append(p)
                 for h in range(H): acc[h]+=dot(vct[h,:,osl],keepp[h],1,0)
             @pl.when(jnp.logical_not(safe))
@@ -132,7 +130,7 @@
                     def put(j,c):
                         jsl=pl.ds(al(off+j*128,128),128)
                         p=jnp.exp2(strict(h,jsl)-top_ref[h:h+1,:]).astype(bf)
-                        pbuf[ps,h,pl.ds(al(j*128,128),128),:]=p
+                        pbuf[ps,h,:,pl.ds(al(j*128,128),128)]=p.T
                         acc[h]+=dot(vct[h,:,jsl],p,1,0)
                         return c
                     lax.fori_loop(0,size//128,put,0)
@@ -162,10 +160,10 @@
     V=pl.BlockSpec(memory_space=pltpu.VMEM); A=pl.BlockSpec(memory_space=pl.ANY)
     S=jax.ShapeDtypeStruct; M=pltpu.VMEM; D=pltpu.SemaphoreType.DMA
     return pl.pallas_call(functools.partial(attend_kernel,L,H),
-        out_shape=[S((cap,H,KB,QB),bf),S((H//2,L,128),bf),S((nq,W,QB),f32),S((H,8,L),f32),S((H,HEAD,L),bf),S((H,L,128),bf)],
+        out_shape=[S((cap,H,QB,KB),bf),S((H//2,L,128),bf),S((nq,W,QB),f32),S((H,8,L),f32),S((H,HEAD,L),bf),S((H,HEAD+16,L),bf)],
         in_specs=[pl.BlockSpec(memory_space=pltpu.SMEM)]*2+[A,V,V],
         out_specs=[A,A,A,V,A,A],
-        scratch_shapes=[M((H,L,128),bf),M((H,HEAD,L),bf),M((H,L,128),bf),M((H*128,L),bf),M((W,L),bf),M((W,L),bf),M((H,HEAD+16,L),bf),M((H,HEAD+16,QB),f32),M((SLOTS,H,KB,QB),bf),
+        scratch_shapes=[M((H,L,128),bf),M((H,HEAD,L),bf),M((H*128,L),bf),M((W,L),bf),M((W,L),bf),M((H,HEAD+16,L),bf),M((H,HEAD+16,QB),f32),M((SLOTS,H,QB,KB),bf),
             M((2,W,QB),f32),M((2,H//2,QB,128),bf),M((8,QB),f32),D((SLOTS,)),D((2,)),D((2,)),D((2,)),D((H+2,))],
         compiler_params=pltpu.CompilerParams(vmem_limit_bytes=VMEM))(base,win,qkvt,codet,meta)
 
@@ -180,25 +178,29 @@
     incl=dot(x.astype(bf),(iota((256,256),0)<=iota((256,256),1)).astype(f32).astype(bf),1,0)
     tot=jnp.broadcast_to(incl[:,255:256],(16,256)).astype(bf)
     base=dot((iota((16,16),0)>iota((16,16),1)).astype(f32).astype(bf),tot,1,0)
-    rank=(incl+base).astype(jnp.int32)-1
-    rank=jnp.concatenate([rank[b:b+1] for b in range(nb)],1)
-    rank=jnp.where(use,rank,-1)
+    mid=seg[:,L//2:L//2+1]
+    late=(seg>=mid).astype(f32)
+    early=jnp.sum(usef*(1.0-late),1,keepdims=True)
+    shift=jnp.ceil(early*(1.0/128.0))*128.0-early
+    shift=jnp.where(jnp.sum(usef,1,keepdims=True)+shift<=L,shift,0.0)
+    csum=jnp.concatenate([(incl+base)[b:b+1] for b in range(nb)],1)+late*shift
+    rank=jnp.where(use,csum.astype(jnp.int32)-1,-1)
+    base=base+shift*jnp.concatenate([late[:,b*256:b*256+1] for b in range(nb)]+[jnp.ones((16-nb,1),f32)],0)
     own=((pad==0)&(known!=1)).astype(jnp.int32)
     bits=iota((CODE,L),0)
     bit=lax.shift_right_logical(jnp.broadcast_to(seg,(CODE,L)),jnp.minimum(bits,9))&1
     codet=jnp.where(bits<10,jnp.where(bit==1,16.0,-16.0),jnp.where(bits==10,1.0,0.0)).astype(bf)
     meta=jnp.concatenate([rank,own,jnp.zeros((6,L),jnp.int32)],0)
     def edge(at): return jnp.concatenate([seg[:,i*QB+at:i*QB+at+1] for i in range(nq)]+[jnp.zeros((8-nq,1),jnp.int32)],0)
-    low=jnp.sum(jnp.where(seg<edge(0),usef,0.0),1,keepdims=True)
-    high=jnp.sum(jnp.where(seg<=edge(QB-1),usef,0.0),1,keepdims=True)
-    csum=jnp.concatenate([(incl+base)[b:b+1] for b in range(nb)],1)
+    low=jnp.sum(jnp.where(seg<edge(0),usef,0.0),1,keepdims=True)+shift*(edge(0)>=mid).astype(f32)
+    high=jnp.sum(jnp.where(seg<=edge(QB-1),usef,0.0),1,keepdims=True)+shift*(edge(QB-1)>=mid).astype(f32)
     starts=jnp.sum((csum<=(256*iota((16,1),0)).astype(f32)).astype(f32),1,keepdims=True)
     win=jnp.broadcast_to(jnp.concatenate([low,high,starts],0),(32,128)).astype(jnp.int32)
     return base[:,:128].astype(jnp.int32),win,codet,meta
 LN2=math.log(2.0)
-SPAN=384
-def back_kernel(L,H,base_ref,win_ref,datt_hbm,p_hbm,ot_hbm,inv_ref,kct_hbm,vaug_hbm,qkvt_hbm,dq_hbm,dkvw_hbm,
-                vaug_ref,kct,dkv,dkvt,pbuf,qacc,qkv,datt,ot,dq,psem,lsem,qsem,osem,tsem):
+SPAN=512
+def back_kernel(L,H,base_ref,win_ref,datt_hbm,p_hbm,ot_hbm,inv_ref,kct_hbm,vct_hbm,qkvt_hbm,dq_hbm,dkvw_hbm,
+                kct,vct,dkv,dkvt,pbuf,qacc,qkv,datt,ot,dq,psem,lsem,qsem,osem,tsem):
     W=H*HEAD; nq=L//QB
     groups=(begin(base_ref,L//256)+127)//128
     pieces=lax.fori_loop(0,nq,lambda i,s:s+window(win_ref,i)[1]+1,0)
@@ -207,7 +209,7 @@
         return pltpu.make_async_copy(p_hbm.at[g],pbuf.at[slot],psem.at[slot])
     def keys(t):
         rows=pl.ds(al(t*KB,KB),KB)
-        return [pltpu.make_async_copy(kct_hbm.at[:,:,rows],kct.at[:,:,rows],lsem.at[0,t]),pltpu.make_async_copy(vaug_hbm.at[:,rows],vaug_ref.at[:,rows],lsem.at[1,t])]
+        return [pltpu.make_async_copy(vct_hbm.at[:,:,rows],vct.at[:,:,rows],lsem.at[0,t]),pltpu.make_async_copy(kct_hbm.at[:,:,rows],kct.at[:,:,rows],lsem.at[1,t])]
     def queries(i):
         slot=lax.rem(i,2); qsl=pl.ds(al(i*QB,QB),QB)
         return [pltpu.make_async_copy(a,b.at[slot],qsem.at[k,slot]) for k,(a,b) in enumerate(((qkvt_hbm.at[:,qsl],qkv),(datt_hbm.at[:,qsl],datt),(ot_hbm.at[i],ot)))]
@@ -222,7 +224,7 @@
         @pl.when(s<pieces)
         def _(): pcopy(s).start()
     def clear(j,c):
-        dkv[pl.ds(al(j*128,128),128),:]=jnp.zeros((128,2*W),f32)
+        dkv[:,pl.ds(al(j*128,128),128)]=jnp.zeros((2*W,128),f32)
         return c
     lax.fori_loop(0,groups,clear,0)
     def ocopy(i):
@@ -238,8 +240,7 @@
             for x in queries(i+1): x.start()
         dt=datt[slot].astype(f32)
         prod=dt*ot[slot]
-        daug=[];dz=[];qz=[];deltas=[];d1s=[]
-        zero=jnp.zeros((HEAD,QB),bf)
+        daug=[];lows=[];deltas=[];d1s=[]
         row=iota((16,QB),0)
         for h in range(H):
             hsl=slice(h*HEAD,(h+1)*HEAD)
@@ -248,14 +249,10 @@
             d1=dt[hsl]*inv
             low=d1.astype(bf)
             a=delta.astype(bf).astype(f32); b=(delta-a).astype(bf).astype(f32)
-            extra=jnp.where(row==0,a,jnp.where(row==1,b,jnp.where(row==2,delta-a-b,0.0))).astype(bf)
-            daug.append(jnp.concatenate([low,extra,jnp.zeros((HEAD-16,QB),bf)],0))
-            q=qkv[slot,hsl,:]
-            dz.append(jnp.concatenate([zero,low] if h%2 else [low,zero],0))
-            qz.append(jnp.concatenate([zero,q] if h%2 else [q,zero],0))
-            deltas.append(delta); d1s.append(d1)
+            extra=jnp.where(row==0,-a,jnp.where(row==1,-b,jnp.where(row==2,a+b-delta,0.0))).astype(bf)
+            daug.append(jnp.concatenate([low,extra,jnp.zeros((HEAD-16,QB),bf)],0).T[:,:HEAD+16])
+            lows.append(low); deltas.append(delta); d1s.append(d1)
         qacc[...]=jnp.zeros_like(qacc)
-        def wide(v): return jnp.concatenate(v,1)
         def piece(off,size,g):
             ps=lax.rem(g,SLOTS)
             osl=pl.ds(off,size)
@@ -267,11 +264,11 @@
             pcopy(g).wait()
             dss=[]
             for h in range(H):
-                dss.append((pbuf[ps,h,:size,:].astype(f32)*dot(vaug_ref[h,osl,:],daug[h],1,0)).astype(bf))
-            for h in range(H): qacc[h*HEAD:(h+1)*HEAD,:]+=dot(kct[h,:,osl],dss[h],1,0)
-            for h in range(0,H,2):
-                dkv[osl,h*HEAD:(h+2)*HEAD]+=dot(wide(dss[h:h+2]),wide(qz[h:h+2]),1,1)
-                dkv[osl,W+h*HEAD:W+(h+2)*HEAD]+=dot(wide([pbuf[ps,h,:size,:],pbuf[ps,h+1,:size,:]]),wide(dz[h:h+2]),1,1)
+                dss.append((pbuf[ps,h,:,:size].astype(f32)*dot(daug[h],vct[h,:,osl],1,0)).astype(bf))
+                dkv[W+h*HEAD:W+(h+1)*HEAD,osl]+=dot(lows[h],pbuf[ps,h,:,:size],1,0)
+            for h in range(H): qacc[h]+=dot(kct[h,:,osl],dss[h].T,1,0)
+            for h in range(H):
+                dkv[h*HEAD:(h+1)*HEAD,osl]+=dot(qkv[slot,h*HEAD:(h+1)*HEAD,:],dss[h],1,0)
         g=by_piece(first,full,rest,g,piece)
         @pl.when(i==0)
         def _(): each_key(lambda x:x.wait(),g)
@@ -281,18 +278,18 @@
             hsl=slice(h*HEAD,(h+1)*HEAD); ksl=slice(W+h*HEAD,W+(h+1)*HEAD); vsl=slice(2*W+h*HEAD,2*W+(h+1)*HEAD)
             ps=inv_ref[h,1:2,qsl]
             ds=ps*(jnp.sum(qkv[slot,vsl,:].astype(f32)*d1s[h],0,keepdims=True)-deltas[h])
-            dq[slot,hsl,:]=((qacc[hsl,:]+ds*qkv[slot,ksl,:].astype(f32))*0.125).astype(bf)
+            dq[slot,hsl,:]=((qacc[h]+ds*qkv[slot,ksl,:].astype(f32))*0.125).astype(bf)
             dq[slot,ksl,:]=(ds*qkv[slot,hsl,:].astype(f32)*LN2).astype(bf)
             dq[slot,vsl,:]=(ps*d1s[h]).astype(bf)
         ocopy(i).start()
         return g
     lax.fori_loop(0,nq,block,0)
-    lanes=iota((128,2*W),1)
+    rows=iota((2*W,128),0)
     def tcopy(s): return pltpu.make_async_copy(dkvt.at[:,pl.ds(al(begin(base_ref,s)//128*128,128),SPAN)],dkvw_hbm.at[s],tsem.at[s])
     def turn(j,c):
         jsl=pl.ds(al(j*128,128),128)
-        x=jnp.where(j<groups,dkv[jsl,:],0.0)
-        dkvt[:,jsl]=jnp.where(lanes<W,x*LN2,x).astype(bf).T
+        x=jnp.where(j<groups,dkv[:,jsl],0.0)
+        dkvt[:,jsl]=jnp.where(rows<W,x*LN2,x).astype(bf)
         for s in range(L//256):
             @pl.when(begin(base_ref,s)//128+SPAN//128-1==j)
             def _(): tcopy(s).start()
@@ -301,7 +298,7 @@
     for i in range(max(nq-2,0),nq): ocopy(i).wait()
     for s in range(L//256): tcopy(s).wait()
 
-def back(base,win,datt,p,ot,inv,kct,vaug,qkvt,H):
+def back(base,win,datt,p,ot,inv,kct,vct,qkvt,H):
     L=qkvt.shape[1]; W=H*HEAD
     V=pl.BlockSpec(memory_space=pltpu.VMEM); A=pl.BlockSpec(memory_space=pl.ANY); N=pl.BlockSpec(memory_space=pltpu.SMEM)
     S=jax.ShapeDtypeStruct; M=pltpu.VMEM; D=pltpu.SemaphoreType.DMA
@@ -309,10 +306,10 @@
         out_shape=[S((3*W,L),bf),S((L//256,2*W,SPAN),bf)],
         in_specs=[N,N,A,A,A,V,A,A,A],
         out_specs=[A,A],
-        scratch_shapes=[M((H,L,128),bf),M((H,HEAD,L),bf),M((L+384,2*W),f32),M((2*W,L+384),bf),M((SLOTS,H,KB,QB),bf),M((W,QB),f32),
+        scratch_shapes=[M((H,HEAD,L),bf),M((H,HEAD+16,L),bf),M((2*W,L+SPAN),f32),M((2*W,L+SPAN),bf),M((SLOTS,H,QB,KB),bf),M((H,HEAD,QB),f32),
             M((2,3*W,QB),bf),M((2,W,QB),bf),M((2,W,QB),f32),M((2,3*W,QB),bf),
             D((SLOTS,)),D((2,L//KB)),D((3,2)),D((2,)),D((L//256,))],
-        compiler_params=pltpu.CompilerParams(vmem_limit_bytes=VMEM))(base,win,datt,p,ot,inv,kct,vaug,qkvt)
+        compiler_params=pltpu.CompilerParams(vmem_limit_bytes=VMEM))(base,win,datt,p,ot,inv,kct,vct,qkvt)
 
 def placed(base_ref,rank_row,span,own,s):
     r0=begin(base_ref,s)//128*128
@@ -852,11 +849,11 @@
         bunds=[bund]+[lax.ppermute(bund,"dp",[(d,(d//2+k)%Z*2+d%2) for d in range(dps)]) for k in range(1,Z)]
         across=[(b,b^2) for b in range(4)]
         cotx=lax.ppermute(far,"blk",across)
-        p,att,ot,inv,kct,vaug=attend(base,win,qkvt,codet,meta,H)
+        p,att,ot,inv,kct,vct=attend(base,win,qkvt,codet,meta,H)
         near,far,r1,datt,parts=middle_net(att.reshape(H//2,2,2,block,128),tok,cot,cotx,bunds,Z,W,F)
         parts=lax.all_to_all(parts,"dp",0,0,tiled=True)
         layx=lax.ppermute(far,"blk",across)
-        dq,dkvw=back(base,win,datt,p,ot,inv,kct,vaug,qkvt,H)
+        dq,dkvw=back(base,win,datt,p,ot,inv,kct,vct,qkvt,H)
         tg,grads=reduce(base,meta,dq,dkvw,tok.reshape(L,D),w_mine,r1,parts,Z,W)
         out=finish(near,layx,tg,grads,W,F)
         return (out[0].reshape(tokens.shape),out[1].reshape(tokens.shape))+tuple(out[2:])
@@ -882,7 +879,7 @@
     scale=jnp.where(jnp.arange(3*W)<W,math.log2(math.e)/8,1.0).astype(f32)
     qkvt=(jnp.einsum("ld,de->el",all_tok,w_mine,preferred_element_type=f32)*scale[:,None]).astype(bf)
     base,win,codet,meta=flags(info)
-    p,att,ot,inv,kct,vaug=attend(base,win,qkvt,codet,meta,H)
+    p,att,ot,inv,kct,vct=attend(base,win,qkvt,codet,meta,H)
     att=att.reshape(H//2,J,2,block,128)
     mine=part(att,2,core).reshape(H//2,J*block,128); his=other(part(att,2,1-core)).reshape(H//2,J*block,128)
     a0=jnp.where(core==0,mine,his); a1=jnp.where(core==0,his,mine)
@@ -890,7 +887,7 @@
     da=da.reshape(2,H//2,J,block,128)
     dmine=part(da,0,core); dhis=other(part(da,0,1-core))
     datt=jnp.stack([jnp.where(core==0,dmine,dhis),jnp.where(core==0,dhis,dmine)],2).reshape(H//2,L,128).transpose(0,2,1).reshape(W,L)
-    dq,dkvw=back(base,win,datt,p,ot,inv,kct,vaug,qkvt,H)
+    dq,dkvw=back(base,win,datt,p,ot,inv,kct,vct,qkvt,H)
     tg,gq=place_all(base,meta,dq,dkvw,all_tok,w_mine,H)
     tg=tg.reshape(J,2,block,D)
     layer_out=scatter_units(out.reshape(J,block,D)).reshape(tokens.shape)

time: 309 us -> 307 us (level)
  Pallas kernels: 282 us -> 161 us
  starting transfers between devices: 25.4 us -> 144 us
    pallas_call x1, Pallas kernels: 151 us -> 32.1 us  [attend(): pl.pallas_call(functools.partial(attend_kernel, L, H), out_shape=[S((cap,...]
    all_to_all x1, starting transfers between devices: 20.8 us -> 139 us  [shards(): parts = lax.all_to_all(parts, 'dp', 0, 0, tiled=True)]
  transfers between devices with their start and end apart: 6 -> 6, of which waited for: 0 -> 1; matrix products, arithmetic and copies ran while one was open for 0% -> 0% of each run, Pallas kernels for 73% -> 34%
where the time goes in v5:
time: 307 us; the launch traced here: 306 us
  Pallas kernels  161 us (52%)
  starting transfers between devices  144 us (47%)
    all_to_all x1, starting transfers between devices, shards(): parts = lax.all_to_all(parts, 'dp', 0, 0, tiled=True)  139 us
    pallas_call x1, Pallas kernels, back(): pl.pallas_call(functools.partial(back_kernel, L, H), out_shape=[S((3 * W,...  40.9 us
    pallas_call x1, Pallas kernels, reduce(): pl.pallas_call(functools.partial(reduce_kernel, Z, block, E, W, C1, rows)...  32.7 us
    pallas_call x1, Pallas kernels, gather(): pl.pallas_call(functools.partial(gather_kernel, Z, block, E, W, rows), ou...  32.4 us
    pallas_call x1, Pallas kernels, attend(): pl.pallas_call(functools.partial(attend_kernel, L, H), out_shape=[S((cap,...  32.1 us
    pallas_call x1, Pallas kernels, middle_net(): pl.pallas_call(functools.partial(middle_net_kernel, Z, block, E, F, W, T)...  19.6 us
  transfers between devices with their start and end apart: 6, of which 1 were waited for; matrix products, arithmetic and copies ran while one was open for 0% of the time, Pallas kernels for 34%

profile of v5, /device:TPU:0, one launch (start us, length us, event | category | flops | bytes accessed | tf_op | source)
XLA Modules:
  0.0 306.4 jit_solution(6636589035053516602)
XLA Ops:
  0.6 32.4 %shard_map.170 = (bf16[2,2,768,512]{3,2,1,0:T(8,128)(2,1)}, bf16[2,2,16,1664]{3,2,1,0:T(8,128)(2,1)}, bf16[512,768]{1,0:T(8,128)(2,1)}, bf16[768,3072]{1,0:T(8,1...) custom-call(bf16[2,768,512]{2,1,0:T(8,128)(2,1)} %bitcast.13, ...), custom_call_target="tpu_custom_call" | custom-call | tf_op jit(solution)/shard_map/pallas_call | solution.py:523
  33.0 0.7 collective-permute-start
  33.7 2.8 collective-permute-start.3
  36.6 0.0 collective-permute-start.2
  36.6 1.1 collective-permute-start.1
  37.6 32.1 %shard_map.171 = (bf16[42,4,512,512]{3,2,1,0:T(8,128)(2,1)}, bf16[2,3072,128]{2,1,0:T(8,128)(2,1)}, f32[6,256,512]{2,1,0:T(8,128)}, f32[4,8,3072]{2,1,0:T(8,128)...) custom-call(s32[16,128]{1,0:T(8,128)} %get-tuple-element.40.base_ref, s32[32,128]{1,0:T(8,128)} %get-tuple-element.41.win_ref, ...), custom_call_target="tpu_custom_call" | custom-call | tf_op jit(solution)/shard_map/pallas_call | solution.py:162
  69.8 0.0 collective-permute-done.3.rest_3_
  69.8 0.0 collective-permute-done.2.rest_2_
  69.8 0.0 collective-permute-done.1.rest_1_
  69.8 0.0 collective-permute-done.cotx_hbm
  69.8 19.6 %shard_map.172 = (bf16[768,512]{1,0:T(8,128)(2,1)}, bf16[768,512]{1,0:T(8,128)(2,1)}, bf16[2,768,512]{2,1,0:T(8,128)(2,1)}, bf16[256,3072]{1,0:T(8,128)(2,1)}, bf16[8,64,1664]{2,1,0:T(8,128)(2,1)}) custom-call(bf16[2,2,2,768,128]{4,3,2,1,0:T(8,128)(2,1)} %bitcast.14, bf16[2,2,768,512]{3,2,1,0:T(8,128)(2,1)} %get-tuple-element.46.tok_hbm, ...), custom_call_target="tpu_custom_call" | custom-call | tf_op jit(solution)/shard_map/pallas_call | solution.py:648
  89.4 139.4 %all-to-all-start = ((bf16[8,64,1664]{2,1,0:T(8,128)(2,1)}), bf16[8,64,1664]{2,1,0:T(8,128)(2,1)}, u32[]{:S(2)}, u32[]{:S(2)}) async-start(bf16[8,64,1664]{2,1,0:T(8,128)(2,1)} %get-tuple-element.61), calls=%async_computation | async-start | bytes 3407872 | tf_op jit(solution)/shard_map/all_to_all | solution.py:854
  228.8 0.0 collective-permute-start.4
  228.8 40.9 %shard_map.173 = (bf16[768,3072]{1,0:T(8,128)(2,1)}, bf16[12,512,512]{2,1,0:T(8,128)(2,1)}) custom-call(s32[16,128]{1,0:T(8,128)} %get-tuple-element.40.base_ref, s32[32,128]{1,0:T(8,128)} %get-tuple-element.41.win_ref, bf16[256,3072]{1,0:T(8,128)(2,1)} %get-tuple-element.51.datt_hbm, bf16[42,4,512,512]{3,2,1,0:T(8,128)(2,1)} %get-tuple-element.52.p_hbm, ...), custom_call_target="tpu_custom_call" | custom-call | tf_op jit(solution)/shard_map/pallas_call | solution.py:305
  269.7 0.4 all-to-all-done.parts_hbm
  270.0 32.7 %shard_map.174 = (bf16[2,768,512]{2,1,0:T(8,128)(2,1)}, f32[16,3200]{1,0:T(8,128)}) custom-call(s32[16,128]{1,0:T(8,128)} %get-tuple-element.40.base_ref, s32[8,3072]{1,0:T(8,128)} %get-tuple-element.44.meta_ref, bf16[768,3072]{1,0:T(8,128)(2,1)} %get-tuple-element.57.dq_hbm, bf16[12,512,512]{2,1,0:T(8,128)(2,1)} %get-tuple-element.58.dkvw_hbm, ...), custom_call_target="tpu_custom_call" | custom-call | tf_op jit(solution)/shard_map/pallas_call | solution.py:794
  302.7 0.0 collective-permute-done.4.far
  302.7 3.5 %shard_map.175 = (bf16[2,768,512]{2,1,0:T(8,128)(2,1)}, bf16[2,768,512]{2,1,0:T(8,128)(2,1)}, f32[16,1536]{1,0:T(8,128)}, f32[16,512]{1,0:T(8,128)}, f32[16,512]...) custom-call(bf16[768,512]{1,0:T(8,128)(2,1)} %get-tuple-element.49.near, ...), custom_call_target="tpu_custom_call" | custom-call | tf_op jit(solution)/shard_map/pallas_call | solution.py:832
Async XLA Ops:
  33.0 36.8 %collective-permute-start = (bf16[768,512]{1,0:T(8,128)(2,1)}, bf16[768,512]{1,0:T(8,128)(2,1)}, u32[]{:S(2)}, u32[]{:S(2)}) collective-permute-start(bf16[768,512]{1,0:T(8,128)(2,1)} %get-tuple-element.47), channel_id=1, source_target_pairs={{0,2},{1,3},{2,0},{3,1},{4,6},{5,7},{6,4},{7,5},{8,10},{9,11},{10,... | collective-permute-start | bytes 2359304 | tf_op jit(solution)/shard_map/ppermute | solution.py:851
  33.7 36.0 %collective-permute-start.3 = (bf16[2,2,16,1664]{3,2,1,0:T(8,128)(2,1)}, bf16[2,2,16,1664]{3,2,1,0:T(8,128)(2,1)}, u32[]{:S(2)}, u32[]{:S(2)}) collective-permute-start(bf16[2,2,16,1664]{3,2,1,0:T(8,128)(2,1)} %get-tuple-element.48.rest_0_), channel_id=1, source_target_pairs={{0,24},{4,28},{8,0},{12,4},{16,8},{20,12},{24,16},{28,20},{1,25},{... | collective-permute-start | bytes 638984 | tf_op jit(solution)/shard_map/ppermute | solution.py:849
  36.6 33.2 %collective-permute-start.2 = (bf16[2,2,16,1664]{3,2,1,0:T(8,128)(2,1)}, bf16[2,2,16,1664]{3,2,1,0:T(8,128)(2,1)}, u32[]{:S(2)}, u32[]{:S(2)}) collective-permute-start(bf16[2,2,16,1664]{3,2,1,0:T(8,128)(2,1)} %get-tuple-element.48.rest_0_), channel_id=1, source_target_pairs={{0,16},{4,20},{8,24},{12,28},{16,0},{20,4},{24,8},{28,12},{1,17},{... | collective-permute-start | bytes 638984 | tf_op jit(solution)/shard_map/ppermute | solution.py:849
  36.6 33.2 %collective-permute-start.1 = (bf16[2,2,16,1664]{3,2,1,0:T(8,128)(2,1)}, bf16[2,2,16,1664]{3,2,1,0:T(8,128)(2,1)}, u32[]{:S(2)}, u32[]{:S(2)}) collective-permute-start(bf16[2,2,16,1664]{3,2,1,0:T(8,128)(2,1)} %get-tuple-element.48.rest_0_), channel_id=1, source_target_pairs={{0,8},{4,12},{8,16},{12,20},{16,24},{20,28},{24,0},{28,4},{1,9},{5... | collective-permute-start | bytes 638984 | tf_op jit(solution)/shard_map/ppermute | solution.py:849
  89.4 180.6 %all-to-all-start = ((bf16[8,64,1664]{2,1,0:T(8,128)(2,1)}), bf16[8,64,1664]{2,1,0:T(8,128)(2,1)}, u32[]{:S(2)}, u32[]{:S(2)}) async-start(bf16[8,64,1664]{2,1,0:T(8,128)(2,1)} %get-tuple-element.61), calls=%async_computation | async-start | bytes 3407872 | tf_op jit(solution)/shard_map/all_to_all | solution.py:854
  228.8 74.0 %collective-permute-start.4 = (bf16[768,512]{1,0:T(8,128)(2,1)}, bf16[768,512]{1,0:T(8,128)(2,1)}, u32[]{:S(2)}, u32[]{:S(2)}) collective-permute-start(bf16[768,512]{1,0:T(8,128)(2,1)} %get-tuple-element.50), channel_id=1, source_target_pairs={{0,2},{1,3},{2,0},{3,1},{4,6},{5,7},{6,4},{7,5},{8,10},{9,11},{10,... | collective-permute-start | bytes 2359304 | tf_op jit(solution)/shard_map/ppermute | solution.py:855

commit v6 on v5

--- a/solution.py
+++ b/solution.py
@@ -10,8 +10,9 @@
 HEAD=64
 QB=512
 KB=512
-SRC=1024
+SRC=768
 SAFE=60.0
+RATE=math.log2(math.e)*HEAD**-0.5
 CODE=16
 VMEM=(64<<20)-(128<<10)
 SLOTS=3
@@ -64,7 +65,7 @@
         ka,va=lax.fori_loop(1,(last-first+SRC-1)//SRC,src,(ka,va))
         dsl=pl.ds(al(d*256,256),256)
         for h in range(H):
-            k1=jnp.where(row[:128]==HEAD+10,-2560.0,ka[h*128:(h+1)*128])
+            k1=jnp.where(row[:128]==HEAD+10,-10240.0,ka[h*128:(h+1)*128])
             kaug_ref[h,dsl,:]=k1.astype(bf).T
             kct_ref[h,:,dsl]=k1[:HEAD].astype(bf)
             vct[h,:HEAD,dsl]=va[h*HEAD:(h+1)*HEAD].astype(bf)
@@ -77,7 +78,7 @@
     for h in range(H):
         q=q_ref[h*HEAD:(h+1)*HEAD,:].astype(f32); k=kvt[h*128:h*128+HEAD,:].astype(f32)
         bound=jnp.maximum(bound,jnp.max(jnp.sum(q*q,0,keepdims=True))*jnp.max(jnp.sum(k*k,0,keepdims=True)))
-    safe=bound<SAFE*SAFE
+    safe=bound*(RATE*RATE)<SAFE*SAFE
 
     def pcopy(g):
         slot=lax.rem(g,SLOTS)
@@ -120,7 +121,7 @@
             def _():
                 keepp=[]
                 for h in range(H):
-                    p=jnp.exp2(dot(kaug_ref[h,osl,:],qa[h],1,0)).astype(bf)
+                    p=jnp.exp2(RATE*dot(kaug_ref[h,osl,:],qa[h],1,0)).astype(bf)
                     pbuf[ps,h,:,:size]=p.T
                     keepp.append(p)
                 for h in range(H): acc[h]+=dot(vct[h,:,osl],keepp[h],1,0)
@@ -129,7 +130,7 @@
                 for h in range(H):
                     def put(j,c):
                         jsl=pl.ds(al(off+j*128,128),128)
-                        p=jnp.exp2(strict(h,jsl)-top_ref[h:h+1,:]).astype(bf)
+                        p=jnp.exp2(RATE*(strict(h,jsl)-top_ref[h:h+1,:])).astype(bf)
                         pbuf[ps,h,:,pl.ds(al(j*128,128),128)]=p.T
                         acc[h]+=dot(vct[h,:,jsl],p,1,0)
                         return c
@@ -139,7 +140,7 @@
         @pl.when(i>=2)
         def _(): ocopy(i-2).wait(); acopy(i-2).wait()
         for h in range(H):
-            ps=jnp.exp2(sself[h]-top_ref[h:h+1,:])
+            ps=jnp.exp2(RATE*(sself[h]-top_ref[h:h+1,:]))
             inv=1.0/(acc[h,HEAD:HEAD+1,:]+ps)
             obuf[slot,h*HEAD:(h+1)*HEAD,:]=(acc[h,:HEAD,:]+ps*v_ref[h*HEAD:(h+1)*HEAD,qsl].astype(f32))*inv
             inv_ref[h,0:1,qsl]=inv
@@ -189,7 +190,7 @@
     own=((pad==0)&(known!=1)).astype(jnp.int32)
     bits=iota((CODE,L),0)
     bit=lax.shift_right_logical(jnp.broadcast_to(seg,(CODE,L)),jnp.minimum(bits,9))&1
-    codet=jnp.where(bits<10,jnp.where(bit==1,16.0,-16.0),jnp.where(bits==10,1.0,0.0)).astype(bf)
+    codet=jnp.where(bits<10,jnp.where(bit==1,32.0,-32.0),jnp.where(bits==10,1.0,0.0)).astype(bf)
     meta=jnp.concatenate([rank,own,jnp.zeros((6,L),jnp.int32)],0)
     def edge(at): return jnp.concatenate([seg[:,i*QB+at:i*QB+at+1] for i in range(nq)]+[jnp.zeros((8-nq,1),jnp.int32)],0)
     low=jnp.sum(jnp.where(seg<edge(0),usef,0.0),1,keepdims=True)+shift*(edge(0)>=mid).astype(f32)
@@ -197,7 +198,6 @@
     starts=jnp.sum((csum<=(256*iota((16,1),0)).astype(f32)).astype(f32),1,keepdims=True)
     win=jnp.broadcast_to(jnp.concatenate([low,high,starts],0),(32,128)).astype(jnp.int32)
     return base[:,:128].astype(jnp.int32),win,codet,meta
-LN2=math.log(2.0)
 SPAN=512
 def back_kernel(L,H,base_ref,win_ref,datt_hbm,p_hbm,ot_hbm,inv_ref,kct_hbm,vct_hbm,qkvt_hbm,dq_hbm,dkvw_hbm,
                 kct,vct,dkv,dkvt,pbuf,qacc,qkv,datt,ot,dq,psem,lsem,qsem,osem,tsem):
@@ -278,8 +278,8 @@
             hsl=slice(h*HEAD,(h+1)*HEAD); ksl=slice(W+h*HEAD,W+(h+1)*HEAD); vsl=slice(2*W+h*HEAD,2*W+(h+1)*HEAD)
             ps=inv_ref[h,1:2,qsl]
             ds=ps*(jnp.sum(qkv[slot,vsl,:].astype(f32)*d1s[h],0,keepdims=True)-deltas[h])
-            dq[slot,hsl,:]=((qacc[h]+ds*qkv[slot,ksl,:].astype(f32))*0.125).astype(bf)
-            dq[slot,ksl,:]=(ds*qkv[slot,hsl,:].astype(f32)*LN2).astype(bf)
+            dq[slot,hsl,:]=((qacc[h]+ds*qkv[slot,ksl,:].astype(f32))*HEAD**-0.5).astype(bf)
+            dq[slot,ksl,:]=(ds*qkv[slot,hsl,:].astype(f32)*HEAD**-0.5).astype(bf)
             dq[slot,vsl,:]=(ps*d1s[h]).astype(bf)
         ocopy(i).start()
         return g
@@ -289,7 +289,7 @@
     def turn(j,c):
         jsl=pl.ds(al(j*128,128),128)
         x=jnp.where(j<groups,dkv[:,jsl],0.0)
-        dkvt[:,jsl]=jnp.where(rows<W,x*LN2,x).astype(bf)
+        dkvt[:,jsl]=jnp.where(rows<W,x*HEAD**-0.5,x).astype(bf)
         for s in range(L//256):
             @pl.when(begin(base_ref,s)//128+SPAN//128-1==j)
             def _(): tcopy(s).start()
@@ -486,7 +486,7 @@
             if onward: net.copy(ref,ref,ts.at[2,k],tr.at[2,k],sib).start()
             g=(jj*2+cc)*NCH+k
             r=dot(wt[...],ref[...],1,1)
-            qkvt[:,pl.ds(al(g*rows,rows),rows)]=jnp.concatenate([r[:W]*(math.log2(math.e)/8),r[W:]],0).astype(bf)
+            qkvt[:,pl.ds(al(g*rows,rows),rows)]=r.astype(bf)
             qcopy(g).start()
             return carry
         lax.fori_loop(0,NCH,body,0)
@@ -876,8 +876,7 @@
     gs=lax.all_gather(jnp.concatenate([norm_gains,norm_shifts],0),("dp","blk"),axis=1,tiled=True).astype(f32)
     gs=jnp.concatenate([gs,jnp.zeros_like(gs)],0)
     w_mine=part(full_qkv.reshape(D,3,2,W),2,core).reshape(D,3*W)
-    scale=jnp.where(jnp.arange(3*W)<W,math.log2(math.e)/8,1.0).astype(f32)
-    qkvt=(jnp.einsum("ld,de->el",all_tok,w_mine,preferred_element_type=f32)*scale[:,None]).astype(bf)
+    qkvt=jnp.einsum("ld,de->el",all_tok,w_mine,preferred_element_type=f32).astype(bf)
     base,win,codet,meta=flags(info)
     p,att,ot,inv,kct,vct=attend(base,win,qkvt,codet,meta,H)
     att=att.reshape(H//2,J,2,block,128)

time: 307 us -> 309 us (level)
  Pallas kernels: 161 us -> 284 us
  starting transfers between devices: 144 us -> 25.6 us
    pallas_call x1, Pallas kernels: 32.1 us -> 154 us  [attend(): pl.pallas_call(functools.partial(attend_kernel, L, H), out_shape=[S((cap,...]
    all_to_all x1, starting transfers between devices: 139 us -> 19.8 us  [shards(): parts = lax.all_to_all(parts, 'dp', 0, 0, tiled=True)]
  transfers between devices with their start and end apart: 6 -> 6, of which waited for: 1 -> 0; matrix products, arithmetic and copies ran while one was open for 0% -> 0% of each run, Pallas kernels for 34% -> 74%
where the time goes in v6:
time: 309 us; the launch traced here: 310 us
  Pallas kernels  284 us (92%)
  starting transfers between devices  25.6 us (8%)
    pallas_call x1, Pallas kernels, attend(): pl.pallas_call(functools.partial(attend_kernel, L, H), out_shape=[S((cap,...  154 us
    pallas_call x1, Pallas kernels, back(): pl.pallas_call(functools.partial(back_kernel, L, H), out_shape=[S((3 * W,...  40.9 us
    pallas_call x1, Pallas kernels, reduce(): pl.pallas_call(functools.partial(reduce_kernel, Z, block, E, W, C1, rows)...  33.9 us
    pallas_call x1, Pallas kernels, gather(): pl.pallas_call(functools.partial(gather_kernel, Z, block, E, W, rows), ou...  32.4 us
    all_to_all x1, starting transfers between devices, shards(): parts = lax.all_to_all(parts, 'dp', 0, 0, tiled=True)  19.8 us
    pallas_call x1, Pallas kernels, middle_net(): pl.pallas_call(functools.partial(middle_net_kernel, Z, block, E, F, W, T)...  19.6 us
  transfers between devices with their start and end apart: 6, of which 0 were waited for; matrix products, arithmetic and copies ran while one was open for 0% of the time, Pallas kernels for 74%

profile of v6, /device:TPU:0, one launch (start us, length us, event | category | flops | bytes accessed | tf_op | source)
XLA Modules:
  0.0 310.3 jit_solution(1933406916592725786)
XLA Ops:
  0.6 32.4 %shard_map.170 = (bf16[2,2,768,512]{3,2,1,0:T(8,128)(2,1)}, bf16[2,2,16,1664]{3,2,1,0:T(8,128)(2,1)}, bf16[512,768]{1,0:T(8,128)(2,1)}, bf16[768,3072]{1,0:T(8,1...) custom-call(bf16[2,768,512]{2,1,0:T(8,128)(2,1)} %bitcast.13, ...), custom_call_target="tpu_custom_call" | custom-call | tf_op jit(solution)/shard_map/pallas_call | solution.py:523
  33.0 0.7 collective-permute-start
  33.7 2.8 collective-permute-start.3
  36.5 0.0 collective-permute-start.2
  36.5 1.1 collective-permute-start.1
  37.7 153.6 %shard_map.171 = (bf16[42,4,512,512]{3,2,1,0:T(8,128)(2,1)}, bf16[2,3072,128]{2,1,0:T(8,128)(2,1)}, f32[6,256,512]{2,1,0:T(8,128)}, f32[4,8,3072]{2,1,0:T(8,128)...) custom-call(s32[16,128]{1,0:T(8,128)} %get-tuple-element.40.base_ref, s32[32,128]{1,0:T(8,128)} %get-tuple-element.41.win_ref, ...), custom_call_target="tpu_custom_call" | custom-call | tf_op jit(solution)/shard_map/pallas_call | solution.py:163
  191.2 0.0 collective-permute-done.3.rest_3_
  191.2 0.0 collective-permute-done.2.rest_2_
  191.3 0.0 collective-permute-done.1.rest_1_
  191.3 0.0 collective-permute-done.cotx_hbm
  191.3 19.6 %shard_map.172 = (bf16[768,512]{1,0:T(8,128)(2,1)}, bf16[768,512]{1,0:T(8,128)(2,1)}, bf16[2,768,512]{2,1,0:T(8,128)(2,1)}, bf16[256,3072]{1,0:T(8,128)(2,1)}, bf16[8,64,1664]{2,1,0:T(8,128)(2,1)}) custom-call(bf16[2,2,2,768,128]{4,3,2,1,0:T(8,128)(2,1)} %bitcast.14, bf16[2,2,768,512]{3,2,1,0:T(8,128)(2,1)} %get-tuple-element.46.tok_hbm, ...), custom_call_target="tpu_custom_call" | custom-call | tf_op jit(solution)/shard_map/pallas_call | solution.py:648
  210.9 19.8 %all-to-all-start = ((bf16[8,64,1664]{2,1,0:T(8,128)(2,1)}), bf16[8,64,1664]{2,1,0:T(8,128)(2,1)}, u32[]{:S(2)}, u32[]{:S(2)}) async-start(bf16[8,64,1664]{2,1,0:T(8,128)(2,1)} %get-tuple-element.61), calls=%async_computation | async-start | bytes 3407872 | tf_op jit(solution)/shard_map/all_to_all | solution.py:854
  230.7 1.2 collective-permute-start.4
  231.9 40.9 %shard_map.173 = (bf16[768,3072]{1,0:T(8,128)(2,1)}, bf16[12,512,512]{2,1,0:T(8,128)(2,1)}) custom-call(s32[16,128]{1,0:T(8,128)} %get-tuple-element.40.base_ref, s32[32,128]{1,0:T(8,128)} %get-tuple-element.41.win_ref, bf16[256,3072]{1,0:T(8,128)(2,1)} %get-tuple-element.51.datt_hbm, bf16[42,4,512,512]{3,2,1,0:T(8,128)(2,1)} %get-tuple-element.52.p_hbm, ...), custom_call_target="tpu_custom_call" | custom-call | tf_op jit(solution)/shard_map/pallas_call | solution.py:305
  272.8 0.0 all-to-all-done.parts_hbm
  272.8 33.9 %shard_map.174 = (bf16[2,768,512]{2,1,0:T(8,128)(2,1)}, f32[16,3200]{1,0:T(8,128)}) custom-call(s32[16,128]{1,0:T(8,128)} %get-tuple-element.40.base_ref, s32[8,3072]{1,0:T(8,128)} %get-tuple-element.44.meta_ref, bf16[768,3072]{1,0:T(8,128)(2,1)} %get-tuple-element.57.dq_hbm, bf16[12,512,512]{2,1,0:T(8,128)(2,1)} %get-tuple-element.58.dkvw_hbm, ...), custom_call_target="tpu_custom_call" | custom-call | tf_op jit(solution)/shard_map/pallas_call | solution.py:794
  306.6 0.0 collective-permute-done.4.far
  306.7 3.5 %shard_map.175 = (bf16[2,768,512]{2,1,0:T(8,128)(2,1)}, bf16[2,768,512]{2,1,0:T(8,128)(2,1)}, f32[16,1536]{1,0:T(8,128)}, f32[16,512]{1,0:T(8,128)}, f32[16,512]...) custom-call(bf16[768,512]{1,0:T(8,128)(2,1)} %get-tuple-element.49.near, ...), custom_call_target="tpu_custom_call" | custom-call | tf_op jit(solution)/shard_map/pallas_call | solution.py:832
Async XLA Ops:
  33.0 158.2 %collective-permute-start = (bf16[768,512]{1,0:T(8,128)(2,1)}, bf16[768,512]{1,0:T(8,128)(2,1)}, u32[]{:S(2)}, u32[]{:S(2)}) collective-permute-start(bf16[768,512]{1,0:T(8,128)(2,1)} %get-tuple-element.47), channel_id=1, source_target_pairs={{0,2},{1,3},{2,0},{3,1},{4,6},{5,7},{6,4},{7,5},{8,10},{9,11},{10,... | collective-permute-start | bytes 2359304 | tf_op jit(solution)/shard_map/ppermute | solution.py:851
  33.7 157.5 %collective-permute-start.3 = (bf16[2,2,16,1664]{3,2,1,0:T(8,128)(2,1)}, bf16[2,2,16,1664]{3,2,1,0:T(8,128)(2,1)}, u32[]{:S(2)}, u32[]{:S(2)}) collective-permute-start(bf16[2,2,16,1664]{3,2,1,0:T(8,128)(2,1)} %get-tuple-element.48.rest_0_), channel_id=1, source_target_pairs={{0,24},{4,28},{8,0},{12,4},{16,8},{20,12},{24,16},{28,20},{1,25},{... | collective-permute-start | bytes 638984 | tf_op jit(solution)/shard_map/ppermute | solution.py:849
  36.5 154.7 %collective-permute-start.2 = (bf16[2,2,16,1664]{3,2,1,0:T(8,128)(2,1)}, bf16[2,2,16,1664]{3,2,1,0:T(8,128)(2,1)}, u32[]{:S(2)}, u32[]{:S(2)}) collective-permute-start(bf16[2,2,16,1664]{3,2,1,0:T(8,128)(2,1)} %get-tuple-element.48.rest_0_), channel_id=1, source_target_pairs={{0,16},{4,20},{8,24},{12,28},{16,0},{20,4},{24,8},{28,12},{1,17},{... | collective-permute-start | bytes 638984 | tf_op jit(solution)/shard_map/ppermute | solution.py:849
  36.5 154.7 %collective-permute-start.1 = (bf16[2,2,16,1664]{3,2,1,0:T(8,128)(2,1)}, bf16[2,2,16,1664]{3,2,1,0:T(8,128)(2,1)}, u32[]{:S(2)}, u32[]{:S(2)}) collective-permute-start(bf16[2,2,16,1664]{3,2,1,0:T(8,128)(2,1)} %get-tuple-element.48.rest_0_), channel_id=1, source_target_pairs={{0,8},{4,12},{8,16},{12,20},{16,24},{20,28},{24,0},{28,4},{1,9},{5... | collective-permute-start | bytes 638984 | tf_op jit(solution)/shard_map/ppermute | solution.py:849
  210.9 61.9 %all-to-all-start = ((bf16[8,64,1664]{2,1,0:T(8,128)(2,1)}), bf16[8,64,1664]{2,1,0:T(8,128)(2,1)}, u32[]{:S(2)}, u32[]{:S(2)}) async-start(bf16[8,64,1664]{2,1,0:T(8,128)(2,1)} %get-tuple-element.61), calls=%async_computation | async-start | bytes 3407872 | tf_op jit(solution)/shard_map/all_to_all | solution.py:854
  230.7 75.9 %collective-permute-start.4 = (bf16[768,512]{1,0:T(8,128)(2,1)}, bf16[768,512]{1,0:T(8,128)(2,1)}, u32[]{:S(2)}, u32[]{:S(2)}) collective-permute-start(bf16[768,512]{1,0:T(8,128)(2,1)} %get-tuple-element.50), channel_id=1, source_target_pairs={{0,2},{1,3},{2,0},{3,1},{4,6},{5,7},{6,4},{7,5},{8,10},{9,11},{10,... | collective-permute-start | bytes 2359304 | tf_op jit(solution)/shard_map/ppermute | solution.py:855

commit v7 on v6

--- a/solution.py
+++ b/solution.py
@@ -15,7 +15,7 @@
 RATE=math.log2(math.e)*HEAD**-0.5
 CODE=16
 VMEM=(64<<20)-(128<<10)
-SLOTS=3
+SLOTS=4
 def dot(a,b,ca,cb): return lax.dot_general(a,b,(((ca,),(cb,)),((),())),preferred_element_type=f32)
 def al(x,n): return pl.multiple_of(x,n)
 def iota(shape,axis): return lax.broadcasted_iota(jnp.int32,shape,axis)
@@ -43,14 +43,18 @@
                   kaug_ref,kct_ref,kvt,q_ref,v_ref,vct,acc,pbuf,obuf,abuf,top_ref,psem,osem,asem,ksem,lsem):
     W=H*HEAD; nq=L//QB
     total=begin(base_ref,L//256)
-    come=[pltpu.make_async_copy(qkvt_hbm.at[W+h*HEAD:W+(h+1)*HEAD],kvt.at[h*128:h*128+HEAD],lsem.at[h]) for h in range(H)]
-    come+=[pltpu.make_async_copy(qkvt_hbm.at[2*W:],v_ref,lsem.at[H]),pltpu.make_async_copy(qkvt_hbm.at[:W],q_ref,lsem.at[H+1])]
-    for x in come: x.start()
+    third=L//3
+    def part(t):
+        cols=slice(t*third,(t+1)*third)
+        x=[pltpu.make_async_copy(qkvt_hbm.at[W+h*HEAD:W+(h+1)*HEAD,cols],kvt.at[h*128:h*128+HEAD,cols],lsem.at[t,h]) for h in range(H)]
+        return x+[pltpu.make_async_copy(qkvt_hbm.at[2*W:,cols],v_ref.at[:,cols],lsem.at[t,H])]
+    for t in range(3):
+        for x in part(t): x.start()
+    queries=pltpu.make_async_copy(qkvt_hbm.at[:W],q_ref,lsem.at[0,H+1]); queries.start()
     for h in range(H):
         kvt[h*128+HEAD:h*128+HEAD+CODE,:]=codet_ref[...]
         kvt[h*128+HEAD+CODE:(h+1)*128,:]=jnp.zeros((HEAD-CODE,L),bf)
     vct[:,HEAD:,:]=jnp.ones((H,16,L),bf)
-    for x in come[:H+1]: x.wait()
     row=iota((256,256),0)
     down=iota((256,SRC),0)
     def dest(d,c):
@@ -61,6 +65,11 @@
             oh=((meta_ref[0:1,ssl]==down+d*256)&(lane>=first+t*SRC-jnp.minimum(first+t*SRC,L-SRC))).astype(f32).astype(bf)
             return a[0]+dot(kvt[:,ssl],oh,1,1),a[1]+dot(v_ref[:,ssl],oh,1,1)
         lane=iota((256,SRC),1)
+        reach=jnp.minimum(first+jnp.maximum((last-first+SRC-1)//SRC,1)*SRC,L)
+        for t in range(3):
+            @pl.when((c<=t)&(reach>t*third))
+            def _():
+                for x in part(t): x.wait()
         ka,va=src(0,(jnp.zeros((H*128,256),f32),jnp.zeros((W,256),f32)))
         ka,va=lax.fori_loop(1,(last-first+SRC-1)//SRC,src,(ka,va))
         dsl=pl.ds(al(d*256,256),256)
@@ -69,11 +78,15 @@
             kaug_ref[h,dsl,:]=k1.astype(bf).T
             kct_ref[h,:,dsl]=k1[:HEAD].astype(bf)
             vct[h,:HEAD,dsl]=va[h*HEAD:(h+1)*HEAD].astype(bf)
-        return c
-    lax.fori_loop(0,(total+255)//256,dest,0)
+        return jnp.maximum(c,(reach+third-1)//third)
+    ready=lax.fori_loop(0,(total+255)//256,dest,0)
+    for t in range(3):
+        @pl.when(ready<=t)
+        def _():
+            for x in part(t): x.wait()
     keep=[pltpu.make_async_copy(kct_ref,kct_hbm,ksem.at[0]),pltpu.make_async_copy(vct,vct_hbm,ksem.at[1])]
     for x in keep: x.start()
-    come[H+1].wait()
+    queries.wait()
     bound=jnp.float32(0)
     for h in range(H):
         q=q_ref[h*HEAD:(h+1)*HEAD,:].astype(f32); k=kvt[h*128:h*128+HEAD,:].astype(f32)
@@ -157,7 +170,7 @@
     for x in keep: x.wait()
 
 def attend(base,win,qkvt,codet,meta,H):
-    L=qkvt.shape[1]; W=H*HEAD; nq=L//QB; cap=nq*(L//KB+1)
+    L=qkvt.shape[1]; W=H*HEAD; nq=L//QB; cap=nq*((L+KB-1)//KB)
     V=pl.BlockSpec(memory_space=pltpu.VMEM); A=pl.BlockSpec(memory_space=pl.ANY)
     S=jax.ShapeDtypeStruct; M=pltpu.VMEM; D=pltpu.SemaphoreType.DMA
     return pl.pallas_call(functools.partial(attend_kernel,L,H),
@@ -165,7 +178,7 @@
         in_specs=[pl.BlockSpec(memory_space=pltpu.SMEM)]*2+[A,V,V],
         out_specs=[A,A,A,V,A,A],
         scratch_shapes=[M((H,L,128),bf),M((H,HEAD,L),bf),M((H*128,L),bf),M((W,L),bf),M((W,L),bf),M((H,HEAD+16,L),bf),M((H,HEAD+16,QB),f32),M((SLOTS,H,QB,KB),bf),
-            M((2,W,QB),f32),M((2,H//2,QB,128),bf),M((8,QB),f32),D((SLOTS,)),D((2,)),D((2,)),D((2,)),D((H+2,))],
+            M((2,W,QB),f32),M((2,H//2,QB,128),bf),M((8,QB),f32),D((SLOTS,)),D((2,)),D((2,)),D((2,)),D((3,H+2))],
         compiler_params=pltpu.CompilerParams(vmem_limit_bytes=VMEM))(base,win,qkvt,codet,meta)
 
 def flags(row):

time: 309 us -> 310 us (level)
  Pallas kernels: 284 us -> 268 us
  starting transfers between devices: 25.6 us -> 40.3 us
    all_to_all x1, starting transfers between devices: 19.8 us -> 34.7 us  [shards(): parts = lax.all_to_all(parts, 'dp', 0, 0, tiled=True)]
    pallas_call x1, Pallas kernels: 154 us -> 140 us  [attend(): pl.pallas_call(functools.partial(attend_kernel, L, H), out_shape=[S((cap,...]
    pallas_call x1, Pallas kernels: 40.9 us -> 37.6 us  [back(): pl.pallas_call(functools.partial(back_kernel, L, H), out_shape=[S((3 * W,...]
  transfers between devices with their start and end apart: 6 -> 6, of which waited for: 0 -> 1; matrix products, arithmetic and copies ran while one was open for 0% -> 0% of each run, Pallas kernels for 74% -> 68%
where the time goes in v7:
time: 310 us; the launch traced here: 311 us
  Pallas kernels  268 us (86%)
  starting transfers between devices  40.3 us (13%)
    pallas_call x1, Pallas kernels, attend(): pl.pallas_call(functools.partial(attend_kernel, L, H), out_shape=[S((cap,...  140 us
    pallas_call x1, Pallas kernels, back(): pl.pallas_call(functools.partial(back_kernel, L, H), out_shape=[S((3 * W,...  37.6 us
    pallas_call x1, Pallas kernels, reduce(): pl.pallas_call(functools.partial(reduce_kernel, Z, block, E, W, C1, rows)...  34.9 us
    all_to_all x1, starting transfers between devices, shards(): parts = lax.all_to_all(parts, 'dp', 0, 0, tiled=True)  34.7 us
    pallas_call x1, Pallas kernels, gather(): pl.pallas_call(functools.partial(gather_kernel, Z, block, E, W, rows), ou...  32.6 us
    pallas_call x1, Pallas kernels, middle_net(): pl.pallas_call(functools.partial(middle_net_kernel, Z, block, E, F, W, T)...  19.6 us
  transfers between devices with their start and end apart: 6, of which 1 were waited for; matrix products, arithmetic and copies ran while one was open for 0% of the time, Pallas kernels for 68%

profile of v7, /device:TPU:0, one launch (start us, length us, event | category | flops | bytes accessed | tf_op | source)
XLA Modules:
  0.0 311.0 jit_solution(11771509570912491444)
XLA Ops:
  0.6 32.6 %shard_map.170 = (bf16[2,2,768,512]{3,2,1,0:T(8,128)(2,1)}, bf16[2,2,16,1664]{3,2,1,0:T(8,128)(2,1)}, bf16[512,768]{1,0:T(8,128)(2,1)}, bf16[768,3072]{1,0:T(8,1...) custom-call(bf16[2,768,512]{2,1,0:T(8,128)(2,1)} %bitcast.13, ...), custom_call_target="tpu_custom_call" | custom-call | tf_op jit(solution)/shard_map/pallas_call | solution.py:536
  33.2 0.5 collective-permute-start
  33.7 2.8 collective-permute-start.3
  36.5 0.0 collective-permute-start.2
  36.5 1.1 collective-permute-start.1
  37.7 140.0 %shard_map.171 = (bf16[36,4,512,512]{3,2,1,0:T(8,128)(2,1)}, bf16[2,3072,128]{2,1,0:T(8,128)(2,1)}, f32[6,256,512]{2,1,0:T(8,128)}, f32[4,8,3072]{2,1,0:T(8,128)...) custom-call(s32[16,128]{1,0:T(8,128)} %get-tuple-element.40.base_ref, s32[32,128]{1,0:T(8,128)} %get-tuple-element.41.win_ref, ...), custom_call_target="tpu_custom_call" | custom-call | tf_op jit(solution)/shard_map/pallas_call | solution.py:176
  177.7 0.0 collective-permute-done.3.rest_3_
  177.7 0.0 collective-permute-done.2.rest_2_
  177.7 0.0 collective-permute-done.1.rest_1_
  177.7 0.0 collective-permute-done.cotx_hbm
  177.7 19.6 %shard_map.172 = (bf16[768,512]{1,0:T(8,128)(2,1)}, bf16[768,512]{1,0:T(8,128)(2,1)}, bf16[2,768,512]{2,1,0:T(8,128)(2,1)}, bf16[256,3072]{1,0:T(8,128)(2,1)}, bf16[8,64,1664]{2,1,0:T(8,128)(2,1)}) custom-call(bf16[2,2,2,768,128]{4,3,2,1,0:T(8,128)(2,1)} %bitcast.14, bf16[2,2,768,512]{3,2,1,0:T(8,128)(2,1)} %get-tuple-element.46.tok_hbm, ...), custom_call_target="tpu_custom_call" | custom-call | tf_op jit(solution)/shard_map/pallas_call | solution.py:661
  197.3 34.7 %all-to-all-start = ((bf16[8,64,1664]{2,1,0:T(8,128)(2,1)}), bf16[8,64,1664]{2,1,0:T(8,128)(2,1)}, u32[]{:S(2)}, u32[]{:S(2)}) async-start(bf16[8,64,1664]{2,1,0:T(8,128)(2,1)} %get-tuple-element.61), calls=%async_computation | async-start | bytes 3407872 | tf_op jit(solution)/shard_map/all_to_all | solution.py:867
  232.0 1.2 collective-permute-start.4
  233.2 37.6 %shard_map.173 = (bf16[768,3072]{1,0:T(8,128)(2,1)}, bf16[12,512,512]{2,1,0:T(8,128)(2,1)}) custom-call(s32[16,128]{1,0:T(8,128)} %get-tuple-element.40.base_ref, s32[32,128]{1,0:T(8,128)} %get-tuple-element.41.win_ref, bf16[256,3072]{1,0:T(8,128)(2,1)} %get-tuple-element.51.datt_hbm, bf16[36,4,512,512]{3,2,1,0:T(8,128)(2,1)} %get-tuple-element.52.p_hbm, ...), custom_call_target="tpu_custom_call" | custom-call | tf_op jit(solution)/shard_map/pallas_call | solution.py:318
  270.8 1.6 all-to-all-done.parts_hbm
  272.4 34.9 %shard_map.174 = (bf16[2,768,512]{2,1,0:T(8,128)(2,1)}, f32[16,3200]{1,0:T(8,128)}) custom-call(s32[16,128]{1,0:T(8,128)} %get-tuple-element.40.base_ref, s32[8,3072]{1,0:T(8,128)} %get-tuple-element.44.meta_ref, bf16[768,3072]{1,0:T(8,128)(2,1)} %get-tuple-element.57.dq_hbm, bf16[12,512,512]{2,1,0:T(8,128)(2,1)} %get-tuple-element.58.dkvw_hbm, ...), custom_call_target="tpu_custom_call" | custom-call | tf_op jit(solution)/shard_map/pallas_call | solution.py:807
  307.3 0.0 collective-permute-done.4.far
  307.3 3.5 %shard_map.175 = (bf16[2,768,512]{2,1,0:T(8,128)(2,1)}, bf16[2,768,512]{2,1,0:T(8,128)(2,1)}, f32[16,1536]{1,0:T(8,128)}, f32[16,512]{1,0:T(8,128)}, f32[16,512]...) custom-call(bf16[768,512]{1,0:T(8,128)(2,1)} %get-tuple-element.49.near, ...), custom_call_target="tpu_custom_call" | custom-call | tf_op jit(solution)/shard_map/pallas_call | solution.py:845
Async XLA Ops:
  33.2 144.5 %collective-permute-start = (bf16[768,512]{1,0:T(8,128)(2,1)}, bf16[768,512]{1,0:T(8,128)(2,1)}, u32[]{:S(2)}, u32[]{:S(2)}) collective-permute-start(bf16[768,512]{1,0:T(8,128)(2,1)} %get-tuple-element.47), channel_id=1, source_target_pairs={{0,2},{1,3},{2,0},{3,1},{4,6},{5,7},{6,4},{7,5},{8,10},{9,11},{10,... | collective-permute-start | bytes 2359304 | tf_op jit(solution)/shard_map/ppermute | solution.py:864
  33.7 144.0 %collective-permute-start.3 = (bf16[2,2,16,1664]{3,2,1,0:T(8,128)(2,1)}, bf16[2,2,16,1664]{3,2,1,0:T(8,128)(2,1)}, u32[]{:S(2)}, u32[]{:S(2)}) collective-permute-start(bf16[2,2,16,1664]{3,2,1,0:T(8,128)(2,1)} %get-tuple-element.48.rest_0_), channel_id=1, source_target_pairs={{0,24},{4,28},{8,0},{12,4},{16,8},{20,12},{24,16},{28,20},{1,25},{... | collective-permute-start | bytes 638984 | tf_op jit(solution)/shard_map/ppermute | solution.py:862
  36.5 141.1 %collective-permute-start.2 = (bf16[2,2,16,1664]{3,2,1,0:T(8,128)(2,1)}, bf16[2,2,16,1664]{3,2,1,0:T(8,128)(2,1)}, u32[]{:S(2)}, u32[]{:S(2)}) collective-permute-start(bf16[2,2,16,1664]{3,2,1,0:T(8,128)(2,1)} %get-tuple-element.48.rest_0_), channel_id=1, source_target_pairs={{0,16},{4,20},{8,24},{12,28},{16,0},{20,4},{24,8},{28,12},{1,17},{... | collective-permute-start | bytes 638984 | tf_op jit(solution)/shard_map/ppermute | solution.py:862
  36.5 141.1 %collective-permute-start.1 = (bf16[2,2,16,1664]{3,2,1,0:T(8,128)(2,1)}, bf16[2,2,16,1664]{3,2,1,0:T(8,128)(2,1)}, u32[]{:S(2)}, u32[]{:S(2)}) collective-permute-start(bf16[2,2,16,1664]{3,2,1,0:T(8,128)(2,1)} %get-tuple-element.48.rest_0_), channel_id=1, source_target_pairs={{0,8},{4,12},{8,16},{12,20},{16,24},{20,28},{24,0},{28,4},{1,9},{5... | collective-permute-start | bytes 638984 | tf_op jit(solution)/shard_map/ppermute | solution.py:862
  197.3 75.1 %all-to-all-start = ((bf16[8,64,1664]{2,1,0:T(8,128)(2,1)}), bf16[8,64,1664]{2,1,0:T(8,128)(2,1)}, u32[]{:S(2)}, u32[]{:S(2)}) async-start(bf16[8,64,1664]{2,1,0:T(8,128)(2,1)} %get-tuple-element.61), calls=%async_computation | async-start | bytes 3407872 | tf_op jit(solution)/shard_map/all_to_all | solution.py:867
  232.0 75.3 %collective-permute-start.4 = (bf16[768,512]{1,0:T(8,128)(2,1)}, bf16[768,512]{1,0:T(8,128)(2,1)}, u32[]{:S(2)}, u32[]{:S(2)}) collective-permute-start(bf16[768,512]{1,0:T(8,128)(2,1)} %get-tuple-element.50), channel_id=1, source_target_pairs={{0,2},{1,3},{2,0},{3,1},{4,6},{5,7},{6,4},{7,5},{8,10},{9,11},{10,... | collective-permute-start | bytes 2359304 | tf_op jit(solution)/shard_map/ppermute | solution.py:868

commit v8 on v7

--- a/solution.py
+++ b/solution.py
@@ -279,7 +279,7 @@
             for h in range(H):
                 dss.append((pbuf[ps,h,:,:size].astype(f32)*dot(daug[h],vct[h,:,osl],1,0)).astype(bf))
                 dkv[W+h*HEAD:W+(h+1)*HEAD,osl]+=dot(lows[h],pbuf[ps,h,:,:size],1,0)
-            for h in range(H): qacc[h]+=dot(kct[h,:,osl],dss[h].T,1,0)
+            for h in range(H): qacc[h]+=dot(kct[h,:,osl],dss[h],1,1)
             for h in range(H):
                 dkv[h*HEAD:(h+1)*HEAD,osl]+=dot(qkv[slot,h*HEAD:(h+1)*HEAD,:],dss[h],1,0)
         g=by_piece(first,full,rest,g,piece)

time: 310 us -> 311 us (level)
  no operation moved by 1% of the time
where the time goes in v8:
time: 311 us; the launch traced here: 310 us
  Pallas kernels  267 us (86%)
  starting transfers between devices  39.2 us (13%)
    pallas_call x1, Pallas kernels, attend(): pl.pallas_call(functools.partial(attend_kernel, L, H), out_shape=[S((cap,...  140 us
    pallas_call x1, Pallas kernels, back(): pl.pallas_call(functools.partial(back_kernel, L, H), out_shape=[S((3 * W,...  37.6 us
    all_to_all x1, starting transfers between devices, shards(): parts = lax.all_to_all(parts, 'dp', 0, 0, tiled=True)  34.7 us
    pallas_call x1, Pallas kernels, reduce(): pl.pallas_call(functools.partial(reduce_kernel, Z, block, E, W, C1, rows)...  33.7 us
    pallas_call x1, Pallas kernels, gather(): pl.pallas_call(functools.partial(gather_kernel, Z, block, E, W, rows), ou...  32.6 us
    pallas_call x1, Pallas kernels, middle_net(): pl.pallas_call(functools.partial(middle_net_kernel, Z, block, E, F, W, T)...  19.6 us
  transfers between devices with their start and end apart: 6, of which 1 were waited for; matrix products, arithmetic and copies ran while one was open for 0% of the time, Pallas kernels for 68%

profile of v8, /device:TPU:0, one launch (start us, length us, event | category | flops | bytes accessed | tf_op | source)
XLA Modules:
  0.0 309.9 jit_solution(11771509570912491444)
XLA Ops:
  0.6 32.6 %shard_map.170 = (bf16[2,2,768,512]{3,2,1,0:T(8,128)(2,1)}, bf16[2,2,16,1664]{3,2,1,0:T(8,128)(2,1)}, bf16[512,768]{1,0:T(8,128)(2,1)}, bf16[768,3072]{1,0:T(8,1...) custom-call(bf16[2,768,512]{2,1,0:T(8,128)(2,1)} %bitcast.13, ...), custom_call_target="tpu_custom_call" | custom-call | tf_op jit(solution)/shard_map/pallas_call | solution.py:536
  33.2 0.5 collective-permute-start
  33.7 2.8 collective-permute-start.3
  36.5 0.0 collective-permute-start.2
  36.5 1.1 collective-permute-start.1
  37.7 140.0 %shard_map.171 = (bf16[36,4,512,512]{3,2,1,0:T(8,128)(2,1)}, bf16[2,3072,128]{2,1,0:T(8,128)(2,1)}, f32[6,256,512]{2,1,0:T(8,128)}, f32[4,8,3072]{2,1,0:T(8,128)...) custom-call(s32[16,128]{1,0:T(8,128)} %get-tuple-element.40.base_ref, s32[32,128]{1,0:T(8,128)} %get-tuple-element.41.win_ref, ...), custom_call_target="tpu_custom_call" | custom-call | tf_op jit(solution)/shard_map/pallas_call | solution.py:176
  177.7 0.0 collective-permute-done.3.rest_3_
  177.7 0.0 collective-permute-done.2.rest_2_
  177.7 0.0 collective-permute-done.1.rest_1_
  177.7 0.0 collective-permute-done.cotx_hbm
  177.7 19.6 %shard_map.172 = (bf16[768,512]{1,0:T(8,128)(2,1)}, bf16[768,512]{1,0:T(8,128)(2,1)}, bf16[2,768,512]{2,1,0:T(8,128)(2,1)}, bf16[256,3072]{1,0:T(8,128)(2,1)}, bf16[8,64,1664]{2,1,0:T(8,128)(2,1)}) custom-call(bf16[2,2,2,768,128]{4,3,2,1,0:T(8,128)(2,1)} %bitcast.14, bf16[2,2,768,512]{3,2,1,0:T(8,128)(2,1)} %get-tuple-element.46.tok_hbm, ...), custom_call_target="tpu_custom_call" | custom-call | tf_op jit(solution)/shard_map/pallas_call | solution.py:661
  197.3 34.7 %all-to-all-start = ((bf16[8,64,1664]{2,1,0:T(8,128)(2,1)}), bf16[8,64,1664]{2,1,0:T(8,128)(2,1)}, u32[]{:S(2)}, u32[]{:S(2)}) async-start(bf16[8,64,1664]{2,1,0:T(8,128)(2,1)} %get-tuple-element.61), calls=%async_computation | async-start | bytes 3407872 | tf_op jit(solution)/shard_map/all_to_all | solution.py:867
  232.1 0.0 collective-permute-start.4
  232.1 37.6 %shard_map.173 = (bf16[768,3072]{1,0:T(8,128)(2,1)}, bf16[12,512,512]{2,1,0:T(8,128)(2,1)}) custom-call(s32[16,128]{1,0:T(8,128)} %get-tuple-element.40.base_ref, s32[32,128]{1,0:T(8,128)} %get-tuple-element.41.win_ref, bf16[256,3072]{1,0:T(8,128)(2,1)} %get-tuple-element.51.datt_hbm, bf16[36,4,512,512]{3,2,1,0:T(8,128)(2,1)} %get-tuple-element.52.p_hbm, ...), custom_call_target="tpu_custom_call" | custom-call | tf_op jit(solution)/shard_map/pallas_call | solution.py:318
  269.7 2.8 all-to-all-done.parts_hbm
  272.5 33.7 %shard_map.174 = (bf16[2,768,512]{2,1,0:T(8,128)(2,1)}, f32[16,3200]{1,0:T(8,128)}) custom-call(s32[16,128]{1,0:T(8,128)} %get-tuple-element.40.base_ref, s32[8,3072]{1,0:T(8,128)} %get-tuple-element.44.meta_ref, bf16[768,3072]{1,0:T(8,128)(2,1)} %get-tuple-element.57.dq_hbm, bf16[12,512,512]{2,1,0:T(8,128)(2,1)} %get-tuple-element.58.dkvw_hbm, ...), custom_call_target="tpu_custom_call" | custom-call | tf_op jit(solution)/shard_map/pallas_call | solution.py:807
  306.3 0.0 collective-permute-done.4.far
  306.3 3.5 %shard_map.175 = (bf16[2,768,512]{2,1,0:T(8,128)(2,1)}, bf16[2,768,512]{2,1,0:T(8,128)(2,1)}, f32[16,1536]{1,0:T(8,128)}, f32[16,512]{1,0:T(8,128)}, f32[16,512]...) custom-call(bf16[768,512]{1,0:T(8,128)(2,1)} %get-tuple-element.49.near, ...), custom_call_target="tpu_custom_call" | custom-call | tf_op jit(solution)/shard_map/pallas_call | solution.py:845
Async XLA Ops:
  33.2 144.5 %collective-permute-start = (bf16[768,512]{1,0:T(8,128)(2,1)}, bf16[768,512]{1,0:T(8,128)(2,1)}, u32[]{:S(2)}, u32[]{:S(2)}) collective-permute-start(bf16[768,512]{1,0:T(8,128)(2,1)} %get-tuple-element.47), channel_id=1, source_target_pairs={{0,2},{1,3},{2,0},{3,1},{4,6},{5,7},{6,4},{7,5},{8,10},{9,11},{10,... | collective-permute-start | bytes 2359304 | tf_op jit(solution)/shard_map/ppermute | solution.py:864
  33.7 144.0 %collective-permute-start.3 = (bf16[2,2,16,1664]{3,2,1,0:T(8,128)(2,1)}, bf16[2,2,16,1664]{3,2,1,0:T(8,128)(2,1)}, u32[]{:S(2)}, u32[]{:S(2)}) collective-permute-start(bf16[2,2,16,1664]{3,2,1,0:T(8,128)(2,1)} %get-tuple-element.48.rest_0_), channel_id=1, source_target_pairs={{0,24},{4,28},{8,0},{12,4},{16,8},{20,12},{24,16},{28,20},{1,25},{... | collective-permute-start | bytes 638984 | tf_op jit(solution)/shard_map/ppermute | solution.py:862
  36.5 141.1 %collective-permute-start.2 = (bf16[2,2,16,1664]{3,2,1,0:T(8,128)(2,1)}, bf16[2,2,16,1664]{3,2,1,0:T(8,128)(2,1)}, u32[]{:S(2)}, u32[]{:S(2)}) collective-permute-start(bf16[2,2,16,1664]{3,2,1,0:T(8,128)(2,1)} %get-tuple-element.48.rest_0_), channel_id=1, source_target_pairs={{0,16},{4,20},{8,24},{12,28},{16,0},{20,4},{24,8},{28,12},{1,17},{... | collective-permute-start | bytes 638984 | tf_op jit(solution)/shard_map/ppermute | solution.py:862
  36.5 141.1 %collective-permute-start.1 = (bf16[2,2,16,1664]{3,2,1,0:T(8,128)(2,1)}, bf16[2,2,16,1664]{3,2,1,0:T(8,128)(2,1)}, u32[]{:S(2)}, u32[]{:S(2)}) collective-permute-start(bf16[2,2,16,1664]{3,2,1,0:T(8,128)(2,1)} %get-tuple-element.48.rest_0_), channel_id=1, source_target_pairs={{0,8},{4,12},{8,16},{12,20},{16,24},{20,28},{24,0},{28,4},{1,9},{5... | collective-permute-start | bytes 638984 | tf_op jit(solution)/shard_map/ppermute | solution.py:862
  197.3 75.2 %all-to-all-start = ((bf16[8,64,1664]{2,1,0:T(8,128)(2,1)}), bf16[8,64,1664]{2,1,0:T(8,128)(2,1)}, u32[]{:S(2)}, u32[]{:S(2)}) async-start(bf16[8,64,1664]{2,1,0:T(8,128)(2,1)} %get-tuple-element.61), calls=%async_computation | async-start | bytes 3407872 | tf_op jit(solution)/shard_map/all_to_all | solution.py:867
  232.1 74.2 %collective-permute-start.4 = (bf16[768,512]{1,0:T(8,128)(2,1)}, bf16[768,512]{1,0:T(8,128)(2,1)}, u32[]{:S(2)}, u32[]{:S(2)}) collective-permute-start(bf16[768,512]{1,0:T(8,128)(2,1)} %get-tuple-element.50), channel_id=1, source_target_pairs={{0,2},{1,3},{2,0},{3,1},{4,6},{5,7},{6,4},{7,5},{8,10},{9,11},{10,... | collective-permute-start | bytes 2359304 | tf_op jit(solution)/shard_map/ppermute | solution.py:868
